TPU v7x, 512 devices: a whole 4x4x16 slice. The times are simulated.
512 devices in a mesh: tm: 64 (over x, y, z_lo), chan: 8 (over z_hi, core).
Axes of the slice: x: 4, y: 4, z: 16 (z_hi: 4, z_lo: 4; z = z_hi * 4 + z_lo), core: 2. Of those that a mesh axis runs over, the one named last changes fastest.
Arguments:
- samples: bfloat16 [2, 2, 512, 196608], P(None, None, None, ('tm', 'chan')), may hold values from -96 to 96
- scales: float32 [512, 768], P('chan', 'tm'), may hold values from 0.01 to 0.06
- flags: int32 [512, 768], P('chan', 'tm'), may hold values 0 or 1
- sweep: float32 [512], P('chan'), may hold values from 128 to 1024
- phase_bin: int32 [196608], P('tm'), may hold values from 0 to 1023, as said below
Outputs:
- profile: float32 [1024, 4, 512], P('tm', None, 'chan')
Inputs may be any that keep to these rules, and one draw needn't show every extreme that they name: `flags`: A nonzero flag marks an excised block. phase_bin[t] = floor((1024 t + 1024 * o) / q) mod 1024, with whole numbers q in [2048, 8192) and o in [0, 2048) fixed by the draw, t counting samples from the start of the window.
All inputs are finite; a program needn't handle non-finite values.
Results may differ from a plain program's by a relative error of at most 0.0015.
Values may be sent and summed in bfloat16 or wider, within the bound.
No kernel may reach another device: no remote copies, remote signals or barrier semaphores. Data moves between devices by JAX's collectives and lax.ppermute only.
A program may use at most 64 MiB of HBM per device.

v0:
```python
import math

import jax
import jax.numpy as jnp
from jax import lax
from jax.sharding import PartitionSpec as P

NFFT = 4096
OVER = 1024
NBIN = 1024


lane_width = 128
exact_mode = lax.Precision.HIGHEST


def shifted(block, axis, distance):
    devices = range(lax.axis_size(axis))
    route = [(i - distance, i) for i in devices if i - distance in devices]
    return lax.ppermute(block, axis, route)


def unit_pair(whole, length, sign):
    angle = sign * 2.0 * math.pi / length * whole.astype(jnp.float32)
    return (jnp.cos(angle), jnp.sin(angle))


def complex_table(tab_re, tab_im):
    return jnp.stack([jnp.stack([tab_re, -tab_im]), jnp.stack([tab_im, tab_re])])


def rows_apply(table, data):
    return jnp.einsum("oijk,pixfkl->poxfjl", table, data, precision=exact_mode)


def lanes_apply(data, table):
    return jnp.einsum("pixfjl,oilm->poxfjm", data, table, precision=exact_mode)


def spin_pair(data, right_re, right_im):
    left_re = data[:, 0]
    left_im = data[:, 1]
    return jnp.stack(
        [left_re * right_re - left_im * right_im, left_re * right_im + left_im * right_re], axis=1
    )


def frame_rows(array):
    return array.reshape(array.shape[:-1] + (array.shape[-1] // lane_width, lane_width))


def on_device(samples, scales, flags, sweep, phase_bin):
    channels = scales.shape[0]
    blocks = scales.shape[1]
    slab_len = samples.shape[-1] * lax.axis_size("chan")
    block_len = slab_len // blocks
    kept_len = NFFT - OVER
    frame_count = slab_len // kept_len
    row_count = NFFT // lane_width
    rim_rows = OVER // lane_width
    weight = scales * (1 - flags).astype(jnp.float32)
    items = lax.all_to_all(samples, "chan", split_axis=2, concat_axis=3, tiled=True)
    shaped = items.reshape(items.shape[:3] + (blocks, block_len)).astype(jnp.float32)
    full = (shaped * weight[:, :, None]).reshape(items.shape[:3] + (slab_len,))
    tail_part = full[..., slab_len - OVER :]
    previous = shifted(tail_part.astype(jnp.bfloat16), "tm", 1).astype(tail_part.dtype)
    row_ids = jnp.arange(row_count, dtype=jnp.int32)
    lane_ids = jnp.arange(lane_width, dtype=jnp.int32)
    row_re, row_im = unit_pair(row_ids[:, None] * row_ids[None, :] % row_count, row_count, -1.0)
    twist_re, twist_im = unit_pair(row_ids[:, None] * lane_ids[None, :] % NFFT, NFFT, -1.0)
    lane_re, lane_im = unit_pair(
        lane_ids[:, None] * lane_ids[None, :] % lane_width, lane_width, -1.0
    )
    row_table = complex_table(row_re, row_im)
    later_list = [
        full[..., number * kept_len - OVER : number * kept_len - OVER + NFFT]
        for number in range(1, frame_count)
    ]
    first_frame = jnp.concatenate([previous, full], axis=-1)
    shaped = frame_rows(jnp.stack([first_frame] + later_list, axis=3))
    section = rows_apply(row_table, shaped)
    spun = spin_pair(section, twist_re, twist_im)
    spectrum = lanes_apply(spun, complex_table(lane_re, lane_im))
    freq = row_ids[:, None] + row_count * lane_ids[None, :]
    offset = jnp.where(freq < NFFT // 2, freq, freq - NFFT).astype(jnp.float32) / NFFT
    phase = (jnp.pi * sweep)[:, None, None] * (offset * offset + offset)[None]
    chirp_re = jnp.cos(phase)[:, None]
    chirp_im = jnp.sin(phase)[:, None]
    spectrum = spin_pair(spectrum, chirp_re, chirp_im)
    backward = lanes_apply(spectrum, complex_table(lane_re, -lane_im))
    backward = spin_pair(backward, twist_re, -twist_im)
    output = rows_apply(complex_table(row_re[rim_rows:], -row_im[rim_rows:]), backward)
    output = (output * (1.0 / NFFT)).reshape(2, 2, channels, slab_len)
    out_re = output[:, 0]
    out_im = output[:, 1]
    power_h = out_re[0] * out_re[0] + out_im[0] * out_im[0]
    power_v = out_re[1] * out_re[1] + out_im[1] * out_im[1]
    cross_re = out_re[0] * out_re[1] + out_im[0] * out_im[1]
    cross_im = out_im[0] * out_re[1] - out_re[0] * out_im[1]
    stokes = jnp.stack(
        [power_h + power_v, power_h - power_v, 2.0 * cross_re, 2.0 * cross_im], 0
    ).astype(jnp.bfloat16)
    stokes_rows = stokes.reshape(4 * channels, slab_len)
    fold_scale = NBIN / (slab_len * lax.axis_size("tm"))
    share_rows = NBIN // lax.axis_size("tm")
    bin_block = math.gcd(NBIN, 128)

    def one_block(first_bin):
        bin_ids = first_bin + jnp.arange(bin_block, dtype=jnp.int32)
        onehot = (phase_bin[None, :] == bin_ids[:, None]).astype(jnp.bfloat16)
        return lax.dot_general(
            onehot, stokes_rows, (((1,), (1,)), ((), ())), preferred_element_type=jnp.float32
        )

    firsts = 0 + bin_block * jnp.arange(NBIN // bin_block, dtype=jnp.int32)
    folded = lax.map(one_block, firsts)
    summed = lax.psum(
        (folded.reshape(NBIN, 4 * channels) * fold_scale).reshape(NBIN, 4, channels), "tm"
    )
    profile = lax.dynamic_slice_in_dim(summed, lax.axis_index("tm") * share_rows, share_rows, 0)
    return profile


def solution(mesh):
    placed = (
        P(None, None, None, ("tm", "chan")),
        P("chan", "tm"),
        P("chan", "tm"),
        P("chan"),
        P("tm"),
    )
    return jax.shard_map(
        on_device, mesh=mesh, in_specs=placed, out_specs=P("tm", None, "chan"), check_vma=False
    )
```

profile of v0, /device:TPU:8, one launch (start us, length us, event | category | flops | bytes accessed | tf_op | source)
XLA Modules:
  0.0 917.6 jit_solution(4088752309370461180)
XLA Ops:
  6.5 4.2 copy.31
  10.8 15.2 %all-to-all-start = ((bf16[2,2,512,384]{3,1,0,2:T(2,128)(2,1)}), bf16[2,2,512,384]{3,1,0,2:T(2,128)(2,1)S(1)}, u32[]{:S(2)}, u32[]{:S(2)}) async-start(bf16[2,2,512,384]{3,1,0,2:T(2,128)(2,1)} %copy.31), calls=%async_computation | async-start | bytes 3145728 | tf_op jit(solution)/shard_map/all_to_all | solution.py:62
  26.4 1.4 copy.61
  27.7 0.5 iota_multiply_fusion
  28.3 0.7 fusion.81
  29.1 0.7 fusion.76
  29.9 0.6 maximum_bitcast_fusion.16
  30.7 0.6 maximum_bitcast_fusion.14
  31.6 0.7 fusion.40
  32.3 0.6 broadcast_multiply_fusion.2
  32.9 66.6 %all-to-all-done = bf16[2,2,512,384]{3,1,0,2:T(2,128)(2,1)S(1)} async-done(((bf16[2,2,512,384]{3,1,0,2:T(2,128)(2,1)}), bf16[2,2,512,384]{3,1,0,2:T(2,128)(2,1)S(1)}, u32[]{:S(2)}, u32[]{:S(2)}) %all-to-all-start) | async-done | bytes 1572896 | tf_op jit(solution)/shard_map/all_to_all | solution.py:62
  99.6 1.1 convert_bitcast_fusion
  100.7 1.8 copy.32
  102.5 2.9 reshape.525
  105.4 3.4 broadcast_multiply_fusion
  108.8 1.2 slice.111
  110.0 5.4 collective-permute-start
  115.9 0.6 multiply_add_fusion.5
  116.5 5.5 multiply_cosine_fusion
  122.1 3.6 collective-permute-done
  125.7 1.4 convert_element_type.131
  127.1 4.6 pad_maximum_fusion
  131.7 6.6 reshape.527
  138.3 5.7 fusion.21
  144.0 0.8 multiply_subtract_fusion.2
  144.8 0.6 maximum_bitcast_fusion
  145.7 6.8 fusion.24
  152.5 1.2 multiply_subtract_fusion.1
  154.0 6.5 fusion.27
  160.6 0.8 multiply_subtract_fusion
  161.4 3.3 fusion.20
  164.7 2.9 reshape.524
  167.6 5.7 fusion.86
  173.3 0.7 fusion.30
  174.3 1.0 copy-done.2
  175.3 15.4 %while.10 = (s32[]{:T(128)}, f32[8,128,256]{2,1,0:T(8,128)S(1)}, s32[3072]{0:T(1024)S(1)}, s32[8]{0:T(128)S(1)}, bf16[256,3072]{1,0:T(8,128)(2,1)S(1)}, /*index=5*/s32[]{:T(128)}) while((s32[]{:T(128)}, f32[8,128,256]{2,1,0:T(8,128)S(1)}, s32[3072]{0:T(1024)S(1)}, s32[8]{0:T(128)S(1)}, bf16[256,3072]{1,0:T(8,128)(2,1)S(1)}, ...), condition=%wide.region_1.2_spmd, body=%wide.region_0.1_spmd.sunk | while | flops 201719936 | bytes 1717337 | solution.py:116
  175.3 0.6 dynamic_slice.10
  175.8 0.6 iota_add_fusion.2
  176.5 0.7 fusion.93
  177.2 0.6 dynamic_slice.10
  177.8 0.6 iota_add_fusion.2
  178.4 0.7 fusion.93
  179.1 0.6 dynamic_slice.10
  179.7 0.6 iota_add_fusion.2
  180.4 0.7 fusion.93
  181.0 0.6 dynamic_slice.10
  181.6 0.6 iota_add_fusion.2
  182.3 0.7 fusion.93
  183.0 0.6 dynamic_slice.10
  183.6 0.6 iota_add_fusion.2
  184.2 0.7 fusion.93
  184.9 0.6 dynamic_slice.10
  185.5 0.6 iota_add_fusion.2
  186.1 0.7 fusion.93
  186.8 0.6 dynamic_slice.10
  187.4 0.6 iota_add_fusion.2
  188.1 0.7 fusion.93
  188.8 0.6 dynamic_slice.10
  189.3 0.6 iota_add_fusion.2
  190.0 0.7 fusion.93
  191.2 1.1 mul.727
  192.4 716.5 %all-reduce.2.cloned.1.call-done = f32[1024,4,64]{0,2,1:T(8,128)} async-done(((f32[1024,4,64]{0,2,1:T(8,128)}), f32[1024,4,64]{0,2,1:T(8,128)}) %all-reduce.2.cloned.1.call-update) | async-done | bytes 1048592 | tf_op jit(solution)/shard_map/psum | solution.py:117
  908.8 1.0 constant_dynamic-slice_fusion
  909.8 0.7 copy.42
  (46 shorter events, 3.0 us)
Async XLA Ops:
  10.8 15.3 %copy-start.10 = (f32[64,12]{0,1:T(8,128)S(1)}, f32[64,12]{0,1:T(8,128)}, u32[]{:S(2)}) copy-start(f32[64,12]{0,1:T(8,128)} %param.8) | copy-start | bytes 9220
  10.8 15.3 %copy-start.11 = (s32[64,12]{0,1:T(8,128)S(1)}, s32[64,12]{0,1:T(8,128)}, u32[]{:S(2)}) copy-start(s32[64,12]{0,1:T(8,128)} %param.9) | copy-start | bytes 9220
  10.8 88.8 %all-to-all-start = ((bf16[2,2,512,384]{3,1,0,2:T(2,128)(2,1)}), bf16[2,2,512,384]{3,1,0,2:T(2,128)(2,1)S(1)}, u32[]{:S(2)}, u32[]{:S(2)}) async-start(bf16[2,2,512,384]{3,1,0,2:T(2,128)(2,1)} %copy.31), calls=%async_computation | async-start | bytes 3145728 | tf_op jit(solution)/shard_map/all_to_all | solution.py:62
  26.0 882.9 %all-reduce.2.cloned.1.call-start = ((), (), s32[]{:S(2)}) async-start(), calls=%async_computation.1 | async-start | bytes 2097152 | tf_op jit(solution)/shard_map/psum | solution.py:117
  26.1 6.2 copy-start.13
  110.0 15.7 %collective-permute-start = (bf16[2,2,64,1024]{3,1,2,0:T(2,128)(2,1)}, bf16[2,2,64,1024]{3,1,2,0:T(2,128)(2,1)}, u32[]{:S(2)}, u32[]{:S(2)}) collective-permute-start(bf16[2,2,64,1024]{3,1,2,0:T(2,128)(2,1)} %slice.111), channel_id=1, source_target_pairs={{0,8},{8,16},{16,24},{24,32},{32,40},{40,48},{48,56},{56,64},{64,7... | collective-permute-start | bytes 1572872 | tf_op jit(solution)/shard_map/ppermute | solution.py:20
  131.7 6.6 copy-start.4
  131.7 6.6 copy-start.5
  138.3 5.7 copy-start.9
  144.8 0.9 copy-start.3
  145.7 6.8 copy-start
  145.7 6.8 copy-start.1
  154.0 6.5 copy-start.8
  160.6 0.8 copy-start.6
  160.6 0.8 copy-start.7
  174.0 1.2 copy-start.2
  174.0 1.2 copy-start.12
  174.0 1.2 copy-start.14
Sparse Core Ops, SparseCore 0:
  192.5 716.3 all-reduce.1
where the time goes:
time: 928 us; the launch traced here: 918 us
  waiting for transfers between devices  787 us (85%)
  local copies, waits for them, and re-layouts  36.2 us (4%)
  other arithmetic  32.2 us (3%)
  matrix products  27.6 us (3%)
  starting transfers between devices  20.7 us (2%)
  between operations  14 us (2%)
    psum x1, waiting for transfers between devices, on_device(): lax.psum((folded.reshape(NBIN, 4 * channels) * fold_scale).reshape(NBIN,...  716 us
    all_to_all x1, waiting for transfers between devices, on_device(): lax.all_to_all(samples, 'chan', split_axis=2, concat_axis=3, tiled=True)  66.6 us
  transfers between devices with their start and end apart: 3, of which 3 were waited for; matrix products, arithmetic and copies ran while one was open for 1% of the time, Pallas kernels for 0%

commit v1 on v0

v1 whole, which is shorter than its diff:
```python
import functools
import math

import jax
import jax.numpy as jnp
import numpy as np
from jax import lax
from jax.experimental import pallas as pl
from jax.experimental.pallas import tpu as pltpu
from jax.sharding import Mesh, PartitionSpec as P

NFFT = 4096
OVER = 1024
BLK = 256
NBIN = 1024
LANES = 128
ROWS = NFFT // LANES
RIM = OVER // LANES
KEPT = ROWS - RIM
RUNS = 4
MEMBERS = 8
PIECE = 384
SLAB = MEMBERS * PIECE
GROUP = 16
BLOCKS = SLAB // BLK
WINDOW = 144
ACC_ROWS = NBIN + WINDOW
HALF_ROOT = math.sqrt(0.5)


def lane_tables():
    angle = 2.0 * np.pi / LANES * (np.arange(LANES)[:, None] * np.arange(LANES)[None, :] % LANES)
    cos, sin = np.cos(angle), np.sin(angle)
    table = np.block([[cos, -sin], [sin, cos]]).astype(np.float32)
    high = table.astype(jnp.bfloat16)
    low = (table - high.astype(np.float32)).astype(jnp.bfloat16)
    return high, low


def twist_tables():
    angle = -2.0 * np.pi / NFFT * (np.arange(ROWS)[:, None] * np.arange(LANES)[None, :])
    return np.cos(angle).astype(np.float32), np.sin(angle).astype(np.float32)


def plus(a, b):
    return (a[0] + b[0], a[1] + b[1])


def minus(a, b):
    return (a[0] - b[0], a[1] - b[1])


def quarter(a, sign):
    return (a[1], -a[0]) if sign < 0 else (-a[1], a[0])


def dft4(x, sign):
    t0, t1 = plus(x[0], x[2]), minus(x[0], x[2])
    t2, t3 = plus(x[1], x[3]), quarter(minus(x[1], x[3]), sign)
    return [plus(t0, t2), plus(t1, t3), minus(t0, t2), minus(t1, t3)]


def dft8(x, sign):
    even = dft4(x[0::2], sign)
    odd = dft4(x[1::2], sign)
    re, im = odd[1]
    if sign < 0:
        odd[1] = ((re + im) * HALF_ROOT, (im - re) * HALF_ROOT)
    else:
        odd[1] = ((re - im) * HALF_ROOT, (im + re) * HALF_ROOT)
    odd[2] = quarter(odd[2], sign)
    re, im = odd[3]
    if sign < 0:
        odd[3] = ((im - re) * HALF_ROOT, (re + im) * -HALF_ROOT)
    else:
        odd[3] = ((re + im) * -HALF_ROOT, (re - im) * HALF_ROOT)
    return [plus(e, o) for e, o in zip(even, odd)] + [minus(e, o) for e, o in zip(even, odd)]


def turned(a, step, sign):
    step %= 32
    if step == 0:
        return a
    if step == 8:
        return quarter(a, sign)
    re, im = a
    if step == 4:
        if sign < 0:
            return ((re + im) * HALF_ROOT, (im - re) * HALF_ROOT)
        return ((re - im) * HALF_ROOT, (im + re) * HALF_ROOT)
    cos = math.cos(2.0 * math.pi * step / 32)
    sin = sign * math.sin(2.0 * math.pi * step / 32)
    return (re * cos - im * sin, re * sin + im * cos)


def split(values):
    high = values.astype(jnp.bfloat16)
    return high, (values - high.astype(jnp.float32)).astype(jnp.bfloat16)


def lane_dft(high, low, table_high, table_low):
    dot = functools.partial(jnp.dot, preferred_element_type=jnp.float32)
    return dot(high, table_high) + (dot(low, table_high) + dot(high, table_low))


def frame_profile(
    row_of, weight_of, base_of, marks_of, chirp_ref, twist_ref, table_ref, mid, y_ref, v_ref, stokes_ref, acc
):
    for pol in range(2):
        for b in range(4):
            rows = []
            for a in range(8):
                row = 4 * a + b
                gain = weight_of(row // 2)
                rows.append(tuple(row_of(row, pol, part).astype(jnp.float32) * gain for part in range(2)))
            for ka, value in enumerate(dft8(rows, -1)):
                value = turned(value, b * ka, -1)
                mid[pol, 0, b, ka] = value[0]
                mid[pol, 1, b, ka] = value[1]
        for ka in range(8):
            values = dft4([(mid[pol, 0, b, ka], mid[pol, 1, b, ka]) for b in range(4)], -1)
            for kb in range(4):
                k = ka + 8 * kb
                re, im = values[kb]
                if k:
                    cos, sin = twist_ref[0, k : k + 1], twist_ref[1, k : k + 1]
                    re, im = re * cos - im * sin, re * sin + im * cos
                for part, value in enumerate((re, im)):
                    high, low = split(value)
                    where = (pl.ds(GROUP * k, GROUP), pl.ds(LANES * part, LANES))
                    y_ref[0, *where] = high
                    y_ref[1, *where] = low
        for m in range(4):
            rows = pl.ds(8 * GROUP * m, 8 * GROUP)
            spectrum = lane_dft(y_ref[0, rows], y_ref[1, rows], table_ref[0], table_ref[1])
            re, im = spectrum[:, :LANES], spectrum[:, LANES:]
            cos, sin = chirp_ref[0, rows], chirp_ref[1, rows]
            swapped = jnp.concatenate([re * sin + im * cos, re * cos - im * sin], axis=1)
            back = lane_dft(*split(swapped), table_ref[0], table_ref[1])
            im, re = (back[:, part].reshape(8, GROUP, LANES) for part in (slice(0, LANES), slice(LANES, None)))
            cos = twist_ref[0, 8 * m : 8 * m + 8][:, None, :]
            sin = twist_ref[1, 8 * m : 8 * m + 8][:, None, :]
            v_ref[0, 8 * m : 8 * m + 8] = re * cos + im * sin
            v_ref[1, 8 * m : 8 * m + 8] = im * cos - re * sin
        for b in range(4):
            values = dft8([(v_ref[0, 4 * a + b], v_ref[1, 4 * a + b]) for a in range(8)], 1)
            for na, value in enumerate(values):
                value = turned(value, b * na, 1)
                mid[pol, 0, b, na] = value[0]
                mid[pol, 1, b, na] = value[1]
    for na in range(8):
        x, y = (
            dft4([(mid[pol, 0, b, na], mid[pol, 1, b, na]) for b in range(4)], 1) for pol in range(2)
        )
        for nb in range(1, 4):
            (xr, xi), (yr, yi) = x[nb], y[nb]
            power_x = xr * xr + xi * xi
            power_y = yr * yr + yi * yi
            cross_re = xr * yr + xi * yi
            cross_im = xi * yr - xr * yi
            row = na + 8 * (nb - 1)
            lanes = pl.ds(LANES * (row % 2), LANES)
            for s, value in enumerate((power_x + power_y, power_x - power_y, 2.0 * cross_re, 2.0 * cross_im)):
                stokes_ref[row // 2, pl.ds(GROUP * s, GROUP), lanes] = value.astype(jnp.bfloat16)
    bins = lax.broadcasted_iota(jnp.int32, (WINDOW, BLK), 0)
    for m in range(BLOCKS):
        onehot = jnp.where(bins == marks_of(m), 1.0, 0.0).astype(jnp.bfloat16)
        part = lax.dot_general(
            onehot, stokes_ref[m], (((1,), (1,)), ((), ())), preferred_element_type=jnp.float32
        )
        place = pl.ds(pl.multiple_of(base_of(m), 8), WINDOW)
        acc[place] += part


def own_row(buf_ref, slab, row, pol, part):
    return buf_ref[row // 3, slab, pol, part, :, pl.ds(LANES * (row % 3), LANES)]


def later_kernel(
    base_ref, buf_ref, weight_ref, marks_ref, chirp_ref, twist_ref, table_ref, acc_ref, mid, y_ref, v_ref, stokes_ref
):
    acc_ref[...] = jnp.zeros_like(acc_ref)

    def step(frame, carry):
        def row_of(row, pol, part):
            if row < RIM:
                return own_row(buf_ref, frame - 1, row + KEPT - RIM, pol, part)
            return own_row(buf_ref, frame, row - RIM, pol, part)

        frame_profile(
            row_of,
            lambda block: weight_ref[BLOCKS * frame + block],
            lambda m: base_ref[BLOCKS * frame + m],
            lambda m: marks_ref[BLOCKS * frame + m],
            chirp_ref,
            twist_ref,
            table_ref,
            mid,
            y_ref,
            v_ref,
            stokes_ref,
            acc_ref,
        )
        return carry

    lax.fori_loop(1, RUNS, step, 0)


def first_kernel(
    base_ref, buf_ref, tail_ref, weight_ref, marks_ref, chirp_ref, twist_ref, table_ref, given_ref, out_ref,
    acc, mid, y_ref, v_ref, stokes_ref,
):
    acc[...] = given_ref[...]

    def row_of(row, pol, part):
        if row < RIM:
            return own_row(tail_ref, 0, row + 1, pol, part)
        return own_row(buf_ref, 0, row - RIM, pol, part)

    frame_profile(
        row_of,
        lambda block: weight_ref[block],
        lambda m: base_ref[m],
        lambda m: marks_ref[m],
        chirp_ref,
        twist_ref,
        table_ref,
        mid,
        y_ref,
        v_ref,
        stokes_ref,
        acc,
    )
    acc[:WINDOW] += acc[NBIN:]
    for share in range(NBIN // 16):
        out_ref[share] = jnp.concatenate([acc[16 * share : 16 * share + 8], acc[16 * share + 8 : 16 * share + 16]], axis=1)


def scratch():
    return [
        pltpu.VMEM((2, 2, 4, 8, GROUP, LANES), jnp.float32),
        pltpu.VMEM((2, ROWS * GROUP, 2 * LANES), jnp.bfloat16),
        pltpu.VMEM((2, ROWS, GROUP, LANES), jnp.float32),
        pltpu.VMEM((BLOCKS, 4 * GROUP, BLK), jnp.bfloat16),
    ]


def whole():
    return pl.BlockSpec(memory_space=pltpu.VMEM)


def fold_frames(buf, tail_of, weight, base, marks, chirp):
    twist = jnp.asarray(np.stack(twist_tables()))
    table = jnp.asarray(np.stack(lane_tables()))
    tail = tail_of(buf)
    params = pltpu.CompilerParams(vmem_limit_bytes=28 * 1024 * 1024)
    flops = 2 * 2 * 2 * 3 * ROWS * GROUP * 256 * 256
    later = pl.pallas_call(
        later_kernel,
        out_shape=jax.ShapeDtypeStruct((ACC_ROWS, 4 * GROUP), jnp.float32),
        in_specs=[pl.BlockSpec(memory_space=pltpu.SMEM)] + [whole()] * 6,
        out_specs=whole(),
        scratch_shapes=scratch(),
        compiler_params=params,
        cost_estimate=pl.CostEstimate(flops=3 * flops, bytes_accessed=30_000_000, transcendentals=0),
        name="later_frames",
    )(base, buf, weight, marks, chirp, twist, table)
    block = (MEMBERS, 1) + buf.shape[2:]
    return pl.pallas_call(
        first_kernel,
        out_shape=jax.ShapeDtypeStruct((NBIN // 16, 8, LANES), jnp.float32),
        grid=(1,),
        in_specs=[pl.BlockSpec(memory_space=pltpu.SMEM), pl.BlockSpec(block, lambda i: (0,) * 6)] + [whole()] * 7,
        out_specs=whole(),
        scratch_shapes=[pltpu.VMEM((ACC_ROWS, 4 * GROUP), jnp.float32)] + scratch(),
        compiler_params=params,
        cost_estimate=pl.CostEstimate(flops=flops, bytes_accessed=10_000_000, transcendentals=0),
        name="first_frame",
    )(base, buf, tail, weight, marks, chirp, twist, table, later)


def gathered(block, axis):
    size = lax.axis_size(axis)
    parts = [block] + [
        lax.ppermute(block, axis, [(i, (i + turn) % size) for i in range(size)]) for turn in range(1, size)
    ]
    me = lax.axis_index(axis)
    pile = jnp.stack(parts)
    return jnp.concatenate(
        [lax.dynamic_slice_in_dim(pile, (me - i + size) % size, 1, 0) for i in range(size)]
    )


def from_before(block):
    size = lax.axis_size("xy")
    return lax.ppermute(block, "xy", [(i, i + 1) for i in range(size - 1)])


def chirp_table(sweep):
    k = jnp.arange(ROWS, dtype=jnp.int32)[:, None] + ROWS * jnp.arange(LANES, dtype=jnp.int32)[None, :]
    u = jnp.where(k < NFFT // 2, k, k - NFFT).astype(jnp.float32) / NFFT
    phase = (jnp.pi * sweep)[None, :, None] * (u * u + u)[:, None, :]
    table = jnp.stack([jnp.cos(phase), jnp.sin(phase)]) * (1.0 / NFFT)
    return table.reshape(2, ROWS * GROUP, LANES)


def on_device(samples, scales, flags, sweep, phase_bin):
    parts = samples.reshape(2, 2, MEMBERS * RUNS, GROUP, PIECE).transpose(2, 0, 1, 3, 4)
    buf = lax.all_to_all(parts, ("chan", "zl"), split_axis=0, concat_axis=0, tiled=True)
    buf = buf.reshape(MEMBERS, RUNS, 2, 2, GROUP, PIECE)

    me = lax.axis_index("zl")
    weight = scales * (1 - flags).astype(jnp.float32)
    message = jnp.concatenate([weight.reshape(-1), phase_bin.astype(jnp.float32)])
    letters = gathered(message, "zl")
    count = scales.shape[0] * BLOCKS
    weights = letters[:, :count].reshape(RUNS, scales.shape[0], BLOCKS)
    weights = lax.dynamic_slice_in_dim(weights, me * GROUP, GROUP, 1)
    weights = weights.transpose(0, 2, 1).reshape(RUNS * BLOCKS, GROUP)
    weights = jnp.concatenate([from_before(weights[-(OVER // BLK) :]), weights])
    weights = jnp.broadcast_to(weights[:, :, None], weights.shape + (LANES,))
    bins = letters[:, count:].astype(jnp.int32).reshape(RUNS * BLOCKS, 1, BLK)
    base = bins[:, 0, 0] // 8 * 8
    marks = (bins - base[:, None, None]) % NBIN
    chirp = chirp_table(lax.dynamic_slice_in_dim(sweep, me * GROUP, GROUP, 0))

    partial = fold_frames(buf, lambda b: from_before(b[5:, RUNS - 1 :]), weights, base, marks, chirp)
    shares = lax.all_to_all(partial, ("xy", "zl"), split_axis=0, concat_axis=0, tiled=True)
    total = shares.reshape(-1, RUNS, 8, 2, 4, GROUP).sum(0) * (NBIN / (SLAB * RUNS * lax.axis_size("xy")))
    return total.transpose(2, 1, 3, 0, 4).reshape(16, 4, RUNS * GROUP)


def solution(mesh):
    inner = Mesh(mesh.devices.reshape(-1, RUNS, MEMBERS), ("xy", "zl", "chan"))
    time = ("xy", "zl")
    placed = (
        P(None, None, None, ("xy", "zl", "chan")),
        P("chan", time),
        P("chan", time),
        P("chan"),
        P(time),
    )
    return jax.shard_map(
        on_device, mesh=inner, in_specs=placed, out_specs=P(time, None, "chan"), check_vma=False
    )
```

time: 928 us -> 135 us (0.15); the launches traced: 918 us -> 134 us
  waiting for transfers between devices: 787 us -> 58.3 us
  local copies, waits for them, and re-layouts: 36.2 us -> 6.19 us
  other arithmetic: 32.2 us -> 4.19 us
  matrix products: 27.6 us -> 0 us
  blocking collectives: 0 us -> 21.4 us
  between operations: 14 us -> 0.42 us
  starting transfers between devices: 20.7 us -> 33 us
  Pallas kernels: 0 us -> 10.9 us
    psum x1 -> x0, waiting for transfers between devices: 716 us -> none  [on_device(): lax.psum((folded.reshape(NBIN, 4 * channels) * fold_scale).reshape(NBIN,...]
    all_to_all x1, waiting for transfers between devices: 66.6 us -> 0.18 us  [on_device(): lax.all_to_all(parts, ('chan', 'zl'), split_axis=0, concat_axis=0, tiled=...]
    ppermute x1 -> x5, waiting for transfers between devices: 3.64 us -> 58.1 us  [the longest x3 58.1 us: gathered(): lax.ppermute(block, axis, [(i, (i + turn) % size) for i in range(size)])]
    dot_general x12 -> x0, matrix products: 27.6 us -> none  [the longest x2 13.3 us: lanes_apply(): return jnp.einsum('pixfjl,oilm->poxfjm', data, table, precision=exact_mode)]
    all_to_all x0 -> x1, blocking collectives: none -> 21.4 us  [on_device(): lax.all_to_all(partial, ('xy', 'zl'), split_axis=0, concat_axis=0, tiled=...]
    ppermute x1 -> x5, starting transfers between devices: 5.4 us -> 17.4 us  [the longest x3 10.4 us: gathered(): lax.ppermute(block, axis, [(i, (i + turn) % size) for i in range(size)])]
    pallas_call x0 -> x2, Pallas kernels: none -> 10.9 us  [the longest x1 7.8 us: fold_frames(): pl.pallas_call(later_kernel, out_shape=jax.ShapeDtypeStruct((ACC_ROWS, 4...]
  transfers between devices with their start and end apart: 3 -> 6, of which waited for: 3 -> 3; matrix products, arithmetic and copies ran while one was open for 1% -> 3% of each run, Pallas kernels for 0% -> 6%
where the time goes in v1:
time: 135 us; the launch traced here: 134 us
  waiting for transfers between devices  58.3 us (43%)
  starting transfers between devices  33 us (24%)
  blocking collectives  21.4 us (16%)
  Pallas kernels  10.9 us (8%)
  local copies, waits for them, and re-layouts  6.19 us (5%)
  other arithmetic  4.19 us (3%)
    ppermute x3, waiting for transfers between devices, gathered(): lax.ppermute(block, axis, [(i, (i + turn) % size) for i in range(size)])  58.1 us
    all_to_all x1, blocking collectives, on_device(): lax.all_to_all(partial, ('xy', 'zl'), split_axis=0, concat_axis=0, tiled=...  21.4 us
    all_to_all x1, starting transfers between devices, on_device(): lax.all_to_all(parts, ('chan', 'zl'), split_axis=0, concat_axis=0, tiled=...  15.6 us
    ppermute x3, starting transfers between devices, gathered(): lax.ppermute(block, axis, [(i, (i + turn) % size) for i in range(size)])  10.4 us
    pallas_call x1, Pallas kernels, fold_frames(): pl.pallas_call(later_kernel, out_shape=jax.ShapeDtypeStruct((ACC_ROWS, 4...  7.8 us
    ppermute x2, starting transfers between devices, from_before(): return lax.ppermute(block, 'xy', [(i, i + 1) for i in range(size - 1)])  6.96 us
    pallas_call x1, Pallas kernels, fold_frames(): pl.pallas_call(first_kernel, out_shape=jax.ShapeDtypeStruct((NBIN // 16,...  3.11 us
    reshape x1, local copies, waits for them, and re-layouts, on_device(): samples.reshape(2, 2, MEMBERS * RUNS, GROUP, PIECE).transpose(2, 0, 1, 3, 4)  2.84 us
  transfers between devices with their start and end apart: 6, of which 3 were waited for; matrix products, arithmetic and copies ran while one was open for 3% of the time, Pallas kernels for 6%

profile of v1, /device:TPU:8, one launch (start us, length us, event | category | flops | bytes accessed | tf_op | source)
XLA Modules:
  0.0 134.5 jit_solution(18045978333197767628)
XLA Ops:
  0.0 2.8 %copy.27 = bf16[2,2,32,16,384]{4,3,1,0,2:T(8,128)(2,1)} copy(bf16[2,2,32,16,384]{4,3,2,1,0:T(8,128)(2,1)} %bitcast.21) | data formatting | bytes 3145728 | tf_op jit(solution)/shard_map/reshape | solution.py:308
  2.8 0.0 copy-start.2
  2.8 0.0 copy-start.3
  2.8 0.0 copy-start.4
  2.8 0.0 copy-start.5
  2.9 15.6 %all-to-all-start = ((bf16[32,2,2,16,384]{4,3,2,1,0:T(8,128)(2,1)}), bf16[32,2,2,16,384]{4,3,2,1,0:T(8,128)(2,1)S(1)}, u32[]{:S(2)}, u32[]{:S(2)}) async-start(bf16[32,2,2,16,384]{4,3,2,1,0:T(8,128)(2,1)} %bitcast.16), calls=%async_computation | async-start | bytes 3145728 | tf_op jit(solution)/shard_map/all_to_all | solution.py:309
  18.5 0.0 copy-done.2
  18.5 0.0 copy-done.3
  18.5 0.0 copy-done.4
  18.5 0.1 copy.18
  18.6 0.1 reshape.190
  18.8 5.5 %collective-permute-start.2 = (f32[3840]{0:T(1024)S(1)}, f32[3840]{0:T(1024)S(1)}, u32[]{:S(2)}, u32[]{:S(2)}) collective-permute-start(f32[3840]{0:T(1024)S(1)} %pad_maximum_fusion.2), channel_id=1, source_target_pairs={{0,24},{8,0},{16,8},{24,16},{1,25},{9,1},{17,9},{25,17},{2,26},{10... | collective-permute-start | bytes 46088 | tf_op jit(solution)/shard_map/ppermute | solution.py:285
  24.3 1.9 %collective-permute-start.1 = (f32[3840]{0:T(1024)S(1)}, f32[3840]{0:T(1024)S(1)}, u32[]{:S(2)}, u32[]{:S(2)}) collective-permute-start(f32[3840]{0:T(1024)S(1)} %pad_maximum_fusion.2), channel_id=1, source_target_pairs={{0,16},{8,24},{16,0},{24,8},{1,17},{9,25},{17,1},{25,9},{2,18},{10... | collective-permute-start | bytes 46088 | tf_op jit(solution)/shard_map/ppermute | solution.py:285
  26.2 3.0 %collective-permute-start = (f32[3840]{0:T(1024)S(1)}, f32[3840]{0:T(1024)S(1)}, u32[]{:S(2)}, u32[]{:S(2)}) collective-permute-start(f32[3840]{0:T(1024)S(1)} %pad_maximum_fusion.2), channel_id=1, source_target_pairs={{0,8},{8,16},{16,24},{24,0},{1,9},{9,17},{17,25},{25,1},{2,10},{10... | collective-permute-start | bytes 46088 | tf_op jit(solution)/shard_map/ppermute | solution.py:285
  29.2 0.0 copy-done.5
  29.2 0.1 dynamic-slice_multiply_fusion
  29.3 0.1 mul.89
  29.4 1.2 fusion.1
  30.6 0.0 copy-start
  30.6 0.0 copy-start.1
  30.8 57.8 %collective-permute-done.2 = f32[3840]{0:T(1024)S(1)} collective-permute-done((f32[3840]{0:T(1024)S(1)}, f32[3840]{0:T(1024)S(1)}, u32[]{:S(2)}, u32[]{:S(2)}) %collective-permute-start.2) | collective-permute-done | bytes 15392 | tf_op jit(solution)/shard_map/ppermute | solution.py:285
  88.6 0.0 collective-permute-done.1
  88.6 0.3 collective-permute-done
  89.0 0.1 pad_maximum_fusion
  89.0 0.1 constant_dynamic-slice_fusion.3
  89.1 0.1 pad_maximum_fusion.1
  89.2 0.1 reshape.191
  89.3 0.1 reshape.194
  89.5 0.1 reshape.195
  89.6 0.1 slice.23
  89.6 3.5 %collective-permute-start.4 = (f32[4,16]{0,1:T(8,128)S(1)}, f32[4,16]{0,1:T(8,128)S(1)}, u32[]{:S(2)}, u32[]{:S(2)}) collective-permute-start(f32[4,16]{0,1:T(8,128)S(1)} %slice.23), channel_id=1, source_target_pairs={{0,32},{32,64},{64,96},{96,128},{128,160},{160,192},{192,224},{224... | collective-permute-start | bytes 776 | tf_op jit(solution)/shard_map/ppermute | solution.py:296
  93.1 1.8 %multiply_reduce_fusion = (s32[48]{0:T(128)S(1)}, s32[48]{0:T(128)S(1)}) fusion(s32[48,1,256]{2,1,0:T(1,128)S(1)} %reshape.191), kind=kLoop, calls=%fused_computation.20 | loop fusion | flops 768 | bytes 576 | tf_op jit(solution)/shard_map/mul | solution.py:323
  94.9 0.2 and_select_fusion.marks_ref
  95.2 0.0 collective-permute-done.4
  95.2 0.1 pad_maximum_fusion.4
  95.3 0.1 copy.21
  95.4 0.2 all-to-all-done
  95.6 3.5 %collective-permute-start.3 = (bf16[3,1,2,2,16,384]{5,4,3,2,1,0:T(8,128)(2,1)S(1)}, bf16[3,1,2,2,16,384]{5,4,3,2,1,0:T(8,128)(2,1)S(1)}, u32[]{:S(2)}, u32[]{:S(2)}) collective-permute-start(bf16[3,1,2,2,16,384]{5,4,3,2,1,0:T(8,128)(2,1)S(1)} %slice.22), channel_id=1, source_target_pairs={{0,32},{32,64},{64,96},{96,128},{128,160},{160,192},{192,224},{224... | collective-permute-start | bytes 442376 | tf_op jit(solution)/shard_map/ppermute | solution.py:296
  99.1 0.2 broadcast_in_dim.2.weight_ref
  99.2 0.0 copy-done
  99.2 0.0 copy-done.1
  99.2 7.8 %later_frames.1.given_ref = f32[1168,64]{1,0:T(8,128)S(1)} custom-call(s32[48]{0:T(128)S(1)} %fusion.5.base_ref, bf16[8,4,2,2,16,384]{5,4,3,2,1,0:T(8,128)(2,1)S(1)} %bitcast.19, f32[52,16,128]{2,1,0:T(8,128)S(1)} %broadcast_in_dim.2.weight_ref, s32[48,1,256]{2,1,0:T(1,128)S(1)} %and_select_fusion.marks_ref, ...), custom_call_target="tpu_custom_call" | custom-call | flops 2415919104 | bytes 30000000 | tf_op jit(solution)/shard_map/later_frames/pallas_call | solution.py:258
  107.1 0.0 collective-permute-done.3.tail_ref
  107.1 3.1 %first_frame.1 = f32[64,8,128]{2,1,0:T(8,128)S(1)} custom-call(s32[48]{0:T(128)S(1)} %fusion.5.base_ref, bf16[8,4,2,2,16,384]{5,4,3,2,1,0:T(8,128)(2,1)S(1)} %bitcast.20, bf16[3,1,2,2,16,384]{5,4,3,2,1,0:T(8,128)(2,1)S(1)} %collective-permute-done.3.tail_ref, f32[52,16,128]{2,1,0:T(8,128)S(1)} %broadcast_in_dim.2.weight_ref, ...), custom_call_target="tpu_custom_call" | custom-call | flops 805306368 | bytes 10000000 | tf_op jit(solution)/shard_map/first_frame/pallas_call | solution.py:269
  110.2 21.4 %all_to_all.10 = f32[64,8,128]{2,1,0:T(8,128)S(1)} all-to-all(f32[64,8,128]{2,1,0:T(8,128)S(1)} %first_frame.1), channel_id=1, replica_groups=mesh['xy'=16,'zl'=4,'chan'=8] {'xy','zl'}, dimensions={0} | all-to-all | bytes 524288 | tf_op jit(solution)/shard_map/all_to_all | solution.py:328
  131.6 1.4 %reshape.196 = f32[16,4,8,2,4,16]{5,4,3,2,1,0:T(4,128)S(1)} reshape(f32[64,8,128]{2,1,0:T(8,128)S(1)} %all_to_all.10) | data formatting | bytes 524288 | tf_op jit(solution)/shard_map/reshape | solution.py:329
  133.0 0.5 reduce_sum.9
  133.6 0.1 copy.24
  133.7 0.7 reshape.198
  (19 shorter events, 0.3 us)
Async XLA Ops:
  2.8 15.6 %copy-start.2 = (s32[3072]{0:T(1024)S(1)}, s32[3072]{0:T(1024)}, u32[]{:S(2)}) copy-start(s32[3072]{0:T(1024)} %param.11) | copy-start | bytes 36868
  2.8 15.7 %copy-start.3 = (f32[64,12]{0,1:T(8,128)S(1)}, f32[64,12]{0,1:T(8,128)}, u32[]{:S(2)}) copy-start(f32[64,12]{0,1:T(8,128)} %param.8) | copy-start | bytes 9220
  2.8 15.7 %copy-start.4 = (s32[64,12]{0,1:T(8,128)S(1)}, s32[64,12]{0,1:T(8,128)}, u32[]{:S(2)}) copy-start(s32[64,12]{0,1:T(8,128)} %param.9) | copy-start | bytes 9220
  2.8 26.4 %copy-start.5 = (f32[64]{0:T(128)S(1)}, f32[64]{0:T(128)}, u32[]{:S(2)}) copy-start(f32[64]{0:T(128)} %param.10) | copy-start | bytes 772
  2.9 92.7 %all-to-all-start = ((bf16[32,2,2,16,384]{4,3,2,1,0:T(8,128)(2,1)}), bf16[32,2,2,16,384]{4,3,2,1,0:T(8,128)(2,1)S(1)}, u32[]{:S(2)}, u32[]{:S(2)}) async-start(bf16[32,2,2,16,384]{4,3,2,1,0:T(8,128)(2,1)} %bitcast.16), calls=%async_computation | async-start | bytes 3145728 | tf_op jit(solution)/shard_map/all_to_all | solution.py:309
  18.8 69.8 %collective-permute-start.2 = (f32[3840]{0:T(1024)S(1)}, f32[3840]{0:T(1024)S(1)}, u32[]{:S(2)}, u32[]{:S(2)}) collective-permute-start(f32[3840]{0:T(1024)S(1)} %pad_maximum_fusion.2), channel_id=1, source_target_pairs={{0,24},{8,0},{16,8},{24,16},{1,25},{9,1},{17,9},{25,17},{2,26},{10... | collective-permute-start | bytes 46088 | tf_op jit(solution)/shard_map/ppermute | solution.py:285
  24.3 64.3 %collective-permute-start.1 = (f32[3840]{0:T(1024)S(1)}, f32[3840]{0:T(1024)S(1)}, u32[]{:S(2)}, u32[]{:S(2)}) collective-permute-start(f32[3840]{0:T(1024)S(1)} %pad_maximum_fusion.2), channel_id=1, source_target_pairs={{0,16},{8,24},{16,0},{24,8},{1,17},{9,25},{17,1},{25,9},{2,18},{10... | collective-permute-start | bytes 46088 | tf_op jit(solution)/shard_map/ppermute | solution.py:285
  26.2 62.8 %collective-permute-start = (f32[3840]{0:T(1024)S(1)}, f32[3840]{0:T(1024)S(1)}, u32[]{:S(2)}, u32[]{:S(2)}) collective-permute-start(f32[3840]{0:T(1024)S(1)} %pad_maximum_fusion.2), channel_id=1, source_target_pairs={{0,8},{8,16},{16,24},{24,0},{1,9},{9,17},{17,25},{25,1},{2,10},{10... | collective-permute-start | bytes 46088 | tf_op jit(solution)/shard_map/ppermute | solution.py:285
  30.6 68.6 %copy-start = (bf16[2,256,256]{2,1,0:T(8,128)(2,1)S(1)}, bf16[2,256,256]{2,1,0:T(8,128)(2,1)}, u32[]{:S(2)}) copy-start(bf16[2,256,256]{2,1,0:T(8,128)(2,1)} %constant.98.clone.table_ref) | copy-start | bytes 786436
  30.6 68.6 %copy-start.1 = (f32[2,32,128]{2,1,0:T(8,128)S(1)}, f32[2,32,128]{2,1,0:T(8,128)}, u32[]{:S(2)}) copy-start(f32[2,32,128]{2,1,0:T(8,128)} %constant.97.clone.twist_ref) | copy-start | bytes 98308
  89.6 5.5 %collective-permute-start.4 = (f32[4,16]{0,1:T(8,128)S(1)}, f32[4,16]{0,1:T(8,128)S(1)}, u32[]{:S(2)}, u32[]{:S(2)}) collective-permute-start(f32[4,16]{0,1:T(8,128)S(1)} %slice.23), channel_id=1, source_target_pairs={{0,32},{32,64},{64,96},{96,128},{128,160},{160,192},{192,224},{224... | collective-permute-start | bytes 776 | tf_op jit(solution)/shard_map/ppermute | solution.py:296
  95.6 11.5 %collective-permute-start.3 = (bf16[3,1,2,2,16,384]{5,4,3,2,1,0:T(8,128)(2,1)S(1)}, bf16[3,1,2,2,16,384]{5,4,3,2,1,0:T(8,128)(2,1)S(1)}, u32[]{:S(2)}, u32[]{:S(2)}) collective-permute-start(bf16[3,1,2,2,16,384]{5,4,3,2,1,0:T(8,128)(2,1)S(1)} %slice.22), channel_id=1, source_target_pairs={{0,32},{32,64},{64,96},{96,128},{128,160},{160,192},{192,224},{224... | collective-permute-start | bytes 442376 | tf_op jit(solution)/shard_map/ppermute | solution.py:296

commit v2 on v1

--- a/solution.py
+++ b/solution.py
@@ -104,9 +104,10 @@
 
 
 def frame_profile(
-    row_of, weight_of, base_of, marks_of, chirp_ref, twist_ref, table_ref, mid, y_ref, v_ref, stokes_ref, acc
+    row_of, weight_of, base_of, marks_of, chirp_ref, twist_ref, table_ref, mid, y_refs, v_refs, stokes_ref, acc
 ):
     for pol in range(2):
+        y_ref, v_ref = y_refs.at[pol], v_refs.at[pol]
         for b in range(4):
             rows = []
             for a in range(8):
@@ -130,18 +131,18 @@
                     where = (pl.ds(GROUP * k, GROUP), pl.ds(LANES * part, LANES))
                     y_ref[0, *where] = high
                     y_ref[1, *where] = low
-        for m in range(4):
-            rows = pl.ds(8 * GROUP * m, 8 * GROUP)
+        for m in range(2):
+            rows = pl.ds(16 * GROUP * m, 16 * GROUP)
             spectrum = lane_dft(y_ref[0, rows], y_ref[1, rows], table_ref[0], table_ref[1])
             re, im = spectrum[:, :LANES], spectrum[:, LANES:]
             cos, sin = chirp_ref[0, rows], chirp_ref[1, rows]
             swapped = jnp.concatenate([re * sin + im * cos, re * cos - im * sin], axis=1)
             back = lane_dft(*split(swapped), table_ref[0], table_ref[1])
-            im, re = (back[:, part].reshape(8, GROUP, LANES) for part in (slice(0, LANES), slice(LANES, None)))
-            cos = twist_ref[0, 8 * m : 8 * m + 8][:, None, :]
-            sin = twist_ref[1, 8 * m : 8 * m + 8][:, None, :]
-            v_ref[0, 8 * m : 8 * m + 8] = re * cos + im * sin
-            v_ref[1, 8 * m : 8 * m + 8] = im * cos - re * sin
+            im, re = (back[:, part].reshape(16, GROUP, LANES) for part in (slice(0, LANES), slice(LANES, None)))
+            cos = twist_ref[0, 16 * m : 16 * m + 16][:, None, :]
+            sin = twist_ref[1, 16 * m : 16 * m + 16][:, None, :]
+            v_ref[0, 16 * m : 16 * m + 16] = re * cos + im * sin
+            v_ref[1, 16 * m : 16 * m + 16] = im * cos - re * sin
         for b in range(4):
             values = dft8([(v_ref[0, 4 * a + b], v_ref[1, 4 * a + b]) for a in range(8)], 1)
             for na, value in enumerate(values):
@@ -176,9 +177,34 @@
     return buf_ref[row // 3, slab, pol, part, :, pl.ds(LANES * (row % 3), LANES)]
 
 
-def later_kernel(
-    base_ref, buf_ref, weight_ref, marks_ref, chirp_ref, twist_ref, table_ref, acc_ref, mid, y_ref, v_ref, stokes_ref
-):
+def turn_of(me, slab):
+    return (me - slab + RUNS) % RUNS
+
+
+def base_from(base_refs, turn, m):
+    value = base_refs[RUNS - 1][m]
+    for other in range(RUNS - 1):
+        value = jnp.where(turn == other, base_refs[other][m], value)
+    return value
+
+
+def lay_gains(gains, weights_of):
+    for block in range(ROWS // 2):
+        gains[block] = jnp.broadcast_to(weights_of(block), (GROUP, LANES))
+
+
+def marks_from(marks_ref, index, m):
+    return jnp.concatenate([marks_ref[index, 2 * m : 2 * m + 1], marks_ref[index, 2 * m + 1 : 2 * m + 2]], axis=1)
+
+
+def later_kernel(me_ref, *refs):
+    base_refs, refs = refs[:RUNS], refs[RUNS:]
+    letter_refs, refs = refs[:RUNS], refs[RUNS:]
+    buf_ref, chirp_ref, twist_ref, table_ref, acc_ref, sorted_ref, gains, marks, *scratches = refs
+    me = me_ref[0]
+    for turn in range(RUNS):
+        sorted_ref[(me - turn + RUNS) % RUNS] = letter_refs[turn][...]
+    marks[...] = sorted_ref[:, GROUP:].astype(jnp.int32)
     acc_ref[...] = jnp.zeros_like(acc_ref)
 
     def step(frame, carry):
@@ -187,18 +213,24 @@
                 return own_row(buf_ref, frame - 1, row + KEPT - RIM, pol, part)
             return own_row(buf_ref, frame, row - RIM, pol, part)
 
+        before, own = sorted_ref[frame - 1, :GROUP], sorted_ref[frame, :GROUP]
+
+        def weights_of(block):
+            if block < RIM // 2:
+                return before[:, block + BLOCKS - RIM // 2 : block + BLOCKS - RIM // 2 + 1]
+            return own[:, block - RIM // 2 : block - RIM // 2 + 1]
+
+        lay_gains(gains, weights_of)
+        turn = turn_of(me, frame)
         frame_profile(
             row_of,
-            lambda block: weight_ref[BLOCKS * frame + block],
-            lambda m: base_ref[BLOCKS * frame + m],
-            lambda m: marks_ref[BLOCKS * frame + m],
+            lambda block: gains[block],
+            lambda m: base_from(base_refs, turn, m),
+            lambda m: marks_from(marks, frame, m),
             chirp_ref,
             twist_ref,
             table_ref,
-            mid,
-            y_ref,
-            v_ref,
-            stokes_ref,
+            *scratches,
             acc_ref,
         )
         return carry
@@ -206,29 +238,36 @@
     lax.fori_loop(1, RUNS, step, 0)
 
 
-def first_kernel(
-    base_ref, buf_ref, tail_ref, weight_ref, marks_ref, chirp_ref, twist_ref, table_ref, given_ref, out_ref,
-    acc, mid, y_ref, v_ref, stokes_ref,
-):
+def first_kernel(me_ref, *refs):
+    base_refs, refs = refs[:RUNS], refs[RUNS:]
+    rim_refs, refs = refs[:RUNS], refs[RUNS:]
+    buf_ref, tail_ref, sorted_ref, chirp_ref, twist_ref, table_ref, given_ref, out_ref, acc, gains, marks, *scratches = refs
     acc[...] = given_ref[...]
+    before = (rim_refs[0][...] + rim_refs[1][...]) + (rim_refs[2][...] + rim_refs[3][...])
+    own = sorted_ref[0, :GROUP]
+    marks[0] = sorted_ref[0, GROUP:].astype(jnp.int32)
+
+    def weights_of(block):
+        if block < RIM // 2:
+            return before[:, block + BLOCKS - RIM // 2 : block + BLOCKS - RIM // 2 + 1]
+        return own[:, block - RIM // 2 : block - RIM // 2 + 1]
 
     def row_of(row, pol, part):
         if row < RIM:
             return own_row(tail_ref, 0, row + 1, pol, part)
         return own_row(buf_ref, 0, row - RIM, pol, part)
 
+    lay_gains(gains, weights_of)
+    turn = turn_of(me_ref[0], 0)
     frame_profile(
         row_of,
-        lambda block: weight_ref[block],
-        lambda m: base_ref[m],
-        lambda m: marks_ref[m],
+        lambda block: gains[block],
+        lambda m: base_from(base_refs, turn, m),
+        lambda m: marks_from(marks, 0, m),
         chirp_ref,
         twist_ref,
         table_ref,
-        mid,
-        y_ref,
-        v_ref,
-        stokes_ref,
+        *scratches,
         acc,
     )
     acc[:WINDOW] += acc[NBIN:]
@@ -239,8 +278,8 @@
 def scratch():
     return [
         pltpu.VMEM((2, 2, 4, 8, GROUP, LANES), jnp.float32),
-        pltpu.VMEM((2, ROWS * GROUP, 2 * LANES), jnp.bfloat16),
-        pltpu.VMEM((2, ROWS, GROUP, LANES), jnp.float32),
+        pltpu.VMEM((2, 2, ROWS * GROUP, 2 * LANES), jnp.bfloat16),
+        pltpu.VMEM((2, 2, ROWS, GROUP, LANES), jnp.float32),
         pltpu.VMEM((BLOCKS, 4 * GROUP, BLK), jnp.bfloat16),
     ]
 
@@ -249,46 +288,71 @@
     return pl.BlockSpec(memory_space=pltpu.VMEM)
 
 
-def fold_frames(buf, tail_of, weight, base, marks, chirp):
+def smem():
+    return pl.BlockSpec(memory_space=pltpu.SMEM)
+
+
+def fold_frames(buf, tail_of, me, bases, letters, rims, chirp):
     twist = jnp.asarray(np.stack(twist_tables()))
     table = jnp.asarray(np.stack(lane_tables()))
     tail = tail_of(buf)
     params = pltpu.CompilerParams(vmem_limit_bytes=28 * 1024 * 1024)
     flops = 2 * 2 * 2 * 3 * ROWS * GROUP * 256 * 256
-    later = pl.pallas_call(
+    letter_rows = GROUP + KEPT
+    later, ordered = pl.pallas_call(
         later_kernel,
-        out_shape=jax.ShapeDtypeStruct((ACC_ROWS, 4 * GROUP), jnp.float32),
-        in_specs=[pl.BlockSpec(memory_space=pltpu.SMEM)] + [whole()] * 6,
-        out_specs=whole(),
-        scratch_shapes=scratch(),
+        out_shape=[
+            jax.ShapeDtypeStruct((ACC_ROWS, 4 * GROUP), jnp.float32),
+            jax.ShapeDtypeStruct((RUNS, letter_rows, LANES), jnp.float32),
+        ],
+        in_specs=[smem()] * (1 + RUNS) + [whole()] * (RUNS + 4),
+        out_specs=[whole()] * 2,
+        scratch_shapes=[
+            pltpu.VMEM((ROWS // 2, GROUP, LANES), jnp.float32),
+            pltpu.VMEM((RUNS, KEPT, LANES), jnp.int32),
+        ]
+        + scratch(),
         compiler_params=params,
         cost_estimate=pl.CostEstimate(flops=3 * flops, bytes_accessed=30_000_000, transcendentals=0),
         name="later_frames",
-    )(base, buf, weight, marks, chirp, twist, table)
+    )(me, *bases, *letters, buf, chirp, twist, table)
     block = (MEMBERS, 1) + buf.shape[2:]
     return pl.pallas_call(
         first_kernel,
         out_shape=jax.ShapeDtypeStruct((NBIN // 16, 8, LANES), jnp.float32),
         grid=(1,),
-        in_specs=[pl.BlockSpec(memory_space=pltpu.SMEM), pl.BlockSpec(block, lambda i: (0,) * 6)] + [whole()] * 7,
+        in_specs=[smem()] * (1 + RUNS)
+        + [whole()] * RUNS
+        + [pl.BlockSpec(block, lambda i: (0,) * 6)]
+        + [whole()] * 6,
         out_specs=whole(),
-        scratch_shapes=[pltpu.VMEM((ACC_ROWS, 4 * GROUP), jnp.float32)] + scratch(),
+        scratch_shapes=[
+            pltpu.VMEM((ACC_ROWS, 4 * GROUP), jnp.float32),
+            pltpu.VMEM((ROWS // 2, GROUP, LANES), jnp.float32),
+            pltpu.VMEM((1, KEPT, LANES), jnp.int32),
+        ]
+        + scratch(),
         compiler_params=params,
         cost_estimate=pl.CostEstimate(flops=flops, bytes_accessed=10_000_000, transcendentals=0),
         name="first_frame",
-    )(base, buf, tail, weight, marks, chirp, twist, table, later)
-
-
-def gathered(block, axis):
+    )(me, *bases, *rims, buf, tail, ordered, chirp, twist, table, later)
+
+
+def last_kernel(scale, shares_ref, out_ref):
+    for slab in range(RUNS):
+        total = jnp.sum(shares_ref[:, slab], axis=0) * scale
+        for half in range(2):
+            for s in range(4):
+                lanes = slice(64 * half + GROUP * s, 64 * half + GROUP * (s + 1))
+                out_ref[8 * half : 8 * half + 8, s, GROUP * slab : GROUP * (slab + 1)] = total[:, lanes]
+
+
+def turned_to(block_for, axis, turn):
     size = lax.axis_size(axis)
-    parts = [block] + [
-        lax.ppermute(block, axis, [(i, (i + turn) % size) for i in range(size)]) for turn in range(1, size)
-    ]
-    me = lax.axis_index(axis)
-    pile = jnp.stack(parts)
-    return jnp.concatenate(
-        [lax.dynamic_slice_in_dim(pile, (me - i + size) % size, 1, 0) for i in range(size)]
-    )
+    there = (lax.axis_index(axis) + turn) % size
+    if turn == 0:
+        return block_for(there)
+    return lax.ppermute(block_for(there), axis, [(i, (i + turn) % size) for i in range(size)])
 
 
 def from_before(block):
@@ -311,23 +375,39 @@
 
     me = lax.axis_index("zl")
     weight = scales * (1 - flags).astype(jnp.float32)
-    message = jnp.concatenate([weight.reshape(-1), phase_bin.astype(jnp.float32)])
-    letters = gathered(message, "zl")
-    count = scales.shape[0] * BLOCKS
-    weights = letters[:, :count].reshape(RUNS, scales.shape[0], BLOCKS)
-    weights = lax.dynamic_slice_in_dim(weights, me * GROUP, GROUP, 1)
-    weights = weights.transpose(0, 2, 1).reshape(RUNS * BLOCKS, GROUP)
-    weights = jnp.concatenate([from_before(weights[-(OVER // BLK) :]), weights])
-    weights = jnp.broadcast_to(weights[:, :, None], weights.shape + (LANES,))
-    bins = letters[:, count:].astype(jnp.int32).reshape(RUNS * BLOCKS, 1, BLK)
-    base = bins[:, 0, 0] // 8 * 8
-    marks = (bins - base[:, None, None]) % NBIN
+    weight = jnp.pad(weight, ((0, 0), (0, LANES - BLOCKS)))
+    bins = phase_bin.reshape(KEPT, LANES)
+    base = bins[::2, 0] // 8 * 8
+    marks = (bins - jnp.repeat(base, 2)[:, None]) % NBIN
+
+    def weights_for(place):
+        return lax.dynamic_slice_in_dim(weight, place * GROUP, GROUP, 0)
+
+    def letter_for(place):
+        return jnp.concatenate([weights_for(place), marks.astype(jnp.float32)])
+
+    letters = [turned_to(letter_for, "zl", turn) for turn in range(RUNS)]
+    bases = [turned_to(lambda place: base, "zl", turn) for turn in range(RUNS)]
+    size = lax.axis_size("xy")
+    rims = [
+        lax.ppermute(
+            weight[GROUP * place : GROUP * (place + 1)],
+            ("xy", "zl"),
+            [(i * RUNS + RUNS - 1, (i + 1) * RUNS + place) for i in range(size - 1)],
+        )
+        for place in range(RUNS)
+    ]
     chirp = chirp_table(lax.dynamic_slice_in_dim(sweep, me * GROUP, GROUP, 0))
 
-    partial = fold_frames(buf, lambda b: from_before(b[5:, RUNS - 1 :]), weights, base, marks, chirp)
+    partial = fold_frames(
+        buf, lambda b: from_before(b[5:, RUNS - 1 :]), me.reshape(1), bases, letters, rims, chirp
+    )
     shares = lax.all_to_all(partial, ("xy", "zl"), split_axis=0, concat_axis=0, tiled=True)
-    total = shares.reshape(-1, RUNS, 8, 2, 4, GROUP).sum(0) * (NBIN / (SLAB * RUNS * lax.axis_size("xy")))
-    return total.transpose(2, 1, 3, 0, 4).reshape(16, 4, RUNS * GROUP)
+    return pl.pallas_call(
+        functools.partial(last_kernel, NBIN / (SLAB * RUNS * size)),
+        out_shape=jax.ShapeDtypeStruct((16, 4, RUNS * GROUP), jnp.float32),
+        name="last_sum",
+    )(shares.reshape(-1, RUNS, 8, LANES))
 
 
 def solution(mesh):

time: 135 us -> 149 us (1.10)
  starting transfers between devices: 33 us -> 41.8 us
  blocking collectives: 21.4 us -> 26.3 us
  waiting for transfers between devices: 58.3 us -> 61.2 us
  local copies, waits for them, and re-layouts: 6.19 us -> 3.39 us
  other arithmetic: 4.19 us -> 1.54 us
  Pallas kernels: 10.9 us -> 13.4 us
    all_to_all x1, waiting for transfers between devices: 0.18 us -> 58.9 us  [on_device(): lax.all_to_all(parts, ('chan', 'zl'), split_axis=0, concat_axis=0, tiled=...]
    ppermute x3 -> x10, waiting for transfers between devices: 58.1 us -> 2.22 us  [the longest x6 2.21 us: turned_to(): lax.ppermute(block_for(there), axis, [(i, (i + turn) % size) for i in ran...]
    ppermute x3 -> x10, starting transfers between devices: 10.4 us -> 22.7 us  [the longest x6 19.4 us: turned_to(): lax.ppermute(block_for(there), axis, [(i, (i + turn) % size) for i in ran...]
    all_to_all x1, blocking collectives: 21.4 us -> 26.3 us  [on_device(): lax.all_to_all(partial, ('xy', 'zl'), split_axis=0, concat_axis=0, tiled=...]
    ppermute x2 -> x1, starting transfers between devices: 6.96 us -> 3.48 us  [from_before(): return lax.ppermute(block, 'xy', [(i, i + 1) for i in range(size - 1)])]
    reshape x7 -> x0, local copies, waits for them, and re-layouts: 2.63 us -> none  [the longest x1 1.4 us: on_device(): shares.reshape(-1, RUNS, 8, 2, 4, GROUP).sum(0)]
    pallas_call x1 -> x2, Pallas kernels: 7.8 us -> 10.2 us  [the longest x1 8.27 us: fold_frames(): pl.pallas_call(later_kernel, out_shape=[jax.ShapeDtypeStruct((ACC_ROWS, 4...]
    mul x3 -> x1, other arithmetic: 1.85 us -> 0.01 us  [on_device(): base = bins[::2, 0] // 8 * 8]
  transfers between devices with their start and end apart: 6 -> 12, of which waited for: 3 -> 2; matrix products, arithmetic and copies ran while one was open for 3% -> 1% of each run, Pallas kernels for 6% -> 6%
where the time goes in v2:
time: 149 us; the launch traced here: 148 us
  waiting for transfers between devices  61.2 us (41%)
  starting transfers between devices  41.8 us (28%)
  blocking collectives  26.3 us (18%)
  Pallas kernels  13.4 us (9%)
  local copies, waits for them, and re-layouts  3.39 us (2%)
  other arithmetic  1.54 us (1%)
    all_to_all x1, waiting for transfers between devices, on_device(): lax.all_to_all(parts, ('chan', 'zl'), split_axis=0, concat_axis=0, tiled=...  58.9 us
    all_to_all x1, blocking collectives, on_device(): lax.all_to_all(partial, ('xy', 'zl'), split_axis=0, concat_axis=0, tiled=...  26.3 us
    ppermute x6, starting transfers between devices, turned_to(): lax.ppermute(block_for(there), axis, [(i, (i + turn) % size) for i in ran...  19.4 us
    all_to_all x1, starting transfers between devices, on_device(): lax.all_to_all(parts, ('chan', 'zl'), split_axis=0, concat_axis=0, tiled=...  15.6 us
    pallas_call x1, Pallas kernels, fold_frames(): pl.pallas_call(later_kernel, out_shape=[jax.ShapeDtypeStruct((ACC_ROWS, 4...  8.27 us
    ppermute x1, starting transfers between devices, from_before(): return lax.ppermute(block, 'xy', [(i, i + 1) for i in range(size - 1)])  3.48 us
    ppermute x4, starting transfers between devices, on_device(): lax.ppermute(weight[GROUP * place:GROUP * (place + 1)], ('xy', 'zl'), [(i...  3.27 us
    pallas_call x1, Pallas kernels, fold_frames(): pl.pallas_call(first_kernel, out_shape=jax.ShapeDtypeStruct((NBIN // 16,...  3.21 us
  transfers between devices with their start and end apart: 12, of which 2 were waited for; matrix products, arithmetic and copies ran while one was open for 1% of the time, Pallas kernels for 6%

profile of v2, /device:TPU:8, one launch (start us, length us, event | category | flops | bytes accessed | tf_op | source)
XLA Modules:
  0.0 148.0 jit_solution(17642880394534511507)
XLA Ops:
  0.0 2.9 %copy.20 = bf16[2,2,32,16,384]{4,3,1,0,2:T(8,128)(2,1)} copy(bf16[2,2,32,16,384]{4,3,2,1,0:T(8,128)(2,1)} %bitcast.19) | data formatting | bytes 3145728 | tf_op jit(solution)/shard_map/reshape | solution.py:372
  2.9 0.0 copy-start.2
  2.9 0.0 copy-start.3
  2.9 0.0 copy-start.4
  2.9 0.0 copy-start.5
  2.9 15.6 %all-to-all-start = ((bf16[32,2,2,16,384]{4,3,2,1,0:T(8,128)(2,1)}), bf16[32,2,2,16,384]{4,3,2,1,0:T(8,128)(2,1)S(1)}, u32[]{:S(2)}, u32[]{:S(2)}) async-start(bf16[32,2,2,16,384]{4,3,2,1,0:T(8,128)(2,1)} %bitcast.14), calls=%async_computation | async-start | bytes 3145728 | tf_op jit(solution)/shard_map/all_to_all | solution.py:373
  18.5 0.0 copy-start
  18.5 0.0 copy-start.1
  18.5 0.0 copy-done.2
  18.6 0.1 reduce
  18.7 3.7 %collective-permute-start = (s32[12]{0:T(128)S(1)}, s32[12]{0:T(128)S(1)}, u32[]{:S(2)}, u32[]{:S(2)}) collective-permute-start(s32[12]{0:T(128)S(1)} %fusion.6.refs_0_), channel_id=1, source_target_pairs={{0,8},{8,16},{16,24},{24,0},{1,9},{9,17},{17,25},{25,1},{2,10},{10... | collective-permute-start | bytes 152 | tf_op jit(solution)/shard_map/ppermute | solution.py:355
  22.4 4.3 %collective-permute-start.1 = (s32[12]{0:T(128)S(1)}, s32[12]{0:T(128)S(1)}, u32[]{:S(2)}, u32[]{:S(2)}) collective-permute-start(s32[12]{0:T(128)S(1)} %fusion.6.refs_0_), channel_id=1, source_target_pairs={{0,16},{8,24},{16,0},{24,8},{1,17},{9,25},{17,1},{25,9},{2,18},{10... | collective-permute-start | bytes 152 | tf_op jit(solution)/shard_map/ppermute | solution.py:355
  26.7 0.0 copy-done.3
  26.7 0.1 copy.16
  26.8 0.0 copy-done.4
  26.8 0.1 copy.15
  26.9 0.1 broadcast_in_dim.2
  27.0 0.1 sub.27
  27.2 0.1 fusion.5
  27.2 2.1 %collective-permute-start.8 = (f32[40,128]{1,0:T(8,128)S(1)}, f32[40,128]{1,0:T(8,128)S(1)}, u32[]{:S(2)}, u32[]{:S(2)}) collective-permute-start(f32[40,128]{1,0:T(8,128)S(1)} %get-tuple-element.20), channel_id=1, source_target_pairs={{0,8},{8,16},{16,24},{24,0},{1,9},{9,17},{17,25},{25,1},{2,10},{10... | collective-permute-start | bytes 61448 | tf_op jit(solution)/shard_map/ppermute | solution.py:355
  29.4 3.7 %collective-permute-start.9 = (f32[40,128]{1,0:T(8,128)S(1)}, f32[40,128]{1,0:T(8,128)S(1)}, u32[]{:S(2)}, u32[]{:S(2)}) collective-permute-start(f32[40,128]{1,0:T(8,128)S(1)} %get-tuple-element.21), channel_id=1, source_target_pairs={{0,16},{8,24},{16,0},{24,8},{1,17},{9,25},{17,1},{25,9},{2,18},{10... | collective-permute-start | bytes 61448 | tf_op jit(solution)/shard_map/ppermute | solution.py:355
  33.1 3.7 %collective-permute-start.10 = (f32[40,128]{1,0:T(8,128)S(1)}, f32[40,128]{1,0:T(8,128)S(1)}, u32[]{:S(2)}, u32[]{:S(2)}) collective-permute-start(f32[40,128]{1,0:T(8,128)S(1)} %get-tuple-element.19), channel_id=1, source_target_pairs={{0,24},{8,0},{16,8},{24,16},{1,25},{9,1},{17,9},{25,17},{2,26},{10... | collective-permute-start | bytes 61448 | tf_op jit(solution)/shard_map/ppermute | solution.py:355
  36.8 0.0 copy-done.5
  36.8 0.1 dynamic-slice_multiply_fusion
  36.9 0.1 mul.90
  37.1 1.2 fusion.1
  38.3 58.9 %all-to-all-done = bf16[32,2,2,16,384]{4,3,2,1,0:T(8,128)(2,1)S(1)} async-done(((bf16[32,2,2,16,384]{4,3,2,1,0:T(8,128)(2,1)}), bf16[32,2,2,16,384]{4,3,2,1,0:T(8,128)(2,1)S(1)}, u32[]{:S(2)}, u32[]{:S(2)}) %all-to-all-start) | async-done | bytes 1572896 | tf_op jit(solution)/shard_map/all_to_all | solution.py:373
  97.2 0.0 collective-permute-done.refs_1_
  97.3 1.9 %collective-permute-start.2 = (s32[12]{0:T(128)S(1)}, s32[12]{0:T(128)S(1)}, u32[]{:S(2)}, u32[]{:S(2)}) collective-permute-start(s32[12]{0:T(128)S(1)} %fusion.6.refs_0_), channel_id=1, source_target_pairs={{0,24},{8,0},{16,8},{24,16},{1,25},{9,1},{17,9},{25,17},{2,26},{10... | collective-permute-start | bytes 152 | tf_op jit(solution)/shard_map/ppermute | solution.py:355
  99.2 0.0 collective-permute-done.1.refs_2_
  99.2 1.3 collective-permute-start.3
  100.5 2.2 %collective-permute-done.2.refs_3_ = s32[12]{0:T(128)S(1)} collective-permute-done((s32[12]{0:T(128)S(1)}, s32[12]{0:T(128)S(1)}, u32[]{:S(2)}, u32[]{:S(2)}) %collective-permute-start.2) | collective-permute-done | bytes 80 | tf_op jit(solution)/shard_map/ppermute | solution.py:355
  102.7 0.7 collective-permute-start.4
  103.3 0.0 collective-permute-done.8.refs_5_
  103.4 0.7 collective-permute-start.5
  104.0 0.0 collective-permute-done.9.refs_6_
  104.0 0.7 collective-permute-start.6
  104.7 0.0 collective-permute-done.10.refs_7_
  104.7 3.5 %collective-permute-start.7 = (bf16[3,1,2,2,16,384]{5,4,3,2,1,0:T(8,128)(2,1)S(1)}, bf16[3,1,2,2,16,384]{5,4,3,2,1,0:T(8,128)(2,1)S(1)}, u32[]{:S(2)}, u32[]{:S(2)}) collective-permute-start(bf16[3,1,2,2,16,384]{5,4,3,2,1,0:T(8,128)(2,1)S(1)} %slice.24), channel_id=1, source_target_pairs={{0,32},{32,64},{64,96},{96,128},{128,160},{160,192},{192,224},{224... | collective-permute-start | bytes 442376 | tf_op jit(solution)/shard_map/ppermute | solution.py:360
  108.2 0.0 copy-done
  108.2 0.0 copy-done.1
  108.2 8.3 %later_frames.1 = (f32[1168,64]{1,0:T(8,128)S(1)}, f32[4,40,128]{2,1,0:T(8,128)S(1)}) custom-call(s32[1]{0:T(128)} %bitcast.me_ref, s32[12]{0:T(128)S(1)} %fusion.6.refs_0_, s32[12]{0:T(128)S(1)} %collective-permute-done.refs_1_, s32[12]{0:T(128)S(1)} %collective-permute-done.1.refs_2_, s32[12]{0:T(128)S(1)} %collective-permute-done.2.refs_3_, ...), custom_call_target="tpu_custom_call" | custom-call | flops 2415919104 | bytes 30000000 | tf_op jit(solution)/shard_map/later_frames/pallas_call | solution.py:302
  116.5 0.0 collective-permute-done.3.refs_4_
  116.5 0.0 collective-permute-done.4.refs_5_
  116.5 0.0 collective-permute-done.5.refs_6_
  116.5 0.0 collective-permute-done.6.refs_7_
  116.5 0.0 collective-permute-done.7.refs_9_
  116.6 3.2 %first_frame.1 = f32[64,8,128]{2,1,0:T(8,128)S(1)} custom-call(s32[1]{0:T(128)} %bitcast.me_ref, s32[12]{0:T(128)S(1)} %fusion.6.refs_0_, s32[12]{0:T(128)S(1)} %collective-permute-done.refs_1_, s32[12]{0:T(128)S(1)} %collective-permute-done.1.refs_2_, s32[12]{0:T(128)S(1)} %collective-permute-done.2.refs_3_, f32[16,128]{1,0:T(8,128)S(1)} %collective-permute-done.3.refs_4_, ...), custom_call_target="tpu_custom_call" | custom-call | flops 805306368 | bytes 10000000 | tf_op jit(solution)/shard_map/first_frame/pallas_call | solution.py:320
  119.8 26.3 %all_to_all.10 = f32[64,8,128]{2,1,0:T(8,128)} all-to-all(f32[64,8,128]{2,1,0:T(8,128)S(1)} %first_frame.1), channel_id=1, replica_groups=mesh['xy'=16,'zl'=4,'chan'=8] {'xy','zl'}, dimensions={0} | all-to-all | bytes 524288 | tf_op jit(solution)/shard_map/all_to_all | solution.py:405
  146.1 1.9 %last_sum.1 = f32[16,4,64]{2,1,0:T(4,128)} custom-call(f32[16,4,8,128]{3,2,1,0:T(8,128)} %bitcast.21), custom_call_target="tpu_custom_call" | custom-call | tf_op jit(solution)/shard_map/last_sum/pallas_call | solution.py:406
  (11 shorter events, 0.2 us)
Async XLA Ops:
  2.9 15.7 %copy-start.2 = (s32[3072]{0:T(1024)S(1)}, s32[3072]{0:T(1024)}, u32[]{:S(2)}) copy-start(s32[3072]{0:T(1024)} %param.11) | copy-start | bytes 36868
  2.9 23.9 %copy-start.3 = (f32[64,12]{0,1:T(8,128)S(1)}, f32[64,12]{0,1:T(8,128)}, u32[]{:S(2)}) copy-start(f32[64,12]{0,1:T(8,128)} %param.8) | copy-start | bytes 9220
  2.9 24.0 %copy-start.4 = (s32[64,12]{0,1:T(8,128)S(1)}, s32[64,12]{0,1:T(8,128)}, u32[]{:S(2)}) copy-start(s32[64,12]{0,1:T(8,128)} %param.9) | copy-start | bytes 9220
  2.9 34.0 %copy-start.5 = (f32[64]{0:T(128)S(1)}, f32[64]{0:T(128)}, u32[]{:S(2)}) copy-start(f32[64]{0:T(128)} %param.10) | copy-start | bytes 772
  2.9 94.3 %all-to-all-start = ((bf16[32,2,2,16,384]{4,3,2,1,0:T(8,128)(2,1)}), bf16[32,2,2,16,384]{4,3,2,1,0:T(8,128)(2,1)S(1)}, u32[]{:S(2)}, u32[]{:S(2)}) async-start(bf16[32,2,2,16,384]{4,3,2,1,0:T(8,128)(2,1)} %bitcast.14), calls=%async_computation | async-start | bytes 3145728 | tf_op jit(solution)/shard_map/all_to_all | solution.py:373
  18.5 89.7 %copy-start = (bf16[2,256,256]{2,1,0:T(8,128)(2,1)S(1)}, bf16[2,256,256]{2,1,0:T(8,128)(2,1)}, u32[]{:S(2)}) copy-start(bf16[2,256,256]{2,1,0:T(8,128)(2,1)} %constant.90.clone.refs_11_.refs_13_) | copy-start | bytes 786436
  18.5 89.7 %copy-start.1 = (f32[2,32,128]{2,1,0:T(8,128)S(1)}, f32[2,32,128]{2,1,0:T(8,128)}, u32[]{:S(2)}) copy-start(f32[2,32,128]{2,1,0:T(8,128)} %constant.89.clone.refs_10_.refs_12_) | copy-start | bytes 98308
  18.7 78.6 %collective-permute-start = (s32[12]{0:T(128)S(1)}, s32[12]{0:T(128)S(1)}, u32[]{:S(2)}, u32[]{:S(2)}) collective-permute-start(s32[12]{0:T(128)S(1)} %fusion.6.refs_0_), channel_id=1, source_target_pairs={{0,8},{8,16},{16,24},{24,0},{1,9},{9,17},{17,25},{25,1},{2,10},{10... | collective-permute-start | bytes 152 | tf_op jit(solution)/shard_map/ppermute | solution.py:355
  22.4 76.8 %collective-permute-start.1 = (s32[12]{0:T(128)S(1)}, s32[12]{0:T(128)S(1)}, u32[]{:S(2)}, u32[]{:S(2)}) collective-permute-start(s32[12]{0:T(128)S(1)} %fusion.6.refs_0_), channel_id=1, source_target_pairs={{0,16},{8,24},{16,0},{24,8},{1,17},{9,25},{17,1},{25,9},{2,18},{10... | collective-permute-start | bytes 152 | tf_op jit(solution)/shard_map/ppermute | solution.py:355
  27.2 76.1 %collective-permute-start.8 = (f32[40,128]{1,0:T(8,128)S(1)}, f32[40,128]{1,0:T(8,128)S(1)}, u32[]{:S(2)}, u32[]{:S(2)}) collective-permute-start(f32[40,128]{1,0:T(8,128)S(1)} %get-tuple-element.20), channel_id=1, source_target_pairs={{0,8},{8,16},{16,24},{24,0},{1,9},{9,17},{17,25},{25,1},{2,10},{10... | collective-permute-start | bytes 61448 | tf_op jit(solution)/shard_map/ppermute | solution.py:355
  29.4 74.6 %collective-permute-start.9 = (f32[40,128]{1,0:T(8,128)S(1)}, f32[40,128]{1,0:T(8,128)S(1)}, u32[]{:S(2)}, u32[]{:S(2)}) collective-permute-start(f32[40,128]{1,0:T(8,128)S(1)} %get-tuple-element.21), channel_id=1, source_target_pairs={{0,16},{8,24},{16,0},{24,8},{1,17},{9,25},{17,1},{25,9},{2,18},{10... | collective-permute-start | bytes 61448 | tf_op jit(solution)/shard_map/ppermute | solution.py:355
  33.1 71.6 %collective-permute-start.10 = (f32[40,128]{1,0:T(8,128)S(1)}, f32[40,128]{1,0:T(8,128)S(1)}, u32[]{:S(2)}, u32[]{:S(2)}) collective-permute-start(f32[40,128]{1,0:T(8,128)S(1)} %get-tuple-element.19), channel_id=1, source_target_pairs={{0,24},{8,0},{16,8},{24,16},{1,25},{9,1},{17,9},{25,17},{2,26},{10... | collective-permute-start | bytes 61448 | tf_op jit(solution)/shard_map/ppermute | solution.py:355
  97.3 5.4 %collective-permute-start.2 = (s32[12]{0:T(128)S(1)}, s32[12]{0:T(128)S(1)}, u32[]{:S(2)}, u32[]{:S(2)}) collective-permute-start(s32[12]{0:T(128)S(1)} %fusion.6.refs_0_), channel_id=1, source_target_pairs={{0,24},{8,0},{16,8},{24,16},{1,25},{9,1},{17,9},{25,17},{2,26},{10... | collective-permute-start | bytes 152 | tf_op jit(solution)/shard_map/ppermute | solution.py:355
  99.2 17.3 %collective-permute-start.3 = (f32[16,128]{1,0:T(8,128)S(1)}, f32[16,128]{1,0:T(8,128)S(1)}, u32[]{:S(2)}, u32[]{:S(2)}) collective-permute-start(f32[16,128]{1,0:T(8,128)S(1)} %get-tuple-element.18), channel_id=1, source_target_pairs={{24,32},{56,64},{88,96},{120,128},{152,160},{184,192},{216,224},{2... | collective-permute-start | bytes 24584 | tf_op jit(solution)/shard_map/ppermute | solution.py:393
  102.7 13.8 %collective-permute-start.4 = (f32[16,128]{1,0:T(8,128)S(1)}, f32[16,128]{1,0:T(8,128)S(1)}, u32[]{:S(2)}, u32[]{:S(2)}) collective-permute-start(f32[16,128]{1,0:T(8,128)S(1)} %get-tuple-element.12), channel_id=1, source_target_pairs={{24,40},{56,72},{88,104},{120,136},{152,168},{184,200},{216,232},{... | collective-permute-start | bytes 24584 | tf_op jit(solution)/shard_map/ppermute | solution.py:393
  103.4 13.2 %collective-permute-start.5 = (f32[16,128]{1,0:T(8,128)S(1)}, f32[16,128]{1,0:T(8,128)S(1)}, u32[]{:S(2)}, u32[]{:S(2)}) collective-permute-start(f32[16,128]{1,0:T(8,128)S(1)} %get-tuple-element.13), channel_id=1, source_target_pairs={{24,48},{56,80},{88,112},{120,144},{152,176},{184,208},{216,240},{... | collective-permute-start | bytes 24584 | tf_op jit(solution)/shard_map/ppermute | solution.py:393
  104.0 12.5 %collective-permute-start.6 = (f32[16,128]{1,0:T(8,128)S(1)}, f32[16,128]{1,0:T(8,128)S(1)}, u32[]{:S(2)}, u32[]{:S(2)}) collective-permute-start(f32[16,128]{1,0:T(8,128)S(1)} %get-tuple-element.14), channel_id=1, source_target_pairs={{24,56},{56,88},{88,120},{120,152},{152,184},{184,216},{216,248},{... | collective-permute-start | bytes 24584 | tf_op jit(solution)/shard_map/ppermute | solution.py:393
  104.7 11.8 %collective-permute-start.7 = (bf16[3,1,2,2,16,384]{5,4,3,2,1,0:T(8,128)(2,1)S(1)}, bf16[3,1,2,2,16,384]{5,4,3,2,1,0:T(8,128)(2,1)S(1)}, u32[]{:S(2)}, u32[]{:S(2)}) collective-permute-start(bf16[3,1,2,2,16,384]{5,4,3,2,1,0:T(8,128)(2,1)S(1)} %slice.24), channel_id=1, source_target_pairs={{0,32},{32,64},{64,96},{96,128},{128,160},{160,192},{192,224},{224... | collective-permute-start | bytes 442376 | tf_op jit(solution)/shard_map/ppermute | solution.py:360

commit v3 on v2

--- a/solution.py
+++ b/solution.py
@@ -25,6 +25,9 @@
 BLOCKS = SLAB // BLK
 WINDOW = 144
 ACC_ROWS = NBIN + WINDOW
+SPAN = 16
+BASE_ROW = GROUP + KEPT
+LETTER_ROWS = BASE_ROW + 8
 HALF_ROOT = math.sqrt(0.5)
 
 
@@ -106,50 +109,52 @@
 def frame_profile(
     row_of, weight_of, base_of, marks_of, chirp_ref, twist_ref, table_ref, mid, y_refs, v_refs, stokes_ref, acc
 ):
-    for pol in range(2):
-        y_ref, v_ref = y_refs.at[pol], v_refs.at[pol]
-        for b in range(4):
-            rows = []
-            for a in range(8):
-                row = 4 * a + b
-                gain = weight_of(row // 2)
-                rows.append(tuple(row_of(row, pol, part).astype(jnp.float32) * gain for part in range(2)))
-            for ka, value in enumerate(dft8(rows, -1)):
-                value = turned(value, b * ka, -1)
-                mid[pol, 0, b, ka] = value[0]
-                mid[pol, 1, b, ka] = value[1]
-        for ka in range(8):
-            values = dft4([(mid[pol, 0, b, ka], mid[pol, 1, b, ka]) for b in range(4)], -1)
-            for kb in range(4):
-                k = ka + 8 * kb
-                re, im = values[kb]
-                if k:
-                    cos, sin = twist_ref[0, k : k + 1], twist_ref[1, k : k + 1]
-                    re, im = re * cos - im * sin, re * sin + im * cos
-                for part, value in enumerate((re, im)):
-                    high, low = split(value)
-                    where = (pl.ds(GROUP * k, GROUP), pl.ds(LANES * part, LANES))
-                    y_ref[0, *where] = high
-                    y_ref[1, *where] = low
-        for m in range(2):
-            rows = pl.ds(16 * GROUP * m, 16 * GROUP)
-            spectrum = lane_dft(y_ref[0, rows], y_ref[1, rows], table_ref[0], table_ref[1])
-            re, im = spectrum[:, :LANES], spectrum[:, LANES:]
-            cos, sin = chirp_ref[0, rows], chirp_ref[1, rows]
-            swapped = jnp.concatenate([re * sin + im * cos, re * cos - im * sin], axis=1)
-            back = lane_dft(*split(swapped), table_ref[0], table_ref[1])
-            im, re = (back[:, part].reshape(16, GROUP, LANES) for part in (slice(0, LANES), slice(LANES, None)))
-            cos = twist_ref[0, 16 * m : 16 * m + 16][:, None, :]
-            sin = twist_ref[1, 16 * m : 16 * m + 16][:, None, :]
-            v_ref[0, 16 * m : 16 * m + 16] = re * cos + im * sin
-            v_ref[1, 16 * m : 16 * m + 16] = im * cos - re * sin
-        for b in range(4):
-            values = dft8([(v_ref[0, 4 * a + b], v_ref[1, 4 * a + b]) for a in range(8)], 1)
-            for na, value in enumerate(values):
-                value = turned(value, b * na, 1)
-                mid[pol, 0, b, na] = value[0]
-                mid[pol, 1, b, na] = value[1]
-    for na in range(8):
+    def rows_in(pol, b):
+        rows = []
+        for a in range(8):
+            row = 4 * a + b
+            gain = weight_of(row // 2)
+            rows.append(tuple(row_of(row, pol, part).astype(jnp.float32) * gain for part in range(2)))
+        for ka, value in enumerate(dft8(rows, -1)):
+            value = turned(value, b * ka, -1)
+            mid[pol, 0, b, ka] = value[0]
+            mid[pol, 1, b, ka] = value[1]
+
+    def rows_across(pol, ka):
+        values = dft4([(mid[pol, 0, b, ka], mid[pol, 1, b, ka]) for b in range(4)], -1)
+        for kb in range(4):
+            k = ka + 8 * kb
+            re, im = values[kb]
+            if k:
+                cos, sin = twist_ref[0, k : k + 1], twist_ref[1, k : k + 1]
+                re, im = re * cos - im * sin, re * sin + im * cos
+            for part, value in enumerate((re, im)):
+                high, low = split(value)
+                where = (pl.ds(GROUP * k, GROUP), pl.ds(LANES * part, LANES))
+                y_refs[pol, 0, *where] = high
+                y_refs[pol, 1, *where] = low
+
+    def lanes_there_and_back(pol, m):
+        rows = pl.ds(SPAN * GROUP * m, SPAN * GROUP)
+        spectrum = lane_dft(y_refs[pol, 0, rows], y_refs[pol, 1, rows], table_ref[0], table_ref[1])
+        re, im = spectrum[:, :LANES], spectrum[:, LANES:]
+        cos, sin = chirp_ref[0, rows], chirp_ref[1, rows]
+        swapped = jnp.concatenate([re * sin + im * cos, re * cos - im * sin], axis=1)
+        back = lane_dft(*split(swapped), table_ref[0], table_ref[1])
+        im, re = (back[:, part].reshape(SPAN, GROUP, LANES) for part in (slice(0, LANES), slice(LANES, None)))
+        cos = twist_ref[0, SPAN * m : SPAN * (m + 1)][:, None, :]
+        sin = twist_ref[1, SPAN * m : SPAN * (m + 1)][:, None, :]
+        v_refs[pol, 0, SPAN * m : SPAN * (m + 1)] = re * cos + im * sin
+        v_refs[pol, 1, SPAN * m : SPAN * (m + 1)] = im * cos - re * sin
+
+    def rows_back(pol, b):
+        values = dft8([(v_refs[pol, 0, 4 * a + b], v_refs[pol, 1, 4 * a + b]) for a in range(8)], 1)
+        for na, value in enumerate(values):
+            value = turned(value, b * na, 1)
+            mid[pol, 0, b, na] = value[0]
+            mid[pol, 1, b, na] = value[1]
+
+    def rows_out(na):
         x, y = (
             dft4([(mid[pol, 0, b, na], mid[pol, 1, b, na]) for b in range(4)], 1) for pol in range(2)
         )
@@ -163,8 +168,10 @@
             lanes = pl.ds(LANES * (row % 2), LANES)
             for s, value in enumerate((power_x + power_y, power_x - power_y, 2.0 * cross_re, 2.0 * cross_im)):
                 stokes_ref[row // 2, pl.ds(GROUP * s, GROUP), lanes] = value.astype(jnp.bfloat16)
+
     bins = lax.broadcasted_iota(jnp.int32, (WINDOW, BLK), 0)
-    for m in range(BLOCKS):
+
+    def fold(m):
         onehot = jnp.where(bins == marks_of(m), 1.0, 0.0).astype(jnp.bfloat16)
         part = lax.dot_general(
             onehot, stokes_ref[m], (((1,), (1,)), ((), ())), preferred_element_type=jnp.float32
@@ -172,20 +179,32 @@
         place = pl.ds(pl.multiple_of(base_of(m), 8), WINDOW)
         acc[place] += part
 
+    spans = ROWS // SPAN
+    for b in range(4):
+        rows_in(0, b)
+    for ka in range(8):
+        rows_across(0, ka)
+    for m in range(spans):
+        lanes_there_and_back(0, m)
+        for b in range(4 * m // spans, 4 * (m + 1) // spans):
+            rows_in(1, b)
+    for ka in range(8):
+        rows_across(1, ka)
+    for m in range(spans):
+        lanes_there_and_back(1, m)
+        for b in range(4 * m // spans, 4 * (m + 1) // spans):
+            rows_back(0, b)
+    for b in range(4):
+        rows_back(1, b)
+    for na in range(8):
+        rows_out(na)
+        if na % 2:
+            for m in range(na // 2, BLOCKS, 4):
+                fold(m)
+
 
 def own_row(buf_ref, slab, row, pol, part):
     return buf_ref[row // 3, slab, pol, part, :, pl.ds(LANES * (row % 3), LANES)]
-
-
-def turn_of(me, slab):
-    return (me - slab + RUNS) % RUNS
-
-
-def base_from(base_refs, turn, m):
-    value = base_refs[RUNS - 1][m]
-    for other in range(RUNS - 1):
-        value = jnp.where(turn == other, base_refs[other][m], value)
-    return value
 
 
 def lay_gains(gains, weights_of):
@@ -198,13 +217,12 @@
 
 
 def later_kernel(me_ref, *refs):
-    base_refs, refs = refs[:RUNS], refs[RUNS:]
     letter_refs, refs = refs[:RUNS], refs[RUNS:]
     buf_ref, chirp_ref, twist_ref, table_ref, acc_ref, sorted_ref, gains, marks, *scratches = refs
     me = me_ref[0]
     for turn in range(RUNS):
         sorted_ref[(me - turn + RUNS) % RUNS] = letter_refs[turn][...]
-    marks[...] = sorted_ref[:, GROUP:].astype(jnp.int32)
+    marks[...] = sorted_ref[:, GROUP : GROUP + KEPT].astype(jnp.int32)
     acc_ref[...] = jnp.zeros_like(acc_ref)
 
     def step(frame, carry):
@@ -221,11 +239,11 @@
             return own[:, block - RIM // 2 : block - RIM // 2 + 1]
 
         lay_gains(gains, weights_of)
-        turn = turn_of(me, frame)
+        bases = sorted_ref[frame, BASE_ROW : BASE_ROW + 1].astype(jnp.int32)
         frame_profile(
             row_of,
             lambda block: gains[block],
-            lambda m: base_from(base_refs, turn, m),
+            lambda m: bases[0, m],
             lambda m: marks_from(marks, frame, m),
             chirp_ref,
             twist_ref,
@@ -238,14 +256,14 @@
     lax.fori_loop(1, RUNS, step, 0)
 
 
-def first_kernel(me_ref, *refs):
-    base_refs, refs = refs[:RUNS], refs[RUNS:]
-    rim_refs, refs = refs[:RUNS], refs[RUNS:]
-    buf_ref, tail_ref, sorted_ref, chirp_ref, twist_ref, table_ref, given_ref, out_ref, acc, gains, marks, *scratches = refs
+def first_kernel(
+    buf_ref, tail_ref, sorted_ref, chirp_ref, twist_ref, table_ref, given_ref, out_ref, acc, gains, marks, *scratches
+):
     acc[...] = given_ref[...]
-    before = (rim_refs[0][...] + rim_refs[1][...]) + (rim_refs[2][...] + rim_refs[3][...])
+    high, middle, low = (tail_ref[0, 0, part // 2, part % 2, :, :LANES].astype(jnp.float32) for part in range(3))
+    before = (high + middle) + low
     own = sorted_ref[0, :GROUP]
-    marks[0] = sorted_ref[0, GROUP:].astype(jnp.int32)
+    marks[0] = sorted_ref[0, GROUP : GROUP + KEPT].astype(jnp.int32)
 
     def weights_of(block):
         if block < RIM // 2:
@@ -258,11 +276,11 @@
         return own_row(buf_ref, 0, row - RIM, pol, part)
 
     lay_gains(gains, weights_of)
-    turn = turn_of(me_ref[0], 0)
+    bases = sorted_ref[0, BASE_ROW : BASE_ROW + 1].astype(jnp.int32)
     frame_profile(
         row_of,
         lambda block: gains[block],
-        lambda m: base_from(base_refs, turn, m),
+        lambda m: bases[0, m],
         lambda m: marks_from(marks, 0, m),
         chirp_ref,
         twist_ref,
@@ -275,6 +293,32 @@
         out_ref[share] = jnp.concatenate([acc[16 * share : 16 * share + 8], acc[16 * share + 8 : 16 * share + 16]], axis=1)
 
 
+def tail_kernel(me_ref, *refs):
+    letter_refs, piece_refs, out_ref, sorted_ref = refs[:RUNS], refs[RUNS:-2], refs[-2], refs[-1]
+    me = me_ref[0]
+    for turn in range(RUNS):
+        sorted_ref[(me - turn + RUNS) % RUNS] = letter_refs[turn][:GROUP]
+    rest = sorted_ref[RUNS - 1]
+    for index, piece in enumerate(piece_refs):
+        out_ref[index] = piece[0]
+    for part in range(3):
+        rounded = rest.astype(jnp.bfloat16)
+        out_ref[0, 0, part // 2, part % 2, :, :LANES] = rounded
+        rest = rest - rounded.astype(jnp.float32)
+
+
+def spread_kernel(samples_ref, out_ref, sems):
+    copies = [
+        pltpu.make_async_copy(samples_ref.at[pol, part], out_ref.at[:, pol, part], sems.at[pol, part])
+        for pol in range(2)
+        for part in range(2)
+    ]
+    for copy in copies:
+        copy.start()
+    for copy in copies:
+        copy.wait()
+
+
 def scratch():
     return [
         pltpu.VMEM((2, 2, 4, 8, GROUP, LANES), jnp.float32),
@@ -292,20 +336,35 @@
     return pl.BlockSpec(memory_space=pltpu.SMEM)
 
 
-def fold_frames(buf, tail_of, me, bases, letters, rims, chirp):
+def tail_message(me, letters, buf):
+    block = (1, 1) + buf.shape[2:]
+    first = MEMBERS - 3
+    return pl.pallas_call(
+        tail_kernel,
+        out_shape=jax.ShapeDtypeStruct((3, 1) + buf.shape[2:], buf.dtype),
+        grid=(1,),
+        in_specs=[smem()]
+        + [whole()] * RUNS
+        + [pl.BlockSpec(block, lambda i, at=first + at: (at, RUNS - 1, 0, 0, 0, 0)) for at in range(3)],
+        out_specs=whole(),
+        scratch_shapes=[pltpu.VMEM((RUNS, GROUP, LANES), jnp.float32)],
+        name="tail_message",
+    )(me, *letters, buf, buf, buf)
+
+
+def fold_frames(buf, tail_of, me, letters, chirp):
     twist = jnp.asarray(np.stack(twist_tables()))
     table = jnp.asarray(np.stack(lane_tables()))
-    tail = tail_of(buf)
+    tail = tail_of(tail_message(me, letters, buf))
     params = pltpu.CompilerParams(vmem_limit_bytes=28 * 1024 * 1024)
     flops = 2 * 2 * 2 * 3 * ROWS * GROUP * 256 * 256
-    letter_rows = GROUP + KEPT
     later, ordered = pl.pallas_call(
         later_kernel,
         out_shape=[
             jax.ShapeDtypeStruct((ACC_ROWS, 4 * GROUP), jnp.float32),
-            jax.ShapeDtypeStruct((RUNS, letter_rows, LANES), jnp.float32),
+            jax.ShapeDtypeStruct((RUNS, LETTER_ROWS, LANES), jnp.float32),
         ],
-        in_specs=[smem()] * (1 + RUNS) + [whole()] * (RUNS + 4),
+        in_specs=[smem()] + [whole()] * (RUNS + 4),
         out_specs=[whole()] * 2,
         scratch_shapes=[
             pltpu.VMEM((ROWS // 2, GROUP, LANES), jnp.float32),
@@ -315,16 +374,13 @@
         compiler_params=params,
         cost_estimate=pl.CostEstimate(flops=3 * flops, bytes_accessed=30_000_000, transcendentals=0),
         name="later_frames",
-    )(me, *bases, *letters, buf, chirp, twist, table)
+    )(me, *letters, buf, chirp, twist, table)
     block = (MEMBERS, 1) + buf.shape[2:]
     return pl.pallas_call(
         first_kernel,
         out_shape=jax.ShapeDtypeStruct((NBIN // 16, 8, LANES), jnp.float32),
         grid=(1,),
-        in_specs=[smem()] * (1 + RUNS)
-        + [whole()] * RUNS
-        + [pl.BlockSpec(block, lambda i: (0,) * 6)]
-        + [whole()] * 6,
+        in_specs=[pl.BlockSpec(block, lambda i: (0,) * 6)] + [whole()] * 6,
         out_specs=whole(),
         scratch_shapes=[
             pltpu.VMEM((ACC_ROWS, 4 * GROUP), jnp.float32),
@@ -335,16 +391,15 @@
         compiler_params=params,
         cost_estimate=pl.CostEstimate(flops=flops, bytes_accessed=10_000_000, transcendentals=0),
         name="first_frame",
-    )(me, *bases, *rims, buf, tail, ordered, chirp, twist, table, later)
+    )(buf, tail, ordered, chirp, twist, table, later)
 
 
 def last_kernel(scale, shares_ref, out_ref):
-    for slab in range(RUNS):
-        total = jnp.sum(shares_ref[:, slab], axis=0) * scale
-        for half in range(2):
-            for s in range(4):
-                lanes = slice(64 * half + GROUP * s, 64 * half + GROUP * (s + 1))
-                out_ref[8 * half : 8 * half + 8, s, GROUP * slab : GROUP * (slab + 1)] = total[:, lanes]
+    total = [jnp.sum(shares_ref[:, slab], axis=0) * scale for slab in range(RUNS)]
+    for half in range(2):
+        for s in range(4):
+            lanes = slice(64 * half + GROUP * s, 64 * half + GROUP * (s + 1))
+            out_ref[pl.ds(32 * half + s, 8, stride=4)] = jnp.concatenate([part[:, lanes] for part in total], axis=1)
 
 
 def turned_to(block_for, axis, turn):
@@ -369,7 +424,14 @@
 
 
 def on_device(samples, scales, flags, sweep, phase_bin):
-    parts = samples.reshape(2, 2, MEMBERS * RUNS, GROUP, PIECE).transpose(2, 0, 1, 3, 4)
+    parts = pl.pallas_call(
+        spread_kernel,
+        out_shape=jax.ShapeDtypeStruct((MEMBERS * RUNS, 2, 2, GROUP, PIECE), samples.dtype),
+        in_specs=[pl.BlockSpec(memory_space=pl.ANY)],
+        out_specs=pl.BlockSpec(memory_space=pl.ANY),
+        scratch_shapes=[pltpu.SemaphoreType.DMA((2, 2))],
+        name="spread",
+    )(samples.reshape(2, 2, MEMBERS * RUNS, GROUP, PIECE))
     buf = lax.all_to_all(parts, ("chan", "zl"), split_axis=0, concat_axis=0, tiled=True)
     buf = buf.reshape(MEMBERS, RUNS, 2, 2, GROUP, PIECE)
 
@@ -383,31 +445,21 @@
     def weights_for(place):
         return lax.dynamic_slice_in_dim(weight, place * GROUP, GROUP, 0)
 
-    def letter_for(place):
-        return jnp.concatenate([weights_for(place), marks.astype(jnp.float32)])
-
-    letters = [turned_to(letter_for, "zl", turn) for turn in range(RUNS)]
-    bases = [turned_to(lambda place: base, "zl", turn) for turn in range(RUNS)]
-    size = lax.axis_size("xy")
-    rims = [
-        lax.ppermute(
-            weight[GROUP * place : GROUP * (place + 1)],
-            ("xy", "zl"),
-            [(i * RUNS + RUNS - 1, (i + 1) * RUNS + place) for i in range(size - 1)],
-        )
-        for place in range(RUNS)
+    base_rows = jnp.pad(base[None, :], ((0, LETTER_ROWS - BASE_ROW - 1), (0, LANES - BLOCKS)))
+    below = jnp.concatenate([marks, base_rows]).astype(jnp.float32)
+    letters = [
+        turned_to(lambda place: jnp.concatenate([weights_for(place), below]), "zl", turn) for turn in range(RUNS)
     ]
     chirp = chirp_table(lax.dynamic_slice_in_dim(sweep, me * GROUP, GROUP, 0))
 
-    partial = fold_frames(
-        buf, lambda b: from_before(b[5:, RUNS - 1 :]), me.reshape(1), bases, letters, rims, chirp
-    )
+    partial = fold_frames(buf, from_before, me.reshape(1), letters, chirp)
     shares = lax.all_to_all(partial, ("xy", "zl"), split_axis=0, concat_axis=0, tiled=True)
+    size = lax.axis_size("xy")
     return pl.pallas_call(
         functools.partial(last_kernel, NBIN / (SLAB * RUNS * size)),
-        out_shape=jax.ShapeDtypeStruct((16, 4, RUNS * GROUP), jnp.float32),
+        out_shape=jax.ShapeDtypeStruct((16 * 4, RUNS * GROUP), jnp.float32),
         name="last_sum",
-    )(shares.reshape(-1, RUNS, 8, LANES))
+    )(shares.reshape(size, RUNS, 8, LANES)).reshape(16, 4, RUNS * GROUP)
 
 
 def solution(mesh):

time: 149 us -> 185 us (1.24)
  Pallas kernels: 13.4 us -> 62.6 us
  starting transfers between devices: 41.8 us -> 30.4 us
  blocking collectives: 26.3 us -> 19.5 us
  waiting for transfers between devices: 61.2 us -> 64.6 us
  local copies, waits for them, and re-layouts: 3.39 us -> 5.3 us
    ppermute x6 -> x3, waiting for transfers between devices: 2.21 us -> 56.7 us  [turned_to(): lax.ppermute(block_for(there), axis, [(i, (i + turn) % size) for i in ran...]
    all_to_all x1, waiting for transfers between devices: 58.9 us -> 7.93 us  [on_device(): lax.all_to_all(parts, ('chan', 'zl'), split_axis=0, concat_axis=0, tiled=...]
    pallas_call x0 -> x2, Pallas kernels: none -> 50.4 us  [the longest x1 48.8 us: on_device(): pl.pallas_call(spread_kernel, out_shape=jax.ShapeDtypeStruct((MEMBERS * R...]
    ppermute x6 -> x3, starting transfers between devices: 19.4 us -> 11.3 us  [turned_to(): lax.ppermute(block_for(there), axis, [(i, (i + turn) % size) for i in ran...]
    all_to_all x1, blocking collectives: 26.3 us -> 19.5 us  [on_device(): lax.all_to_all(partial, ('xy', 'zl'), split_axis=0, concat_axis=0, tiled=...]
    unnamed x14 -> x34, local copies, waits for them, and re-layouts: 0.22 us -> 5 us
    ppermute x4 -> x0, starting transfers between devices: 3.27 us -> none  [on_device(): lax.ppermute(weight[GROUP * place:GROUP * (place + 1)], ('xy', 'zl'), [(i...]
    reshape x1 -> x0, local copies, waits for them, and re-layouts: 2.87 us -> none  [on_device(): samples.reshape(2, 2, MEMBERS * RUNS, GROUP, PIECE).transpose(2, 0, 1, 3, 4)]
  transfers between devices with their start and end apart: 12 -> 5, of which waited for: 2 -> 3; matrix products, arithmetic and copies ran while one was open for 1% -> 1% of each run, Pallas kernels for 6% -> 4%
where the time goes in v3:
time: 185 us
  waiting for transfers between devices  64.6 us (35%)
  Pallas kernels  62.6 us (34%)
  starting transfers between devices  30.4 us (16%)
  blocking collectives  19.5 us (11%)
  local copies, waits for them, and re-layouts  5.3 us (3%)
  other arithmetic  2.17 us (1%)
    ppermute x3, waiting for transfers between devices, turned_to(): lax.ppermute(block_for(there), axis, [(i, (i + turn) % size) for i in ran...  56.7 us
    pallas_call x1, Pallas kernels, on_device(): pl.pallas_call(spread_kernel, out_shape=jax.ShapeDtypeStruct((MEMBERS * R...  48.8 us
    all_to_all x1, blocking collectives, on_device(): lax.all_to_all(partial, ('xy', 'zl'), split_axis=0, concat_axis=0, tiled=...  19.5 us
    all_to_all x1, starting transfers between devices, on_device(): lax.all_to_all(parts, ('chan', 'zl'), split_axis=0, concat_axis=0, tiled=...  15.6 us
    ppermute x3, starting transfers between devices, turned_to(): lax.ppermute(block_for(there), axis, [(i, (i + turn) % size) for i in ran...  11.3 us
    all_to_all x1, waiting for transfers between devices, on_device(): lax.all_to_all(parts, ('chan', 'zl'), split_axis=0, concat_axis=0, tiled=...  7.93 us
    pallas_call x1, Pallas kernels, fold_frames(): pl.pallas_call(later_kernel, out_shape=[jax.ShapeDtypeStruct((ACC_ROWS, 4...  7.78 us
    unnamed x34, local copies, waits for them, and re-layouts  5 us
  transfers between devices with their start and end apart: 5, of which 3 were waited for; matrix products, arithmetic and copies ran while one was open for 1% of the time, Pallas kernels for 4%

profile of v3, /device:TPU:8, one launch (start us, length us, event | category | flops | bytes accessed | tf_op | source)
XLA Modules:
  0.0 184.9 jit_solution(9741754256162465221)
XLA Ops:
  0.0 48.8 %spread.1 = bf16[32,2,2,16,384]{4,3,2,1,0:T(8,128)(2,1)} custom-call(bf16[2,2,32,16,384]{4,3,2,1,0:T(8,128)(2,1)} %bitcast.29), custom_call_target="tpu_custom_call" | custom-call | tf_op jit(solution)/shard_map/spread/pallas_call | solution.py:427
  48.8 0.0 copy-start.12
  48.8 0.0 copy-start.13
  48.8 0.0 copy-start.14
  48.8 0.0 copy-start.15
  48.8 15.6 %all-to-all-start = ((bf16[32,2,2,16,384]{4,3,2,1,0:T(8,128)(2,1)}), bf16[32,2,2,16,384]{4,3,2,1,0:T(8,128)(2,1)S(1)}, u32[]{:S(2)}, u32[]{:S(2)}) async-start(bf16[32,2,2,16,384]{4,3,2,1,0:T(8,128)(2,1)} %spread.1), calls=%async_computation | async-start | bytes 3145728 | tf_op jit(solution)/shard_map/all_to_all | solution.py:435
  64.5 0.0 copy-done.12
  64.5 0.1 reduce
  64.7 0.1 broadcast_in_dim.2
  64.8 0.1 sub.29
  64.8 0.0 copy-done.13
  64.9 0.1 copy.14
  64.9 0.0 copy-done.14
  64.9 0.1 copy.13
  65.1 0.1 add_select_fusion
  65.2 0.6 pad_maximum_fusion
  65.8 3.7 %collective-permute-start = (f32[48,128]{1,0:T(8,128)S(1)}, f32[48,128]{1,0:T(8,128)S(1)}, u32[]{:S(2)}, u32[]{:S(2)}) collective-permute-start(f32[48,128]{1,0:T(8,128)S(1)} %get-tuple-element.16), channel_id=1, source_target_pairs={{0,8},{8,16},{16,24},{24,0},{1,9},{9,17},{17,25},{25,1},{2,10},{10... | collective-permute-start | bytes 73736 | tf_op jit(solution)/shard_map/ppermute | solution.py:410
  69.5 4.3 %collective-permute-start.1 = (f32[48,128]{1,0:T(8,128)S(1)}, f32[48,128]{1,0:T(8,128)S(1)}, u32[]{:S(2)}, u32[]{:S(2)}) collective-permute-start(f32[48,128]{1,0:T(8,128)S(1)} %get-tuple-element.17), channel_id=1, source_target_pairs={{0,16},{8,24},{16,0},{24,8},{1,17},{9,25},{17,1},{25,9},{2,18},{10... | collective-permute-start | bytes 73736 | tf_op jit(solution)/shard_map/ppermute | solution.py:410
  73.8 3.4 %collective-permute-start.2 = (f32[48,128]{1,0:T(8,128)S(1)}, f32[48,128]{1,0:T(8,128)S(1)}, u32[]{:S(2)}, u32[]{:S(2)}) collective-permute-start(f32[48,128]{1,0:T(8,128)S(1)} %get-tuple-element.15), channel_id=1, source_target_pairs={{0,24},{8,0},{16,8},{24,16},{1,25},{9,1},{17,9},{25,17},{2,26},{10... | collective-permute-start | bytes 73736 | tf_op jit(solution)/shard_map/ppermute | solution.py:410
  77.2 0.0 copy-done.15
  77.2 0.1 dynamic-slice_multiply_fusion
  77.3 0.1 mul.100
  77.4 1.2 fusion.1
  78.6 55.9 %collective-permute-done.refs_1_ = f32[48,128]{1,0:T(8,128)S(1)} collective-permute-done((f32[48,128]{1,0:T(8,128)S(1)}, f32[48,128]{1,0:T(8,128)S(1)}, u32[]{:S(2)}, u32[]{:S(2)}) %collective-permute-start) | collective-permute-done | bytes 24608 | tf_op jit(solution)/shard_map/ppermute | solution.py:410
  134.5 0.0 copy-start.6
  134.6 0.0 collective-permute-done.1.refs_2_
  134.6 0.0 copy-start.8
  134.6 0.7 collective-permute-done.2.refs_3_
  135.3 0.0 copy-start.10
  135.3 7.9 %all-to-all-done = bf16[32,2,2,16,384]{4,3,2,1,0:T(8,128)(2,1)S(1)} async-done(((bf16[32,2,2,16,384]{4,3,2,1,0:T(8,128)(2,1)}), bf16[32,2,2,16,384]{4,3,2,1,0:T(8,128)(2,1)S(1)}, u32[]{:S(2)}, u32[]{:S(2)}) %all-to-all-start) | async-done | bytes 1572896 | tf_op jit(solution)/shard_map/all_to_all | solution.py:435
  143.2 0.0 copy-start
  143.2 0.0 copy-done.6
  143.2 0.0 copy-done.8
  143.2 0.0 copy-done.10
  143.2 1.1 copy-done
  144.4 0.0 copy-start.3
  144.4 0.0 copy-start.4
  144.4 0.0 copy-start.5
  144.4 1.6 tail_message.1
  146.0 3.5 %collective-permute-start.3 = (bf16[3,1,2,2,16,384]{5,4,3,2,1,0:T(8,128)(2,1)}, bf16[3,1,2,2,16,384]{5,4,3,2,1,0:T(8,128)(2,1)S(1)}, u32[]{:S(2)}, u32[]{:S(2)}) collective-permute-start(bf16[3,1,2,2,16,384]{5,4,3,2,1,0:T(8,128)(2,1)} %tail_message.1), channel_id=1, source_target_pairs={{0,32},{32,64},{64,96},{96,128},{128,160},{160,192},{192,224},{224... | collective-permute-start | bytes 442376 | tf_op jit(solution)/shard_map/ppermute | solution.py:415
  149.5 0.0 copy-done.3
  149.5 0.0 copy-done.4
  149.5 0.0 copy-done.5
  149.5 0.0 copy-start.1
  149.5 1.4 copy-done.1
  150.9 0.0 copy-start.7
  150.9 0.7 copy-done.7
  151.7 0.0 copy-start.9
  151.7 0.7 copy-done.9
  152.4 0.0 copy-start.11
  152.4 0.7 copy-done.11
  153.2 0.0 copy-start.2
  153.2 7.8 %later_frames.1 = (f32[1168,64]{1,0:T(8,128)S(1)}, f32[4,48,128]{2,1,0:T(8,128)S(1)}) custom-call(s32[1]{0:T(128)} %bitcast.2.me_ref, f32[48,128]{1,0:T(8,128)S(1)} %copy-done.4, f32[48,128]{1,0:T(8,128)S(1)} %copy-done.7, f32[48,128]{1,0:T(8,128)S(1)} %copy-done.9, f32[48,128]{1,0:T(8,128)S(1)} %copy-done.11, bf16[8,4,2,2,16,384]{5,4,3,2,1,0:T(8,128)(2,1)S(1)} %bitcast.27, ...), custom_call_target="tpu_custom_call" | custom-call | flops 2415919104 | bytes 30000000 | tf_op jit(solution)/shard_map/later_frames/pallas_call | solution.py:361
  160.9 0.0 collective-permute-done.3.tail_ref
  161.0 0.0 copy-done.2
  161.0 2.8 %first_frame.1 = f32[64,8,128]{2,1,0:T(8,128)S(1)} custom-call(bf16[8,4,2,2,16,384]{5,4,3,2,1,0:T(8,128)(2,1)S(1)} %bitcast.28, bf16[3,1,2,2,16,384]{5,4,3,2,1,0:T(8,128)(2,1)S(1)} %collective-permute-done.3.tail_ref, f32[4,48,128]{2,1,0:T(8,128)S(1)} %get-tuple-element.7.sorted_ref, f32[2,512,128]{2,1,0:T(8,128)S(1)} %maximum_multiply_fusion.refs_5_.chirp_ref, ...), custom_call_target="tpu_custom_call" | custom-call | flops 805306368 | bytes 10000000 | tf_op jit(solution)/shard_map/first_frame/pallas_call | solution.py:379
  163.7 19.5 %all_to_all.10 = f32[64,8,128]{2,1,0:T(8,128)} all-to-all(f32[64,8,128]{2,1,0:T(8,128)S(1)} %first_frame.1), channel_id=1, replica_groups=mesh['xy'=16,'zl'=4,'chan'=8] {'xy','zl'}, dimensions={0} | all-to-all | bytes 524288 | tf_op jit(solution)/shard_map/all_to_all | solution.py:456
  183.2 1.7 last_sum.1
  (11 shorter events, 0.2 us)
Async XLA Ops:
  48.8 15.7 %copy-start.12 = (s32[3072]{0:T(1024)S(1)}, s32[3072]{0:T(1024)}, u32[]{:S(2)}) copy-start(s32[3072]{0:T(1024)} %param.11) | copy-start | bytes 36868
  48.8 16.0 %copy-start.13 = (f32[64,12]{0,1:T(8,128)S(1)}, f32[64,12]{0,1:T(8,128)}, u32[]{:S(2)}) copy-start(f32[64,12]{0,1:T(8,128)} %param.8) | copy-start | bytes 9220
  48.8 16.1 %copy-start.14 = (s32[64,12]{0,1:T(8,128)S(1)}, s32[64,12]{0,1:T(8,128)}, u32[]{:S(2)}) copy-start(s32[64,12]{0,1:T(8,128)} %param.9) | copy-start | bytes 9220
  48.8 28.3 %copy-start.15 = (f32[64]{0:T(128)S(1)}, f32[64]{0:T(128)}, u32[]{:S(2)}) copy-start(f32[64]{0:T(128)} %param.10) | copy-start | bytes 772
  48.8 94.4 %all-to-all-start = ((bf16[32,2,2,16,384]{4,3,2,1,0:T(8,128)(2,1)}), bf16[32,2,2,16,384]{4,3,2,1,0:T(8,128)(2,1)S(1)}, u32[]{:S(2)}, u32[]{:S(2)}) async-start(bf16[32,2,2,16,384]{4,3,2,1,0:T(8,128)(2,1)} %spread.1), calls=%async_computation | async-start | bytes 3145728 | tf_op jit(solution)/shard_map/all_to_all | solution.py:435
  65.8 68.7 %collective-permute-start = (f32[48,128]{1,0:T(8,128)S(1)}, f32[48,128]{1,0:T(8,128)S(1)}, u32[]{:S(2)}, u32[]{:S(2)}) collective-permute-start(f32[48,128]{1,0:T(8,128)S(1)} %get-tuple-element.16), channel_id=1, source_target_pairs={{0,8},{8,16},{16,24},{24,0},{1,9},{9,17},{17,25},{25,1},{2,10},{10... | collective-permute-start | bytes 73736 | tf_op jit(solution)/shard_map/ppermute | solution.py:410
  69.5 65.1 %collective-permute-start.1 = (f32[48,128]{1,0:T(8,128)S(1)}, f32[48,128]{1,0:T(8,128)S(1)}, u32[]{:S(2)}, u32[]{:S(2)}) collective-permute-start(f32[48,128]{1,0:T(8,128)S(1)} %get-tuple-element.17), channel_id=1, source_target_pairs={{0,16},{8,24},{16,0},{24,8},{1,17},{9,25},{17,1},{25,9},{2,18},{10... | collective-permute-start | bytes 73736 | tf_op jit(solution)/shard_map/ppermute | solution.py:410
  73.8 61.5 %collective-permute-start.2 = (f32[48,128]{1,0:T(8,128)S(1)}, f32[48,128]{1,0:T(8,128)S(1)}, u32[]{:S(2)}, u32[]{:S(2)}) collective-permute-start(f32[48,128]{1,0:T(8,128)S(1)} %get-tuple-element.15), channel_id=1, source_target_pairs={{0,24},{8,0},{16,8},{24,16},{1,25},{9,1},{17,9},{25,17},{2,26},{10... | collective-permute-start | bytes 73736 | tf_op jit(solution)/shard_map/ppermute | solution.py:410
  134.5 8.7 %copy-start.6 = (f32[48,128]{1,0:T(8,128)}, f32[48,128]{1,0:T(8,128)S(1)}, u32[]{:S(2)}) copy-start(f32[48,128]{1,0:T(8,128)S(1)} %collective-permute-done.refs_1_) | copy-start | bytes 73732
  134.6 8.7 %copy-start.8 = (f32[48,128]{1,0:T(8,128)}, f32[48,128]{1,0:T(8,128)S(1)}, u32[]{:S(2)}) copy-start(f32[48,128]{1,0:T(8,128)S(1)} %collective-permute-done.1.refs_2_) | copy-start | bytes 73732
  135.3 7.9 %copy-start.10 = (f32[48,128]{1,0:T(8,128)}, f32[48,128]{1,0:T(8,128)S(1)}, u32[]{:S(2)}) copy-start(f32[48,128]{1,0:T(8,128)S(1)} %collective-permute-done.2.refs_3_) | copy-start | bytes 73732
  143.2 1.2 copy-start
  144.4 5.1 %copy-start.3 = (bf16[2,256,256]{2,1,0:T(8,128)(2,1)S(1)}, bf16[2,256,256]{2,1,0:T(8,128)(2,1)}, u32[]{:S(2)}) copy-start(bf16[2,256,256]{2,1,0:T(8,128)(2,1)} %constant.90.clone.refs_7_.table_ref) | copy-start | bytes 786436
  144.4 5.1 %copy-start.4 = (f32[48,128]{1,0:T(8,128)S(1)}, f32[48,128]{1,0:T(8,128)}, u32[]{:S(2)}) copy-start(f32[48,128]{1,0:T(8,128)} %get-tuple-element.18.refs_0_) | copy-start | bytes 73732
  144.4 5.1 %copy-start.5 = (f32[2,32,128]{2,1,0:T(8,128)S(1)}, f32[2,32,128]{2,1,0:T(8,128)}, u32[]{:S(2)}) copy-start(f32[2,32,128]{2,1,0:T(8,128)} %constant.89.clone.refs_6_.twist_ref) | copy-start | bytes 98308
  146.0 14.9 %collective-permute-start.3 = (bf16[3,1,2,2,16,384]{5,4,3,2,1,0:T(8,128)(2,1)}, bf16[3,1,2,2,16,384]{5,4,3,2,1,0:T(8,128)(2,1)S(1)}, u32[]{:S(2)}, u32[]{:S(2)}) collective-permute-start(bf16[3,1,2,2,16,384]{5,4,3,2,1,0:T(8,128)(2,1)} %tail_message.1), channel_id=1, source_target_pairs={{0,32},{32,64},{64,96},{96,128},{128,160},{160,192},{192,224},{224... | collective-permute-start | bytes 442376 | tf_op jit(solution)/shard_map/ppermute | solution.py:415
  149.5 1.4 copy-start.1
  150.9 0.7 copy-start.7
  151.7 0.7 copy-start.9
  152.4 0.7 copy-start.11
  153.2 7.8 %copy-start.2 = (bf16[32,2,2,16,384]{4,3,2,1,0:T(8,128)(2,1)S(1)}, bf16[32,2,2,16,384]{4,3,2,1,0:T(8,128)(2,1)}, u32[]{:S(2)}) copy-start(bf16[32,2,2,16,384]{4,3,2,1,0:T(8,128)(2,1)} %copy-done) | copy-start | bytes 4718596

commit v4 on v3

--- a/solution.py
+++ b/solution.py
@@ -332,6 +332,10 @@
     return pl.BlockSpec(memory_space=pltpu.VMEM)
 
 
+def small_kernel():
+    return pltpu.CompilerParams(vmem_limit_bytes=4 * 1024 * 1024)
+
+
 def smem():
     return pl.BlockSpec(memory_space=pltpu.SMEM)
 
@@ -348,6 +352,7 @@
         + [pl.BlockSpec(block, lambda i, at=first + at: (at, RUNS - 1, 0, 0, 0, 0)) for at in range(3)],
         out_specs=whole(),
         scratch_shapes=[pltpu.VMEM((RUNS, GROUP, LANES), jnp.float32)],
+        compiler_params=small_kernel(),
         name="tail_message",
     )(me, *letters, buf, buf, buf)
 
@@ -428,8 +433,9 @@
         spread_kernel,
         out_shape=jax.ShapeDtypeStruct((MEMBERS * RUNS, 2, 2, GROUP, PIECE), samples.dtype),
         in_specs=[pl.BlockSpec(memory_space=pl.ANY)],
-        out_specs=pl.BlockSpec(memory_space=pl.ANY),
+        out_specs=whole(),
         scratch_shapes=[pltpu.SemaphoreType.DMA((2, 2))],
+        compiler_params=small_kernel(),
         name="spread",
     )(samples.reshape(2, 2, MEMBERS * RUNS, GROUP, PIECE))
     buf = lax.all_to_all(parts, ("chan", "zl"), split_axis=0, concat_axis=0, tiled=True)
@@ -458,6 +464,7 @@
     return pl.pallas_call(
         functools.partial(last_kernel, NBIN / (SLAB * RUNS * size)),
         out_shape=jax.ShapeDtypeStruct((16 * 4, RUNS * GROUP), jnp.float32),
+        compiler_params=small_kernel(),
         name="last_sum",
     )(shares.reshape(size, RUNS, 8, LANES)).reshape(16, 4, RUNS * GROUP)
 

time: 185 us -> 132 us (0.71)
  Pallas kernels: 62.6 us -> 12.4 us
  local copies, waits for them, and re-layouts: 5.3 us -> 1.92 us
    pallas_call x1, Pallas kernels: 48.8 us -> 1.35 us  [on_device(): pl.pallas_call(spread_kernel, out_shape=jax.ShapeDtypeStruct((MEMBERS * R...]
    unnamed x34 -> x16, local copies, waits for them, and re-layouts: 5 us -> 1.63 us
  transfers between devices with their start and end apart: 5 -> 5, of which waited for: 3 -> 3; matrix products, arithmetic and copies ran while one was open for 1% -> 2% of each run, Pallas kernels for 4% -> 6%
where the time goes in v4:
time: 132 us; the launch traced here: 131 us
  waiting for transfers between devices  65.2 us (49%)
  starting transfers between devices  30.6 us (23%)
  blocking collectives  19.3 us (15%)
  Pallas kernels  12.4 us (9%)
  local copies, waits for them, and re-layouts  1.92 us (1%)
  other arithmetic  1.56 us (1%)
    ppermute x3, waiting for transfers between devices, turned_to(): lax.ppermute(block_for(there), axis, [(i, (i + turn) % size) for i in ran...  57.3 us
    all_to_all x1, blocking collectives, on_device(): lax.all_to_all(partial, ('xy', 'zl'), split_axis=0, concat_axis=0, tiled=...  19.3 us
    all_to_all x1, starting transfers between devices, on_device(): lax.all_to_all(parts, ('chan', 'zl'), split_axis=0, concat_axis=0, tiled=...  15.6 us
    ppermute x3, starting transfers between devices, turned_to(): lax.ppermute(block_for(there), axis, [(i, (i + turn) % size) for i in ran...  11.3 us
    all_to_all x1, waiting for transfers between devices, on_device(): lax.all_to_all(parts, ('chan', 'zl'), split_axis=0, concat_axis=0, tiled=...  7.93 us
    pallas_call x1, Pallas kernels, fold_frames(): pl.pallas_call(later_kernel, out_shape=[jax.ShapeDtypeStruct((ACC_ROWS, 4...  7.61 us
    ppermute x1, starting transfers between devices, from_before(): return lax.ppermute(block, 'xy', [(i, i + 1) for i in range(size - 1)])  3.62 us
    pallas_call x1, Pallas kernels, fold_frames(): pl.pallas_call(first_kernel, out_shape=jax.ShapeDtypeStruct((NBIN // 16,...  2.71 us
  transfers between devices with their start and end apart: 5, of which 3 were waited for; matrix products, arithmetic and copies ran while one was open for 2% of the time, Pallas kernels for 6%

profile of v4, /device:TPU:8, one launch (start us, length us, event | category | flops | bytes accessed | tf_op | source)
XLA Modules:
  0.0 131.3 jit_solution(54827632673700689)
XLA Ops:
  0.0 0.0 copy-start
  0.0 1.4 %copy-done = bf16[2,2,512,384]{3,2,1,0:T(8,128)(2,1)S(1)} copy-done((bf16[2,2,512,384]{3,2,1,0:T(8,128)(2,1)S(1)}, bf16[2,2,512,384]{3,2,1,0:T(8,128)(2,1)}, u32[]{:S(2)}) %copy-start) | copy-done | bytes 1572888
  1.4 1.4 %spread.1 = bf16[32,2,2,16,384]{4,3,2,1,0:T(8,128)(2,1)} custom-call(bf16[2,2,32,16,384]{4,3,2,1,0:T(8,128)(2,1)S(1)} %bitcast.29), custom_call_target="tpu_custom_call" | custom-call | tf_op jit(solution)/shard_map/spread/pallas_call | solution.py:432
  2.8 0.0 copy-start.3
  2.8 0.0 copy-start.4
  2.8 0.0 copy-start.5
  2.8 0.0 copy-start.6
  2.8 15.6 %all-to-all-start = ((bf16[32,2,2,16,384]{4,3,2,1,0:T(8,128)(2,1)}), bf16[32,2,2,16,384]{4,3,2,1,0:T(8,128)(2,1)S(1)}, u32[]{:S(2)}, u32[]{:S(2)}) async-start(bf16[32,2,2,16,384]{4,3,2,1,0:T(8,128)(2,1)} %spread.1), calls=%async_computation | async-start | bytes 3145728 | tf_op jit(solution)/shard_map/all_to_all | solution.py:441
  18.5 0.0 copy-done.3
  18.5 0.1 reduce
  18.7 0.1 broadcast_in_dim.2
  18.7 0.1 sub.29
  18.8 0.0 copy-done.4
  18.8 0.1 copy.14
  18.9 0.0 copy-done.5
  18.9 0.1 copy.13
  19.0 0.1 add_select_fusion
  19.2 3.7 %collective-permute-start = (f32[48,128]{1,0:T(8,128)S(1)}, f32[48,128]{1,0:T(8,128)S(1)}, u32[]{:S(2)}, u32[]{:S(2)}) collective-permute-start(f32[48,128]{1,0:T(8,128)S(1)} %get-tuple-element.16), channel_id=1, source_target_pairs={{0,8},{8,16},{16,24},{24,0},{1,9},{9,17},{17,25},{25,1},{2,10},{10... | collective-permute-start | bytes 73736 | tf_op jit(solution)/shard_map/ppermute | solution.py:415
  22.9 4.3 %collective-permute-start.1 = (f32[48,128]{1,0:T(8,128)S(1)}, f32[48,128]{1,0:T(8,128)S(1)}, u32[]{:S(2)}, u32[]{:S(2)}) collective-permute-start(f32[48,128]{1,0:T(8,128)S(1)} %get-tuple-element.17), channel_id=1, source_target_pairs={{0,16},{8,24},{16,0},{24,8},{1,17},{9,25},{17,1},{25,9},{2,18},{10... | collective-permute-start | bytes 73736 | tf_op jit(solution)/shard_map/ppermute | solution.py:415
  27.2 3.4 %collective-permute-start.2 = (f32[48,128]{1,0:T(8,128)S(1)}, f32[48,128]{1,0:T(8,128)S(1)}, u32[]{:S(2)}, u32[]{:S(2)}) collective-permute-start(f32[48,128]{1,0:T(8,128)S(1)} %get-tuple-element.15), channel_id=1, source_target_pairs={{0,24},{8,0},{16,8},{24,16},{1,25},{9,1},{17,9},{25,17},{2,26},{10... | collective-permute-start | bytes 73736 | tf_op jit(solution)/shard_map/ppermute | solution.py:415
  30.6 0.0 copy-done.6
  30.6 0.1 dynamic-slice_multiply_fusion
  30.6 0.1 mul.100
  30.8 1.2 fusion.1
  32.0 56.5 %collective-permute-done.refs_1_ = f32[48,128]{1,0:T(8,128)S(1)} collective-permute-done((f32[48,128]{1,0:T(8,128)S(1)}, f32[48,128]{1,0:T(8,128)S(1)}, u32[]{:S(2)}, u32[]{:S(2)}) %collective-permute-start) | collective-permute-done | bytes 24608 | tf_op jit(solution)/shard_map/ppermute | solution.py:415
  88.5 0.0 collective-permute-done.1.refs_2_
  88.5 0.7 collective-permute-done.2.refs_3_
  89.3 7.9 %all-to-all-done = bf16[32,2,2,16,384]{4,3,2,1,0:T(8,128)(2,1)S(1)} async-done(((bf16[32,2,2,16,384]{4,3,2,1,0:T(8,128)(2,1)}), bf16[32,2,2,16,384]{4,3,2,1,0:T(8,128)(2,1)S(1)}, u32[]{:S(2)}, u32[]{:S(2)}) %all-to-all-start) | async-done | bytes 1572896 | tf_op jit(solution)/shard_map/all_to_all | solution.py:441
  97.2 0.0 copy-start.1
  97.2 0.0 copy-start.2
  97.2 3.6 %collective-permute-start.3 = (bf16[3,1,2,2,16,384]{5,4,3,2,1,0:T(8,128)(2,1)S(1)}, bf16[3,1,2,2,16,384]{5,4,3,2,1,0:T(8,128)(2,1)S(1)}, u32[]{:S(2)}, u32[]{:S(2)}) collective-permute-start(bf16[3,1,2,2,16,384]{5,4,3,2,1,0:T(8,128)(2,1)S(1)} %tail_message.1), channel_id=1, source_target_pairs={{0,32},{32,64},{64,96},{96,128},{128,160},{160,192},{192,224},{224... | collective-permute-start | bytes 442376 | tf_op jit(solution)/shard_map/ppermute | solution.py:420
  100.9 0.0 copy-done.1
  100.9 0.0 copy-done.2
  100.9 7.6 %later_frames.1 = (f32[1168,64]{1,0:T(8,128)S(1)}, f32[4,48,128]{2,1,0:T(8,128)S(1)}) custom-call(s32[1]{0:T(128)} %bitcast.2.me_ref, f32[48,128]{1,0:T(8,128)S(1)} %get-tuple-element.18.refs_0_, f32[48,128]{1,0:T(8,128)S(1)} %collective-permute-done.refs_1_, f32[48,128]{1,0:T(8,128)S(1)} %collective-permute-done.1.refs_2_, ...), custom_call_target="tpu_custom_call" | custom-call | flops 2415919104 | bytes 30000000 | tf_op jit(solution)/shard_map/later_frames/pallas_call | solution.py:366
  108.5 0.0 collective-permute-done.3.tail_ref
  108.5 2.7 %first_frame.1 = f32[64,8,128]{2,1,0:T(8,128)S(1)} custom-call(bf16[8,4,2,2,16,384]{5,4,3,2,1,0:T(8,128)(2,1)S(1)} %bitcast.28, bf16[3,1,2,2,16,384]{5,4,3,2,1,0:T(8,128)(2,1)S(1)} %collective-permute-done.3.tail_ref, f32[4,48,128]{2,1,0:T(8,128)S(1)} %get-tuple-element.7.sorted_ref, f32[2,512,128]{2,1,0:T(8,128)S(1)} %maximum_multiply_fusion.refs_5_.chirp_ref, ...), custom_call_target="tpu_custom_call" | custom-call | flops 805306368 | bytes 10000000 | tf_op jit(solution)/shard_map/first_frame/pallas_call | solution.py:384
  111.2 19.3 %all_to_all.10 = f32[64,8,128]{2,1,0:T(8,128)S(1)} all-to-all(f32[64,8,128]{2,1,0:T(8,128)S(1)} %first_frame.1), channel_id=1, replica_groups=mesh['xy'=16,'zl'=4,'chan'=8] {'xy','zl'}, dimensions={0} | all-to-all | bytes 524288 | tf_op jit(solution)/shard_map/all_to_all | solution.py:462
  130.6 0.7 last_sum.1
  (13 shorter events, 0.2 us)
Async XLA Ops:
  0.0 1.4 %copy-start = (bf16[2,2,512,384]{3,2,1,0:T(8,128)(2,1)S(1)}, bf16[2,2,512,384]{3,2,1,0:T(8,128)(2,1)}, u32[]{:S(2)}) copy-start(bf16[2,2,512,384]{3,2,1,0:T(8,128)(2,1)} %param.7) | copy-start | bytes 4718596
  2.8 15.7 %copy-start.3 = (s32[3072]{0:T(1024)S(1)}, s32[3072]{0:T(1024)}, u32[]{:S(2)}) copy-start(s32[3072]{0:T(1024)} %param.11) | copy-start | bytes 36868
  2.8 16.0 %copy-start.4 = (f32[64,12]{0,1:T(8,128)S(1)}, f32[64,12]{0,1:T(8,128)}, u32[]{:S(2)}) copy-start(f32[64,12]{0,1:T(8,128)} %param.8) | copy-start | bytes 9220
  2.8 16.1 %copy-start.5 = (s32[64,12]{0,1:T(8,128)S(1)}, s32[64,12]{0,1:T(8,128)}, u32[]{:S(2)}) copy-start(s32[64,12]{0,1:T(8,128)} %param.9) | copy-start | bytes 9220
  2.8 27.7 %copy-start.6 = (f32[64]{0:T(128)S(1)}, f32[64]{0:T(128)}, u32[]{:S(2)}) copy-start(f32[64]{0:T(128)} %param.10) | copy-start | bytes 772
  2.8 94.4 %all-to-all-start = ((bf16[32,2,2,16,384]{4,3,2,1,0:T(8,128)(2,1)}), bf16[32,2,2,16,384]{4,3,2,1,0:T(8,128)(2,1)S(1)}, u32[]{:S(2)}, u32[]{:S(2)}) async-start(bf16[32,2,2,16,384]{4,3,2,1,0:T(8,128)(2,1)} %spread.1), calls=%async_computation | async-start | bytes 3145728 | tf_op jit(solution)/shard_map/all_to_all | solution.py:441
  19.2 69.3 %collective-permute-start = (f32[48,128]{1,0:T(8,128)S(1)}, f32[48,128]{1,0:T(8,128)S(1)}, u32[]{:S(2)}, u32[]{:S(2)}) collective-permute-start(f32[48,128]{1,0:T(8,128)S(1)} %get-tuple-element.16), channel_id=1, source_target_pairs={{0,8},{8,16},{16,24},{24,0},{1,9},{9,17},{17,25},{25,1},{2,10},{10... | collective-permute-start | bytes 73736 | tf_op jit(solution)/shard_map/ppermute | solution.py:415
  22.9 65.6 %collective-permute-start.1 = (f32[48,128]{1,0:T(8,128)S(1)}, f32[48,128]{1,0:T(8,128)S(1)}, u32[]{:S(2)}, u32[]{:S(2)}) collective-permute-start(f32[48,128]{1,0:T(8,128)S(1)} %get-tuple-element.17), channel_id=1, source_target_pairs={{0,16},{8,24},{16,0},{24,8},{1,17},{9,25},{17,1},{25,9},{2,18},{10... | collective-permute-start | bytes 73736 | tf_op jit(solution)/shard_map/ppermute | solution.py:415
  27.2 62.1 %collective-permute-start.2 = (f32[48,128]{1,0:T(8,128)S(1)}, f32[48,128]{1,0:T(8,128)S(1)}, u32[]{:S(2)}, u32[]{:S(2)}) collective-permute-start(f32[48,128]{1,0:T(8,128)S(1)} %get-tuple-element.15), channel_id=1, source_target_pairs={{0,24},{8,0},{16,8},{24,16},{1,25},{9,1},{17,9},{25,17},{2,26},{10... | collective-permute-start | bytes 73736 | tf_op jit(solution)/shard_map/ppermute | solution.py:415
  97.2 3.7 %copy-start.1 = (bf16[2,256,256]{2,1,0:T(8,128)(2,1)S(1)}, bf16[2,256,256]{2,1,0:T(8,128)(2,1)}, u32[]{:S(2)}) copy-start(bf16[2,256,256]{2,1,0:T(8,128)(2,1)} %constant.90.clone.refs_7_.table_ref) | copy-start | bytes 786436
  97.2 3.7 %copy-start.2 = (f32[2,32,128]{2,1,0:T(8,128)S(1)}, f32[2,32,128]{2,1,0:T(8,128)}, u32[]{:S(2)}) copy-start(f32[2,32,128]{2,1,0:T(8,128)} %constant.89.clone.refs_6_.twist_ref) | copy-start | bytes 98308
  97.2 11.3 %collective-permute-start.3 = (bf16[3,1,2,2,16,384]{5,4,3,2,1,0:T(8,128)(2,1)S(1)}, bf16[3,1,2,2,16,384]{5,4,3,2,1,0:T(8,128)(2,1)S(1)}, u32[]{:S(2)}, u32[]{:S(2)}) collective-permute-start(bf16[3,1,2,2,16,384]{5,4,3,2,1,0:T(8,128)(2,1)S(1)} %tail_message.1), channel_id=1, source_target_pairs={{0,32},{32,64},{64,96},{96,128},{128,160},{160,192},{192,224},{224... | collective-permute-start | bytes 442376 | tf_op jit(solution)/shard_map/ppermute | solution.py:420

commit v5 on v4

--- a/solution.py
+++ b/solution.py
@@ -25,7 +25,7 @@
 BLOCKS = SLAB // BLK
 WINDOW = 144
 ACC_ROWS = NBIN + WINDOW
-SPAN = 16
+DOT_ROWS = 256
 BASE_ROW = GROUP + KEPT
 LETTER_ROWS = BASE_ROW + 8
 HALF_ROOT = math.sqrt(0.5)
@@ -107,7 +107,7 @@
 
 
 def frame_profile(
-    row_of, weight_of, base_of, marks_of, chirp_ref, twist_ref, table_ref, mid, y_refs, v_refs, stokes_ref, acc
+    row_of, weight_of, base_of, marks_of, chirp_ref, twist_ref, table_ref, mid, y_refs, s_refs, stokes_ref, acc
 ):
     def rows_in(pol, b):
         rows = []
@@ -134,21 +134,30 @@
                 y_refs[pol, 0, *where] = high
                 y_refs[pol, 1, *where] = low
 
-    def lanes_there_and_back(pol, m):
-        rows = pl.ds(SPAN * GROUP * m, SPAN * GROUP)
-        spectrum = lane_dft(y_refs[pol, 0, rows], y_refs[pol, 1, rows], table_ref[0], table_ref[1])
-        re, im = spectrum[:, :LANES], spectrum[:, LANES:]
+    def lanes(pol, m):
+        rows = pl.ds(DOT_ROWS * m, DOT_ROWS)
+        s_refs[pol, rows] = lane_dft(y_refs[pol, 0, rows], y_refs[pol, 1, rows], table_ref[0], table_ref[1])
+
+    def filtered(pol, k):
+        rows = pl.ds(GROUP * k, GROUP)
+        re, im = s_refs[pol, rows, :LANES], s_refs[pol, rows, LANES:]
         cos, sin = chirp_ref[0, rows], chirp_ref[1, rows]
-        swapped = jnp.concatenate([re * sin + im * cos, re * cos - im * sin], axis=1)
-        back = lane_dft(*split(swapped), table_ref[0], table_ref[1])
-        im, re = (back[:, part].reshape(SPAN, GROUP, LANES) for part in (slice(0, LANES), slice(LANES, None)))
-        cos = twist_ref[0, SPAN * m : SPAN * (m + 1)][:, None, :]
-        sin = twist_ref[1, SPAN * m : SPAN * (m + 1)][:, None, :]
-        v_refs[pol, 0, SPAN * m : SPAN * (m + 1)] = re * cos + im * sin
-        v_refs[pol, 1, SPAN * m : SPAN * (m + 1)] = im * cos - re * sin
+        for part, value in enumerate((re * sin + im * cos, re * cos - im * sin)):
+            high, low = split(value)
+            where = (rows, pl.ds(LANES * part, LANES))
+            y_refs[pol, 0, *where] = high
+            y_refs[pol, 1, *where] = low
+
+    def untwisted(pol, k):
+        rows = pl.ds(GROUP * k, GROUP)
+        im, re = s_refs[pol, rows, :LANES], s_refs[pol, rows, LANES:]
+        if k == 0:
+            return re, im
+        cos, sin = twist_ref[0, k : k + 1], twist_ref[1, k : k + 1]
+        return re * cos + im * sin, im * cos - re * sin
 
     def rows_back(pol, b):
-        values = dft8([(v_refs[pol, 0, 4 * a + b], v_refs[pol, 1, 4 * a + b]) for a in range(8)], 1)
+        values = dft8([untwisted(pol, 4 * a + b) for a in range(8)], 1)
         for na, value in enumerate(values):
             value = turned(value, b * na, 1)
             mid[pol, 0, b, na] = value[0]
@@ -169,31 +178,39 @@
             for s, value in enumerate((power_x + power_y, power_x - power_y, 2.0 * cross_re, 2.0 * cross_im)):
                 stokes_ref[row // 2, pl.ds(GROUP * s, GROUP), lanes] = value.astype(jnp.bfloat16)
 
-    bins = lax.broadcasted_iota(jnp.int32, (WINDOW, BLK), 0)
+    bins = lax.broadcasted_iota(jnp.int32, (WINDOW, BLK), 0).astype(jnp.bfloat16)
 
     def fold(m):
-        onehot = jnp.where(bins == marks_of(m), 1.0, 0.0).astype(jnp.bfloat16)
+        onehot = jnp.where(bins == marks_of(m).astype(jnp.bfloat16), jnp.bfloat16(1), jnp.bfloat16(0))
         part = lax.dot_general(
             onehot, stokes_ref[m], (((1,), (1,)), ((), ())), preferred_element_type=jnp.float32
         )
         place = pl.ds(pl.multiple_of(base_of(m), 8), WINDOW)
         acc[place] += part
 
-    spans = ROWS // SPAN
+    spans = ROWS * GROUP // DOT_ROWS
     for b in range(4):
         rows_in(0, b)
     for ka in range(8):
         rows_across(0, ka)
     for m in range(spans):
-        lanes_there_and_back(0, m)
-        for b in range(4 * m // spans, 4 * (m + 1) // spans):
-            rows_in(1, b)
+        lanes(0, m)
+    for b in range(4):
+        rows_in(1, b)
     for ka in range(8):
         rows_across(1, ka)
+    for k in range(ROWS):
+        filtered(0, k)
     for m in range(spans):
-        lanes_there_and_back(1, m)
-        for b in range(4 * m // spans, 4 * (m + 1) // spans):
-            rows_back(0, b)
+        lanes(1, m)
+    for m in range(spans):
+        lanes(0, m)
+    for k in range(ROWS):
+        filtered(1, k)
+    for b in range(4):
+        rows_back(0, b)
+    for m in range(spans):
+        lanes(1, m)
     for b in range(4):
         rows_back(1, b)
     for na in range(8):
@@ -290,7 +307,8 @@
     )
     acc[:WINDOW] += acc[NBIN:]
     for share in range(NBIN // 16):
-        out_ref[share] = jnp.concatenate([acc[16 * share : 16 * share + 8], acc[16 * share + 8 : 16 * share + 16]], axis=1)
+        place = share % RUNS * (NBIN // 16 // RUNS) + share // RUNS
+        out_ref[place] = jnp.concatenate([acc[16 * share : 16 * share + 8], acc[16 * share + 8 : 16 * share + 16]], axis=1)
 
 
 def tail_kernel(me_ref, *refs):
@@ -323,7 +341,7 @@
     return [
         pltpu.VMEM((2, 2, 4, 8, GROUP, LANES), jnp.float32),
         pltpu.VMEM((2, 2, ROWS * GROUP, 2 * LANES), jnp.bfloat16),
-        pltpu.VMEM((2, 2, ROWS, GROUP, LANES), jnp.float32),
+        pltpu.VMEM((2, ROWS * GROUP, 2 * LANES), jnp.float32),
         pltpu.VMEM((BLOCKS, 4 * GROUP, BLK), jnp.bfloat16),
     ]
 
@@ -400,7 +418,7 @@
 
 
 def last_kernel(scale, shares_ref, out_ref):
-    total = [jnp.sum(shares_ref[:, slab], axis=0) * scale for slab in range(RUNS)]
+    total = [jnp.sum(shares_ref[slab], axis=0) * scale for slab in range(RUNS)]
     for half in range(2):
         for s in range(4):
             lanes = slice(64 * half + GROUP * s, 64 * half + GROUP * (s + 1))
@@ -432,7 +450,7 @@
     parts = pl.pallas_call(
         spread_kernel,
         out_shape=jax.ShapeDtypeStruct((MEMBERS * RUNS, 2, 2, GROUP, PIECE), samples.dtype),
-        in_specs=[pl.BlockSpec(memory_space=pl.ANY)],
+        in_specs=[pl.BlockSpec(memory_space=pltpu.HBM)],
         out_specs=whole(),
         scratch_shapes=[pltpu.SemaphoreType.DMA((2, 2))],
         compiler_params=small_kernel(),
@@ -459,14 +477,14 @@
     chirp = chirp_table(lax.dynamic_slice_in_dim(sweep, me * GROUP, GROUP, 0))
 
     partial = fold_frames(buf, from_before, me.reshape(1), letters, chirp)
-    shares = lax.all_to_all(partial, ("xy", "zl"), split_axis=0, concat_axis=0, tiled=True)
+    shares = lax.all_to_all(partial, ("zl", "xy"), split_axis=0, concat_axis=0, tiled=True)
     size = lax.axis_size("xy")
     return pl.pallas_call(
         functools.partial(last_kernel, NBIN / (SLAB * RUNS * size)),
         out_shape=jax.ShapeDtypeStruct((16 * 4, RUNS * GROUP), jnp.float32),
         compiler_params=small_kernel(),
         name="last_sum",
-    )(shares.reshape(size, RUNS, 8, LANES)).reshape(16, 4, RUNS * GROUP)
+    )(shares.reshape(RUNS, size, 8, LANES)).reshape(16, 4, RUNS * GROUP)
 
 
 def solution(mesh):

time: 132 us -> 130 us (0.985)
  the two profiles are of different devices: /device:TPU:8 before, /device:TPU:2 now
where the time goes in v5:
time: 130 us
  waiting for transfers between devices  65.2 us (50%)
  starting transfers between devices  30.6 us (24%)
  blocking collectives  19.2 us (15%)
  Pallas kernels  11.3 us (9%)
  local copies, waits for them, and re-layouts  1.92 us (1%)
  other arithmetic  1.56 us (1%)
    ppermute x3, waiting for transfers between devices, turned_to(): lax.ppermute(block_for(there), axis, [(i, (i + turn) % size) for i in ran...  57.3 us
    all_to_all x1, blocking collectives, on_device(): lax.all_to_all(partial, ('zl', 'xy'), split_axis=0, concat_axis=0, tiled=...  19.2 us
    all_to_all x1, starting transfers between devices, on_device(): lax.all_to_all(parts, ('chan', 'zl'), split_axis=0, concat_axis=0, tiled=...  15.6 us
    ppermute x3, starting transfers between devices, turned_to(): lax.ppermute(block_for(there), axis, [(i, (i + turn) % size) for i in ran...  11.3 us
    all_to_all x1, waiting for transfers between devices, on_device(): lax.all_to_all(parts, ('chan', 'zl'), split_axis=0, concat_axis=0, tiled=...  7.93 us
    pallas_call x1, Pallas kernels, fold_frames(): pl.pallas_call(later_kernel, out_shape=[jax.ShapeDtypeStruct((ACC_ROWS, 4...  6.79 us
    ppermute x1, starting transfers between devices, from_before(): return lax.ppermute(block, 'xy', [(i, i + 1) for i in range(size - 1)])  3.62 us
  transfers between devices with their start and end apart: 5, of which 3 were waited for; matrix products, arithmetic and copies ran while one was open for 2% of the time, Pallas kernels for 5%

profile of v5, /device:TPU:2, one launch (start us, length us, event | category | flops | bytes accessed | tf_op | source)
XLA Modules:
  0.0 130.1 jit_solution(15502526938083320362)
XLA Ops:
  0.0 0.0 copy-start
  0.0 1.4 %copy-done = bf16[2,2,512,384]{3,2,1,0:T(8,128)(2,1)S(1)} copy-done((bf16[2,2,512,384]{3,2,1,0:T(8,128)(2,1)S(1)}, bf16[2,2,512,384]{3,2,1,0:T(8,128)(2,1)}, u32[]{:S(2)}) %copy-start) | copy-done | bytes 1572888
  1.4 1.4 %spread.1 = bf16[32,2,2,16,384]{4,3,2,1,0:T(8,128)(2,1)} custom-call(bf16[2,2,32,16,384]{4,3,2,1,0:T(8,128)(2,1)S(1)} %bitcast.29), custom_call_target="tpu_custom_call" | custom-call | tf_op jit(solution)/shard_map/spread/pallas_call | solution.py:450
  2.8 0.0 copy-start.3
  2.8 0.0 copy-start.4
  2.8 0.0 copy-start.5
  2.8 0.0 copy-start.6
  2.8 15.6 %all-to-all-start = ((bf16[32,2,2,16,384]{4,3,2,1,0:T(8,128)(2,1)}), bf16[32,2,2,16,384]{4,3,2,1,0:T(8,128)(2,1)S(1)}, u32[]{:S(2)}, u32[]{:S(2)}) async-start(bf16[32,2,2,16,384]{4,3,2,1,0:T(8,128)(2,1)} %spread.1), calls=%async_computation | async-start | bytes 3145728 | tf_op jit(solution)/shard_map/all_to_all | solution.py:459
  18.5 0.0 copy-done.3
  18.5 0.1 reduce
  18.7 0.1 broadcast_in_dim.2
  18.7 0.1 sub.29
  18.8 0.0 copy-done.4
  18.8 0.1 copy.14
  18.9 0.0 copy-done.5
  18.9 0.1 copy.13
  19.0 0.1 add_select_fusion
  19.2 3.7 %collective-permute-start = (f32[48,128]{1,0:T(8,128)S(1)}, f32[48,128]{1,0:T(8,128)S(1)}, u32[]{:S(2)}, u32[]{:S(2)}) collective-permute-start(f32[48,128]{1,0:T(8,128)S(1)} %get-tuple-element.16), channel_id=1, source_target_pairs={{0,8},{8,16},{16,24},{24,0},{1,9},{9,17},{17,25},{25,1},{2,10},{10... | collective-permute-start | bytes 73736 | tf_op jit(solution)/shard_map/ppermute | solution.py:433
  22.9 4.3 %collective-permute-start.1 = (f32[48,128]{1,0:T(8,128)S(1)}, f32[48,128]{1,0:T(8,128)S(1)}, u32[]{:S(2)}, u32[]{:S(2)}) collective-permute-start(f32[48,128]{1,0:T(8,128)S(1)} %get-tuple-element.17), channel_id=1, source_target_pairs={{0,16},{8,24},{16,0},{24,8},{1,17},{9,25},{17,1},{25,9},{2,18},{10... | collective-permute-start | bytes 73736 | tf_op jit(solution)/shard_map/ppermute | solution.py:433
  27.2 3.4 %collective-permute-start.2 = (f32[48,128]{1,0:T(8,128)S(1)}, f32[48,128]{1,0:T(8,128)S(1)}, u32[]{:S(2)}, u32[]{:S(2)}) collective-permute-start(f32[48,128]{1,0:T(8,128)S(1)} %get-tuple-element.15), channel_id=1, source_target_pairs={{0,24},{8,0},{16,8},{24,16},{1,25},{9,1},{17,9},{25,17},{2,26},{10... | collective-permute-start | bytes 73736 | tf_op jit(solution)/shard_map/ppermute | solution.py:433
  30.6 0.0 copy-done.6
  30.6 0.1 dynamic-slice_multiply_fusion
  30.6 0.1 mul.100
  30.8 1.2 fusion.1
  32.0 56.5 %collective-permute-done.refs_1_ = f32[48,128]{1,0:T(8,128)S(1)} collective-permute-done((f32[48,128]{1,0:T(8,128)S(1)}, f32[48,128]{1,0:T(8,128)S(1)}, u32[]{:S(2)}, u32[]{:S(2)}) %collective-permute-start) | collective-permute-done | bytes 24608 | tf_op jit(solution)/shard_map/ppermute | solution.py:433
  88.5 0.0 collective-permute-done.1.refs_2_
  88.5 0.7 collective-permute-done.2.refs_3_
  89.3 7.9 %all-to-all-done = bf16[32,2,2,16,384]{4,3,2,1,0:T(8,128)(2,1)S(1)} async-done(((bf16[32,2,2,16,384]{4,3,2,1,0:T(8,128)(2,1)}), bf16[32,2,2,16,384]{4,3,2,1,0:T(8,128)(2,1)S(1)}, u32[]{:S(2)}, u32[]{:S(2)}) %all-to-all-start) | async-done | bytes 1572896 | tf_op jit(solution)/shard_map/all_to_all | solution.py:459
  97.2 0.0 copy-start.1
  97.2 0.0 copy-start.2
  97.2 3.6 %collective-permute-start.3 = (bf16[3,1,2,2,16,384]{5,4,3,2,1,0:T(8,128)(2,1)S(1)}, bf16[3,1,2,2,16,384]{5,4,3,2,1,0:T(8,128)(2,1)S(1)}, u32[]{:S(2)}, u32[]{:S(2)}) collective-permute-start(bf16[3,1,2,2,16,384]{5,4,3,2,1,0:T(8,128)(2,1)S(1)} %tail_message.1), channel_id=1, source_target_pairs={{0,32},{32,64},{64,96},{96,128},{128,160},{160,192},{192,224},{224... | collective-permute-start | bytes 442376 | tf_op jit(solution)/shard_map/ppermute | solution.py:438
  100.9 0.0 copy-done.1
  100.9 0.0 copy-done.2
  100.9 6.8 %later_frames.1 = (f32[1168,64]{1,0:T(8,128)S(1)}, f32[4,48,128]{2,1,0:T(8,128)S(1)}) custom-call(s32[1]{0:T(128)} %bitcast.2.me_ref, f32[48,128]{1,0:T(8,128)S(1)} %get-tuple-element.18.refs_0_, f32[48,128]{1,0:T(8,128)S(1)} %collective-permute-done.refs_1_, f32[48,128]{1,0:T(8,128)S(1)} %collective-permute-done.1.refs_2_, ...), custom_call_target="tpu_custom_call" | custom-call | flops 2415919104 | bytes 30000000 | tf_op jit(solution)/shard_map/later_frames/pallas_call | solution.py:384
  107.7 0.0 collective-permute-done.3.tail_ref
  107.7 2.4 %first_frame.1 = f32[64,8,128]{2,1,0:T(8,128)S(1)} custom-call(bf16[8,4,2,2,16,384]{5,4,3,2,1,0:T(8,128)(2,1)S(1)} %bitcast.28, bf16[3,1,2,2,16,384]{5,4,3,2,1,0:T(8,128)(2,1)S(1)} %collective-permute-done.3.tail_ref, f32[4,48,128]{2,1,0:T(8,128)S(1)} %get-tuple-element.7.sorted_ref, f32[2,512,128]{2,1,0:T(8,128)S(1)} %maximum_multiply_fusion.refs_5_.chirp_ref, ...), custom_call_target="tpu_custom_call" | custom-call | flops 805306368 | bytes 10000000 | tf_op jit(solution)/shard_map/first_frame/pallas_call | solution.py:402
  110.1 19.2 %all_to_all.10 = f32[64,8,128]{2,1,0:T(8,128)S(1)} all-to-all(f32[64,8,128]{2,1,0:T(8,128)S(1)} %first_frame.1), channel_id=1, replica_groups=mesh['xy'=16,'zl'=4,'chan'=8] {'zl','xy'}, dimensions={0} | all-to-all | bytes 524288 | tf_op jit(solution)/shard_map/all_to_all | solution.py:480
  129.3 0.7 last_sum.1
  (13 shorter events, 0.2 us)
Async XLA Ops:
  0.0 1.4 %copy-start = (bf16[2,2,512,384]{3,2,1,0:T(8,128)(2,1)S(1)}, bf16[2,2,512,384]{3,2,1,0:T(8,128)(2,1)}, u32[]{:S(2)}) copy-start(bf16[2,2,512,384]{3,2,1,0:T(8,128)(2,1)} %param.7) | copy-start | bytes 4718596
  2.8 15.7 %copy-start.3 = (s32[3072]{0:T(1024)S(1)}, s32[3072]{0:T(1024)}, u32[]{:S(2)}) copy-start(s32[3072]{0:T(1024)} %param.11) | copy-start | bytes 36868
  2.8 16.0 %copy-start.4 = (f32[64,12]{0,1:T(8,128)S(1)}, f32[64,12]{0,1:T(8,128)}, u32[]{:S(2)}) copy-start(f32[64,12]{0,1:T(8,128)} %param.8) | copy-start | bytes 9220
  2.8 16.1 %copy-start.5 = (s32[64,12]{0,1:T(8,128)S(1)}, s32[64,12]{0,1:T(8,128)}, u32[]{:S(2)}) copy-start(s32[64,12]{0,1:T(8,128)} %param.9) | copy-start | bytes 9220
  2.8 27.7 %copy-start.6 = (f32[64]{0:T(128)S(1)}, f32[64]{0:T(128)}, u32[]{:S(2)}) copy-start(f32[64]{0:T(128)} %param.10) | copy-start | bytes 772
  2.8 94.4 %all-to-all-start = ((bf16[32,2,2,16,384]{4,3,2,1,0:T(8,128)(2,1)}), bf16[32,2,2,16,384]{4,3,2,1,0:T(8,128)(2,1)S(1)}, u32[]{:S(2)}, u32[]{:S(2)}) async-start(bf16[32,2,2,16,384]{4,3,2,1,0:T(8,128)(2,1)} %spread.1), calls=%async_computation | async-start | bytes 3145728 | tf_op jit(solution)/shard_map/all_to_all | solution.py:459
  19.2 69.3 %collective-permute-start = (f32[48,128]{1,0:T(8,128)S(1)}, f32[48,128]{1,0:T(8,128)S(1)}, u32[]{:S(2)}, u32[]{:S(2)}) collective-permute-start(f32[48,128]{1,0:T(8,128)S(1)} %get-tuple-element.16), channel_id=1, source_target_pairs={{0,8},{8,16},{16,24},{24,0},{1,9},{9,17},{17,25},{25,1},{2,10},{10... | collective-permute-start | bytes 73736 | tf_op jit(solution)/shard_map/ppermute | solution.py:433
  22.9 65.6 %collective-permute-start.1 = (f32[48,128]{1,0:T(8,128)S(1)}, f32[48,128]{1,0:T(8,128)S(1)}, u32[]{:S(2)}, u32[]{:S(2)}) collective-permute-start(f32[48,128]{1,0:T(8,128)S(1)} %get-tuple-element.17), channel_id=1, source_target_pairs={{0,16},{8,24},{16,0},{24,8},{1,17},{9,25},{17,1},{25,9},{2,18},{10... | collective-permute-start | bytes 73736 | tf_op jit(solution)/shard_map/ppermute | solution.py:433
  27.2 62.1 %collective-permute-start.2 = (f32[48,128]{1,0:T(8,128)S(1)}, f32[48,128]{1,0:T(8,128)S(1)}, u32[]{:S(2)}, u32[]{:S(2)}) collective-permute-start(f32[48,128]{1,0:T(8,128)S(1)} %get-tuple-element.15), channel_id=1, source_target_pairs={{0,24},{8,0},{16,8},{24,16},{1,25},{9,1},{17,9},{25,17},{2,26},{10... | collective-permute-start | bytes 73736 | tf_op jit(solution)/shard_map/ppermute | solution.py:433
  97.2 3.7 %copy-start.1 = (bf16[2,256,256]{2,1,0:T(8,128)(2,1)S(1)}, bf16[2,256,256]{2,1,0:T(8,128)(2,1)}, u32[]{:S(2)}) copy-start(bf16[2,256,256]{2,1,0:T(8,128)(2,1)} %constant.90.clone.refs_7_.table_ref) | copy-start | bytes 786436
  97.2 3.7 %copy-start.2 = (f32[2,32,128]{2,1,0:T(8,128)S(1)}, f32[2,32,128]{2,1,0:T(8,128)}, u32[]{:S(2)}) copy-start(f32[2,32,128]{2,1,0:T(8,128)} %constant.89.clone.refs_6_.twist_ref) | copy-start | bytes 98308
  97.2 10.4 %collective-permute-start.3 = (bf16[3,1,2,2,16,384]{5,4,3,2,1,0:T(8,128)(2,1)S(1)}, bf16[3,1,2,2,16,384]{5,4,3,2,1,0:T(8,128)(2,1)S(1)}, u32[]{:S(2)}, u32[]{:S(2)}) collective-permute-start(bf16[3,1,2,2,16,384]{5,4,3,2,1,0:T(8,128)(2,1)S(1)} %tail_message.1), channel_id=1, source_target_pairs={{0,32},{32,64},{64,96},{96,128},{128,160},{160,192},{192,224},{224... | collective-permute-start | bytes 442376 | tf_op jit(solution)/shard_map/ppermute | solution.py:438

commit v6 on v5

--- a/solution.py
+++ b/solution.py
@@ -308,7 +308,9 @@
     acc[:WINDOW] += acc[NBIN:]
     for share in range(NBIN // 16):
         place = share % RUNS * (NBIN // 16 // RUNS) + share // RUNS
-        out_ref[place] = jnp.concatenate([acc[16 * share : 16 * share + 8], acc[16 * share + 8 : 16 * share + 16]], axis=1)
+        out_ref[place] = jnp.concatenate([acc[16 * share : 16 * share + 8], acc[16 * share + 8 : 16 * share + 16]], axis=1).astype(
+            out_ref.dtype
+        )
 
 
 def tail_kernel(me_ref, *refs):
@@ -325,15 +327,16 @@
         rest = rest - rounded.astype(jnp.float32)
 
 
-def spread_kernel(samples_ref, out_ref, sems):
-    copies = [
-        pltpu.make_async_copy(samples_ref.at[pol, part], out_ref.at[:, pol, part], sems.at[pol, part])
-        for pol in range(2)
-        for part in range(2)
-    ]
-    for copy in copies:
+def spread_kernel(samples_ref, out_ref, held, in_sems, out_sems):
+    places = [(pol, part) for pol in range(2) for part in range(2)]
+    arriving = [pltpu.make_async_copy(samples_ref.at[at], held.at[at], in_sems.at[at]) for at in places]
+    leaving = [pltpu.make_async_copy(held.at[at], out_ref.at[:, at[0], at[1]], out_sems.at[at]) for at in places]
+    for copy in arriving:
         copy.start()
-    for copy in copies:
+    for came, copy in zip(arriving, leaving):
+        came.wait()
+        copy.start()
+    for copy in leaving:
         copy.wait()
 
 
@@ -401,7 +404,7 @@
     block = (MEMBERS, 1) + buf.shape[2:]
     return pl.pallas_call(
         first_kernel,
-        out_shape=jax.ShapeDtypeStruct((NBIN // 16, 8, LANES), jnp.float32),
+        out_shape=jax.ShapeDtypeStruct((NBIN // 16, 8, LANES), jnp.bfloat16),
         grid=(1,),
         in_specs=[pl.BlockSpec(block, lambda i: (0,) * 6)] + [whole()] * 6,
         out_specs=whole(),
@@ -418,7 +421,7 @@
 
 
 def last_kernel(scale, shares_ref, out_ref):
-    total = [jnp.sum(shares_ref[slab], axis=0) * scale for slab in range(RUNS)]
+    total = [jnp.sum(shares_ref[slab].astype(jnp.float32), axis=0) * scale for slab in range(RUNS)]
     for half in range(2):
         for s in range(4):
             lanes = slice(64 * half + GROUP * s, 64 * half + GROUP * (s + 1))
@@ -451,9 +454,13 @@
         spread_kernel,
         out_shape=jax.ShapeDtypeStruct((MEMBERS * RUNS, 2, 2, GROUP, PIECE), samples.dtype),
         in_specs=[pl.BlockSpec(memory_space=pltpu.HBM)],
-        out_specs=whole(),
-        scratch_shapes=[pltpu.SemaphoreType.DMA((2, 2))],
-        compiler_params=small_kernel(),
+        out_specs=pl.BlockSpec(memory_space=pltpu.HBM),
+        scratch_shapes=[
+            pltpu.VMEM((2, 2, MEMBERS * RUNS, GROUP, PIECE), samples.dtype),
+            pltpu.SemaphoreType.DMA((2, 2)),
+            pltpu.SemaphoreType.DMA((2, 2)),
+        ],
+        compiler_params=pltpu.CompilerParams(vmem_limit_bytes=60 * 1024 * 1024),
         name="spread",
     )(samples.reshape(2, 2, MEMBERS * RUNS, GROUP, PIECE))
     buf = lax.all_to_all(parts, ("chan", "zl"), split_axis=0, concat_axis=0, tiled=True)

time: 130 us -> 129 us (level)
  the two profiles are of different devices: /device:TPU:2 before, /device:TPU:8 now
where the time goes in v6:
time: 129 us; the launch traced here: 128 us
  waiting for transfers between devices  65.2 us (51%)
  starting transfers between devices  30.6 us (24%)
  blocking collectives  18.2 us (14%)
  Pallas kernels  12.1 us (9%)
  other arithmetic  1.56 us (1%)
    ppermute x3, waiting for transfers between devices, turned_to(): lax.ppermute(block_for(there), axis, [(i, (i + turn) % size) for i in ran...  57.3 us
    all_to_all x1, blocking collectives, on_device(): lax.all_to_all(partial, ('zl', 'xy'), split_axis=0, concat_axis=0, tiled=...  18.2 us
    all_to_all x1, starting transfers between devices, on_device(): lax.all_to_all(parts, ('chan', 'zl'), split_axis=0, concat_axis=0, tiled=...  15.6 us
    ppermute x3, starting transfers between devices, turned_to(): lax.ppermute(block_for(there), axis, [(i, (i + turn) % size) for i in ran...  11.3 us
    all_to_all x1, waiting for transfers between devices, on_device(): lax.all_to_all(parts, ('chan', 'zl'), split_axis=0, concat_axis=0, tiled=...  7.93 us
    pallas_call x1, Pallas kernels, fold_frames(): pl.pallas_call(later_kernel, out_shape=[jax.ShapeDtypeStruct((ACC_ROWS, 4...  6.79 us
    ppermute x1, starting transfers between devices, from_before(): return lax.ppermute(block, 'xy', [(i, i + 1) for i in range(size - 1)])  3.62 us
  transfers between devices with their start and end apart: 5, of which 3 were waited for; matrix products, arithmetic and copies ran while one was open for 2% of the time, Pallas kernels for 5%

profile of v6, /device:TPU:8, one launch (start us, length us, event | category | flops | bytes accessed | tf_op | source)
XLA Modules:
  0.0 128.4 jit_solution(14317975515758090402)
XLA Ops:
  0.0 2.2 %spread.1 = bf16[32,2,2,16,384]{4,3,2,1,0:T(8,128)(2,1)} custom-call(bf16[2,2,32,16,384]{4,3,2,1,0:T(8,128)(2,1)} %bitcast.30), custom_call_target="tpu_custom_call" | custom-call | tf_op jit(solution)/shard_map/spread/pallas_call | solution.py:453
  2.2 0.0 copy-start.2
  2.2 0.0 copy-start.3
  2.3 0.0 copy-start.4
  2.3 0.0 copy-start.5
  2.3 15.6 %all-to-all-start = ((bf16[32,2,2,16,384]{4,3,2,1,0:T(8,128)(2,1)}), bf16[32,2,2,16,384]{4,3,2,1,0:T(8,128)(2,1)S(1)}, u32[]{:S(2)}, u32[]{:S(2)}) async-start(bf16[32,2,2,16,384]{4,3,2,1,0:T(8,128)(2,1)} %spread.1), calls=%async_computation | async-start | bytes 3145728 | tf_op jit(solution)/shard_map/all_to_all | solution.py:466
  18.0 0.0 copy-done.2
  18.0 0.1 reduce
  18.1 0.1 broadcast_in_dim.2
  18.2 0.1 sub.29
  18.3 0.0 copy-done.3
  18.3 0.1 copy.14
  18.4 0.0 copy-done.4
  18.4 0.1 copy.13
  18.5 0.1 add_select_fusion
  18.7 3.7 %collective-permute-start = (f32[48,128]{1,0:T(8,128)S(1)}, f32[48,128]{1,0:T(8,128)S(1)}, u32[]{:S(2)}, u32[]{:S(2)}) collective-permute-start(f32[48,128]{1,0:T(8,128)S(1)} %get-tuple-element.16), channel_id=1, source_target_pairs={{0,8},{8,16},{16,24},{24,0},{1,9},{9,17},{17,25},{25,1},{2,10},{10... | collective-permute-start | bytes 73736 | tf_op jit(solution)/shard_map/ppermute | solution.py:436
  22.4 4.3 %collective-permute-start.1 = (f32[48,128]{1,0:T(8,128)S(1)}, f32[48,128]{1,0:T(8,128)S(1)}, u32[]{:S(2)}, u32[]{:S(2)}) collective-permute-start(f32[48,128]{1,0:T(8,128)S(1)} %get-tuple-element.17), channel_id=1, source_target_pairs={{0,16},{8,24},{16,0},{24,8},{1,17},{9,25},{17,1},{25,9},{2,18},{10... | collective-permute-start | bytes 73736 | tf_op jit(solution)/shard_map/ppermute | solution.py:436
  26.6 3.4 %collective-permute-start.2 = (f32[48,128]{1,0:T(8,128)S(1)}, f32[48,128]{1,0:T(8,128)S(1)}, u32[]{:S(2)}, u32[]{:S(2)}) collective-permute-start(f32[48,128]{1,0:T(8,128)S(1)} %get-tuple-element.15), channel_id=1, source_target_pairs={{0,24},{8,0},{16,8},{24,16},{1,25},{9,1},{17,9},{25,17},{2,26},{10... | collective-permute-start | bytes 73736 | tf_op jit(solution)/shard_map/ppermute | solution.py:436
  30.0 0.0 copy-done.5
  30.0 0.1 dynamic-slice_multiply_fusion
  30.1 0.1 mul.100
  30.2 1.2 fusion.1
  31.5 56.5 %collective-permute-done.refs_1_ = f32[48,128]{1,0:T(8,128)S(1)} collective-permute-done((f32[48,128]{1,0:T(8,128)S(1)}, f32[48,128]{1,0:T(8,128)S(1)}, u32[]{:S(2)}, u32[]{:S(2)}) %collective-permute-start) | collective-permute-done | bytes 24608 | tf_op jit(solution)/shard_map/ppermute | solution.py:436
  88.0 0.0 collective-permute-done.1.refs_2_
  88.0 0.7 collective-permute-done.2.refs_3_
  88.7 7.9 %all-to-all-done = bf16[32,2,2,16,384]{4,3,2,1,0:T(8,128)(2,1)S(1)} async-done(((bf16[32,2,2,16,384]{4,3,2,1,0:T(8,128)(2,1)}), bf16[32,2,2,16,384]{4,3,2,1,0:T(8,128)(2,1)S(1)}, u32[]{:S(2)}, u32[]{:S(2)}) %all-to-all-start) | async-done | bytes 1572896 | tf_op jit(solution)/shard_map/all_to_all | solution.py:466
  96.7 0.0 copy-start
  96.7 0.0 copy-start.1
  96.7 3.6 %collective-permute-start.3 = (bf16[3,1,2,2,16,384]{5,4,3,2,1,0:T(8,128)(2,1)S(1)}, bf16[3,1,2,2,16,384]{5,4,3,2,1,0:T(8,128)(2,1)S(1)}, u32[]{:S(2)}, u32[]{:S(2)}) collective-permute-start(bf16[3,1,2,2,16,384]{5,4,3,2,1,0:T(8,128)(2,1)S(1)} %tail_message.1), channel_id=1, source_target_pairs={{0,32},{32,64},{64,96},{96,128},{128,160},{160,192},{192,224},{224... | collective-permute-start | bytes 442376 | tf_op jit(solution)/shard_map/ppermute | solution.py:441
  100.3 0.0 copy-done
  100.3 0.0 copy-done.1
  100.3 6.8 %later_frames.1 = (f32[1168,64]{1,0:T(8,128)S(1)}, f32[4,48,128]{2,1,0:T(8,128)S(1)}) custom-call(s32[1]{0:T(128)} %bitcast.2.me_ref, f32[48,128]{1,0:T(8,128)S(1)} %get-tuple-element.18.refs_0_, f32[48,128]{1,0:T(8,128)S(1)} %collective-permute-done.refs_1_, f32[48,128]{1,0:T(8,128)S(1)} %collective-permute-done.1.refs_2_, ...), custom_call_target="tpu_custom_call" | custom-call | flops 2415919104 | bytes 30000000 | tf_op jit(solution)/shard_map/later_frames/pallas_call | solution.py:387
  107.1 0.0 collective-permute-done.3.tail_ref
  107.2 2.4 %first_frame.1 = bf16[64,8,128]{2,1,0:T(8,128)(2,1)S(1)} custom-call(bf16[8,4,2,2,16,384]{5,4,3,2,1,0:T(8,128)(2,1)S(1)} %bitcast.28, bf16[3,1,2,2,16,384]{5,4,3,2,1,0:T(8,128)(2,1)S(1)} %collective-permute-done.3.tail_ref, f32[4,48,128]{2,1,0:T(8,128)S(1)} %get-tuple-element.7.sorted_ref, f32[2,512,128]{2,1,0:T(8,128)S(1)} %maximum_multiply_fusion.refs_5_.chirp_ref, ...), custom_call_target="tpu_custom_call" | custom-call | flops 805306368 | bytes 10000000 | tf_op jit(solution)/shard_map/first_frame/pallas_call | solution.py:405
  109.5 18.2 %all_to_all.10 = bf16[64,8,128]{2,1,0:T(8,128)(2,1)S(1)} all-to-all(bf16[64,8,128]{2,1,0:T(8,128)(2,1)S(1)} %first_frame.1), channel_id=1, replica_groups=mesh['xy'=16,'zl'=4,'chan'=8] {'zl','xy'}, dimensions={0} | all-to-all | bytes 262144 | tf_op jit(solution)/shard_map/all_to_all | solution.py:487
  127.7 0.7 last_sum.1
  (13 shorter events, 0.2 us)
Async XLA Ops:
  2.2 15.7 %copy-start.2 = (s32[3072]{0:T(1024)S(1)}, s32[3072]{0:T(1024)}, u32[]{:S(2)}) copy-start(s32[3072]{0:T(1024)} %param.11) | copy-start | bytes 36868
  2.2 16.0 %copy-start.3 = (f32[64,12]{0,1:T(8,128)S(1)}, f32[64,12]{0,1:T(8,128)}, u32[]{:S(2)}) copy-start(f32[64,12]{0,1:T(8,128)} %param.8) | copy-start | bytes 9220
  2.3 16.1 %copy-start.4 = (s32[64,12]{0,1:T(8,128)S(1)}, s32[64,12]{0,1:T(8,128)}, u32[]{:S(2)}) copy-start(s32[64,12]{0,1:T(8,128)} %param.9) | copy-start | bytes 9220
  2.3 27.7 %copy-start.5 = (f32[64]{0:T(128)S(1)}, f32[64]{0:T(128)}, u32[]{:S(2)}) copy-start(f32[64]{0:T(128)} %param.10) | copy-start | bytes 772
  2.3 94.4 %all-to-all-start = ((bf16[32,2,2,16,384]{4,3,2,1,0:T(8,128)(2,1)}), bf16[32,2,2,16,384]{4,3,2,1,0:T(8,128)(2,1)S(1)}, u32[]{:S(2)}, u32[]{:S(2)}) async-start(bf16[32,2,2,16,384]{4,3,2,1,0:T(8,128)(2,1)} %spread.1), calls=%async_computation | async-start | bytes 3145728 | tf_op jit(solution)/shard_map/all_to_all | solution.py:466
  18.7 69.3 %collective-permute-start = (f32[48,128]{1,0:T(8,128)S(1)}, f32[48,128]{1,0:T(8,128)S(1)}, u32[]{:S(2)}, u32[]{:S(2)}) collective-permute-start(f32[48,128]{1,0:T(8,128)S(1)} %get-tuple-element.16), channel_id=1, source_target_pairs={{0,8},{8,16},{16,24},{24,0},{1,9},{9,17},{17,25},{25,1},{2,10},{10... | collective-permute-start | bytes 73736 | tf_op jit(solution)/shard_map/ppermute | solution.py:436
  22.4 65.6 %collective-permute-start.1 = (f32[48,128]{1,0:T(8,128)S(1)}, f32[48,128]{1,0:T(8,128)S(1)}, u32[]{:S(2)}, u32[]{:S(2)}) collective-permute-start(f32[48,128]{1,0:T(8,128)S(1)} %get-tuple-element.17), channel_id=1, source_target_pairs={{0,16},{8,24},{16,0},{24,8},{1,17},{9,25},{17,1},{25,9},{2,18},{10... | collective-permute-start | bytes 73736 | tf_op jit(solution)/shard_map/ppermute | solution.py:436
  26.6 62.1 %collective-permute-start.2 = (f32[48,128]{1,0:T(8,128)S(1)}, f32[48,128]{1,0:T(8,128)S(1)}, u32[]{:S(2)}, u32[]{:S(2)}) collective-permute-start(f32[48,128]{1,0:T(8,128)S(1)} %get-tuple-element.15), channel_id=1, source_target_pairs={{0,24},{8,0},{16,8},{24,16},{1,25},{9,1},{17,9},{25,17},{2,26},{10... | collective-permute-start | bytes 73736 | tf_op jit(solution)/shard_map/ppermute | solution.py:436
  96.7 3.7 %copy-start = (bf16[2,256,256]{2,1,0:T(8,128)(2,1)S(1)}, bf16[2,256,256]{2,1,0:T(8,128)(2,1)}, u32[]{:S(2)}) copy-start(bf16[2,256,256]{2,1,0:T(8,128)(2,1)} %constant.90.clone.refs_7_.table_ref) | copy-start | bytes 786436
  96.7 3.7 %copy-start.1 = (f32[2,32,128]{2,1,0:T(8,128)S(1)}, f32[2,32,128]{2,1,0:T(8,128)}, u32[]{:S(2)}) copy-start(f32[2,32,128]{2,1,0:T(8,128)} %constant.89.clone.refs_6_.twist_ref) | copy-start | bytes 98308
  96.7 10.4 %collective-permute-start.3 = (bf16[3,1,2,2,16,384]{5,4,3,2,1,0:T(8,128)(2,1)S(1)}, bf16[3,1,2,2,16,384]{5,4,3,2,1,0:T(8,128)(2,1)S(1)}, u32[]{:S(2)}, u32[]{:S(2)}) collective-permute-start(bf16[3,1,2,2,16,384]{5,4,3,2,1,0:T(8,128)(2,1)S(1)} %tail_message.1), channel_id=1, source_target_pairs={{0,32},{32,64},{64,96},{96,128},{128,160},{160,192},{192,224},{224... | collective-permute-start | bytes 442376 | tf_op jit(solution)/shard_map/ppermute | solution.py:441

commit v7 on v6

--- a/solution.py
+++ b/solution.py
@@ -175,7 +175,7 @@
             cross_im = xi * yr - xr * yi
             row = na + 8 * (nb - 1)
             lanes = pl.ds(LANES * (row % 2), LANES)
-            for s, value in enumerate((power_x + power_y, power_x - power_y, 2.0 * cross_re, 2.0 * cross_im)):
+            for s, value in enumerate((power_x + power_y, power_x - power_y, cross_re, cross_im)):
                 stokes_ref[row // 2, pl.ds(GROUP * s, GROUP), lanes] = value.astype(jnp.bfloat16)
 
     bins = lax.broadcasted_iota(jnp.int32, (WINDOW, BLK), 0).astype(jnp.bfloat16)
@@ -308,9 +308,7 @@
     acc[:WINDOW] += acc[NBIN:]
     for share in range(NBIN // 16):
         place = share % RUNS * (NBIN // 16 // RUNS) + share // RUNS
-        out_ref[place] = jnp.concatenate([acc[16 * share : 16 * share + 8], acc[16 * share + 8 : 16 * share + 16]], axis=1).astype(
-            out_ref.dtype
-        )
+        out_ref[place] = jnp.concatenate([acc[16 * share : 16 * share + 8], acc[16 * share + 8 : 16 * share + 16]], axis=1)
 
 
 def tail_kernel(me_ref, *refs):
@@ -404,7 +402,7 @@
     block = (MEMBERS, 1) + buf.shape[2:]
     return pl.pallas_call(
         first_kernel,
-        out_shape=jax.ShapeDtypeStruct((NBIN // 16, 8, LANES), jnp.bfloat16),
+        out_shape=jax.ShapeDtypeStruct((NBIN // 16, 8, LANES), jnp.float32),
         grid=(1,),
         in_specs=[pl.BlockSpec(block, lambda i: (0,) * 6)] + [whole()] * 6,
         out_specs=whole(),
@@ -421,11 +419,12 @@
 
 
 def last_kernel(scale, shares_ref, out_ref):
-    total = [jnp.sum(shares_ref[slab].astype(jnp.float32), axis=0) * scale for slab in range(RUNS)]
+    total = [jnp.sum(shares_ref[slab], axis=0) * scale for slab in range(RUNS)]
     for half in range(2):
         for s in range(4):
             lanes = slice(64 * half + GROUP * s, 64 * half + GROUP * (s + 1))
-            out_ref[pl.ds(32 * half + s, 8, stride=4)] = jnp.concatenate([part[:, lanes] for part in total], axis=1)
+            row = jnp.concatenate([part[:, lanes] for part in total], axis=1)
+            out_ref[pl.ds(32 * half + s, 8, stride=4)] = row if s < 2 else 2.0 * row
 
 
 def turned_to(block_for, axis, turn):

time: 129 us -> 130 us (level)
  no operation moved by 1% of the time
where the time goes in v7:
time: 130 us; the launch traced here: 129 us
  waiting for transfers between devices  65.2 us (50%)
  starting transfers between devices  30.6 us (24%)
  blocking collectives  19.2 us (15%)
  Pallas kernels  12.1 us (9%)
  other arithmetic  1.56 us (1%)
    ppermute x3, waiting for transfers between devices, turned_to(): lax.ppermute(block_for(there), axis, [(i, (i + turn) % size) for i in ran...  57.3 us
    all_to_all x1, blocking collectives, on_device(): lax.all_to_all(partial, ('zl', 'xy'), split_axis=0, concat_axis=0, tiled=...  19.2 us
    all_to_all x1, starting transfers between devices, on_device(): lax.all_to_all(parts, ('chan', 'zl'), split_axis=0, concat_axis=0, tiled=...  15.6 us
    ppermute x3, starting transfers between devices, turned_to(): lax.ppermute(block_for(there), axis, [(i, (i + turn) % size) for i in ran...  11.3 us
    all_to_all x1, waiting for transfers between devices, on_device(): lax.all_to_all(parts, ('chan', 'zl'), split_axis=0, concat_axis=0, tiled=...  7.93 us
    pallas_call x1, Pallas kernels, fold_frames(): pl.pallas_call(later_kernel, out_shape=[jax.ShapeDtypeStruct((ACC_ROWS, 4...  6.75 us
    ppermute x1, starting transfers between devices, from_before(): return lax.ppermute(block, 'xy', [(i, i + 1) for i in range(size - 1)])  3.62 us
  transfers between devices with their start and end apart: 5, of which 3 were waited for; matrix products, arithmetic and copies ran while one was open for 2% of the time, Pallas kernels for 5%

profile of v7, /device:TPU:8, one launch (start us, length us, event | category | flops | bytes accessed | tf_op | source)
XLA Modules:
  0.0 129.4 jit_solution(946389033348912946)
XLA Ops:
  0.0 2.2 %spread.1 = bf16[32,2,2,16,384]{4,3,2,1,0:T(8,128)(2,1)} custom-call(bf16[2,2,32,16,384]{4,3,2,1,0:T(8,128)(2,1)} %bitcast.30), custom_call_target="tpu_custom_call" | custom-call | tf_op jit(solution)/shard_map/spread/pallas_call | solution.py:452
  2.2 0.0 copy-start.2
  2.2 0.0 copy-start.3
  2.3 0.0 copy-start.4
  2.3 0.0 copy-start.5
  2.3 15.6 %all-to-all-start = ((bf16[32,2,2,16,384]{4,3,2,1,0:T(8,128)(2,1)}), bf16[32,2,2,16,384]{4,3,2,1,0:T(8,128)(2,1)S(1)}, u32[]{:S(2)}, u32[]{:S(2)}) async-start(bf16[32,2,2,16,384]{4,3,2,1,0:T(8,128)(2,1)} %spread.1), calls=%async_computation | async-start | bytes 3145728 | tf_op jit(solution)/shard_map/all_to_all | solution.py:465
  18.0 0.0 copy-done.2
  18.0 0.1 reduce
  18.1 0.1 broadcast_in_dim.2
  18.2 0.1 sub.29
  18.3 0.0 copy-done.3
  18.3 0.1 copy.14
  18.4 0.0 copy-done.4
  18.4 0.1 copy.13
  18.5 0.1 add_select_fusion
  18.7 3.7 %collective-permute-start = (f32[48,128]{1,0:T(8,128)S(1)}, f32[48,128]{1,0:T(8,128)S(1)}, u32[]{:S(2)}, u32[]{:S(2)}) collective-permute-start(f32[48,128]{1,0:T(8,128)S(1)} %get-tuple-element.16), channel_id=1, source_target_pairs={{0,8},{8,16},{16,24},{24,0},{1,9},{9,17},{17,25},{25,1},{2,10},{10... | collective-permute-start | bytes 73736 | tf_op jit(solution)/shard_map/ppermute | solution.py:435
  22.4 4.3 %collective-permute-start.1 = (f32[48,128]{1,0:T(8,128)S(1)}, f32[48,128]{1,0:T(8,128)S(1)}, u32[]{:S(2)}, u32[]{:S(2)}) collective-permute-start(f32[48,128]{1,0:T(8,128)S(1)} %get-tuple-element.17), channel_id=1, source_target_pairs={{0,16},{8,24},{16,0},{24,8},{1,17},{9,25},{17,1},{25,9},{2,18},{10... | collective-permute-start | bytes 73736 | tf_op jit(solution)/shard_map/ppermute | solution.py:435
  26.6 3.4 %collective-permute-start.2 = (f32[48,128]{1,0:T(8,128)S(1)}, f32[48,128]{1,0:T(8,128)S(1)}, u32[]{:S(2)}, u32[]{:S(2)}) collective-permute-start(f32[48,128]{1,0:T(8,128)S(1)} %get-tuple-element.15), channel_id=1, source_target_pairs={{0,24},{8,0},{16,8},{24,16},{1,25},{9,1},{17,9},{25,17},{2,26},{10... | collective-permute-start | bytes 73736 | tf_op jit(solution)/shard_map/ppermute | solution.py:435
  30.0 0.0 copy-done.5
  30.0 0.1 dynamic-slice_multiply_fusion
  30.1 0.1 mul.100
  30.2 1.2 fusion.1
  31.5 56.5 %collective-permute-done.refs_1_ = f32[48,128]{1,0:T(8,128)S(1)} collective-permute-done((f32[48,128]{1,0:T(8,128)S(1)}, f32[48,128]{1,0:T(8,128)S(1)}, u32[]{:S(2)}, u32[]{:S(2)}) %collective-permute-start) | collective-permute-done | bytes 24608 | tf_op jit(solution)/shard_map/ppermute | solution.py:435
  88.0 0.0 collective-permute-done.1.refs_2_
  88.0 0.7 collective-permute-done.2.refs_3_
  88.7 7.9 %all-to-all-done = bf16[32,2,2,16,384]{4,3,2,1,0:T(8,128)(2,1)S(1)} async-done(((bf16[32,2,2,16,384]{4,3,2,1,0:T(8,128)(2,1)}), bf16[32,2,2,16,384]{4,3,2,1,0:T(8,128)(2,1)S(1)}, u32[]{:S(2)}, u32[]{:S(2)}) %all-to-all-start) | async-done | bytes 1572896 | tf_op jit(solution)/shard_map/all_to_all | solution.py:465
  96.7 0.0 copy-start
  96.7 0.0 copy-start.1
  96.7 3.6 %collective-permute-start.3 = (bf16[3,1,2,2,16,384]{5,4,3,2,1,0:T(8,128)(2,1)S(1)}, bf16[3,1,2,2,16,384]{5,4,3,2,1,0:T(8,128)(2,1)S(1)}, u32[]{:S(2)}, u32[]{:S(2)}) collective-permute-start(bf16[3,1,2,2,16,384]{5,4,3,2,1,0:T(8,128)(2,1)S(1)} %tail_message.1), channel_id=1, source_target_pairs={{0,32},{32,64},{64,96},{96,128},{128,160},{160,192},{192,224},{224... | collective-permute-start | bytes 442376 | tf_op jit(solution)/shard_map/ppermute | solution.py:440
  100.3 0.0 copy-done
  100.3 0.0 copy-done.1
  100.3 6.7 %later_frames.1 = (f32[1168,64]{1,0:T(8,128)S(1)}, f32[4,48,128]{2,1,0:T(8,128)S(1)}) custom-call(s32[1]{0:T(128)} %bitcast.2.me_ref, f32[48,128]{1,0:T(8,128)S(1)} %get-tuple-element.18.refs_0_, f32[48,128]{1,0:T(8,128)S(1)} %collective-permute-done.refs_1_, f32[48,128]{1,0:T(8,128)S(1)} %collective-permute-done.1.refs_2_, ...), custom_call_target="tpu_custom_call" | custom-call | flops 2415919104 | bytes 30000000 | tf_op jit(solution)/shard_map/later_frames/pallas_call | solution.py:385
  107.1 0.0 collective-permute-done.3.tail_ref
  107.1 2.4 %first_frame.1 = f32[64,8,128]{2,1,0:T(8,128)S(1)} custom-call(bf16[8,4,2,2,16,384]{5,4,3,2,1,0:T(8,128)(2,1)S(1)} %bitcast.28, bf16[3,1,2,2,16,384]{5,4,3,2,1,0:T(8,128)(2,1)S(1)} %collective-permute-done.3.tail_ref, f32[4,48,128]{2,1,0:T(8,128)S(1)} %get-tuple-element.7.sorted_ref, f32[2,512,128]{2,1,0:T(8,128)S(1)} %maximum_multiply_fusion.refs_5_.chirp_ref, ...), custom_call_target="tpu_custom_call" | custom-call | flops 805306368 | bytes 10000000 | tf_op jit(solution)/shard_map/first_frame/pallas_call | solution.py:403
  109.5 19.2 %all_to_all.10 = f32[64,8,128]{2,1,0:T(8,128)S(1)} all-to-all(f32[64,8,128]{2,1,0:T(8,128)S(1)} %first_frame.1), channel_id=1, replica_groups=mesh['xy'=16,'zl'=4,'chan'=8] {'zl','xy'}, dimensions={0} | all-to-all | bytes 524288 | tf_op jit(solution)/shard_map/all_to_all | solution.py:486
  128.7 0.7 last_sum.1
  (13 shorter events, 0.2 us)
Async XLA Ops:
  2.2 15.7 %copy-start.2 = (s32[3072]{0:T(1024)S(1)}, s32[3072]{0:T(1024)}, u32[]{:S(2)}) copy-start(s32[3072]{0:T(1024)} %param.11) | copy-start | bytes 36868
  2.2 16.0 %copy-start.3 = (f32[64,12]{0,1:T(8,128)S(1)}, f32[64,12]{0,1:T(8,128)}, u32[]{:S(2)}) copy-start(f32[64,12]{0,1:T(8,128)} %param.8) | copy-start | bytes 9220
  2.3 16.1 %copy-start.4 = (s32[64,12]{0,1:T(8,128)S(1)}, s32[64,12]{0,1:T(8,128)}, u32[]{:S(2)}) copy-start(s32[64,12]{0,1:T(8,128)} %param.9) | copy-start | bytes 9220
  2.3 27.7 %copy-start.5 = (f32[64]{0:T(128)S(1)}, f32[64]{0:T(128)}, u32[]{:S(2)}) copy-start(f32[64]{0:T(128)} %param.10) | copy-start | bytes 772
  2.3 94.4 %all-to-all-start = ((bf16[32,2,2,16,384]{4,3,2,1,0:T(8,128)(2,1)}), bf16[32,2,2,16,384]{4,3,2,1,0:T(8,128)(2,1)S(1)}, u32[]{:S(2)}, u32[]{:S(2)}) async-start(bf16[32,2,2,16,384]{4,3,2,1,0:T(8,128)(2,1)} %spread.1), calls=%async_computation | async-start | bytes 3145728 | tf_op jit(solution)/shard_map/all_to_all | solution.py:465
  18.7 69.3 %collective-permute-start = (f32[48,128]{1,0:T(8,128)S(1)}, f32[48,128]{1,0:T(8,128)S(1)}, u32[]{:S(2)}, u32[]{:S(2)}) collective-permute-start(f32[48,128]{1,0:T(8,128)S(1)} %get-tuple-element.16), channel_id=1, source_target_pairs={{0,8},{8,16},{16,24},{24,0},{1,9},{9,17},{17,25},{25,1},{2,10},{10... | collective-permute-start | bytes 73736 | tf_op jit(solution)/shard_map/ppermute | solution.py:435
  22.4 65.6 %collective-permute-start.1 = (f32[48,128]{1,0:T(8,128)S(1)}, f32[48,128]{1,0:T(8,128)S(1)}, u32[]{:S(2)}, u32[]{:S(2)}) collective-permute-start(f32[48,128]{1,0:T(8,128)S(1)} %get-tuple-element.17), channel_id=1, source_target_pairs={{0,16},{8,24},{16,0},{24,8},{1,17},{9,25},{17,1},{25,9},{2,18},{10... | collective-permute-start | bytes 73736 | tf_op jit(solution)/shard_map/ppermute | solution.py:435
  26.6 62.1 %collective-permute-start.2 = (f32[48,128]{1,0:T(8,128)S(1)}, f32[48,128]{1,0:T(8,128)S(1)}, u32[]{:S(2)}, u32[]{:S(2)}) collective-permute-start(f32[48,128]{1,0:T(8,128)S(1)} %get-tuple-element.15), channel_id=1, source_target_pairs={{0,24},{8,0},{16,8},{24,16},{1,25},{9,1},{17,9},{25,17},{2,26},{10... | collective-permute-start | bytes 73736 | tf_op jit(solution)/shard_map/ppermute | solution.py:435
  96.7 3.7 %copy-start = (bf16[2,256,256]{2,1,0:T(8,128)(2,1)S(1)}, bf16[2,256,256]{2,1,0:T(8,128)(2,1)}, u32[]{:S(2)}) copy-start(bf16[2,256,256]{2,1,0:T(8,128)(2,1)} %constant.90.clone.refs_7_.table_ref) | copy-start | bytes 786436
  96.7 3.7 %copy-start.1 = (f32[2,32,128]{2,1,0:T(8,128)S(1)}, f32[2,32,128]{2,1,0:T(8,128)}, u32[]{:S(2)}) copy-start(f32[2,32,128]{2,1,0:T(8,128)} %constant.89.clone.refs_6_.twist_ref) | copy-start | bytes 98308
  96.7 10.4 %collective-permute-start.3 = (bf16[3,1,2,2,16,384]{5,4,3,2,1,0:T(8,128)(2,1)S(1)}, bf16[3,1,2,2,16,384]{5,4,3,2,1,0:T(8,128)(2,1)S(1)}, u32[]{:S(2)}, u32[]{:S(2)}) collective-permute-start(bf16[3,1,2,2,16,384]{5,4,3,2,1,0:T(8,128)(2,1)S(1)} %tail_message.1), channel_id=1, source_target_pairs={{0,32},{32,64},{64,96},{96,128},{128,160},{160,192},{192,224},{224... | collective-permute-start | bytes 442376 | tf_op jit(solution)/shard_map/ppermute | solution.py:440

commit v8 on v7

--- a/solution.py
+++ b/solution.py
@@ -28,6 +28,7 @@
 DOT_ROWS = 256
 BASE_ROW = GROUP + KEPT
 LETTER_ROWS = BASE_ROW + 8
+PARTS_APART = 16
 HALF_ROOT = math.sqrt(0.5)
 
 
@@ -224,6 +225,20 @@
     return buf_ref[row // 3, slab, pol, part, :, pl.ds(LANES * (row % 3), LANES)]
 
 
+def in_parts(weight):
+    high = lax.reduce_precision(weight, 8, 7)
+    middle = lax.reduce_precision(weight - high, 8, 7)
+    parts = [high, middle, weight - high - middle]
+    width = PARTS_APART - weight.shape[1]
+    side_by_side = jnp.concatenate([jnp.pad(part, ((0, 0), (0, width))) for part in parts], axis=1)
+    return jnp.pad(side_by_side, ((0, 0), (0, LANES - 3 * PARTS_APART))).astype(jnp.bfloat16)
+
+
+def joined(rows):
+    first, second, third = (rows[:, PARTS_APART * part : PARTS_APART * (part + 1)] for part in range(3))
+    return (first + second) + third
+
+
 def lay_gains(gains, weights_of):
     for block in range(ROWS // 2):
         gains[block] = jnp.broadcast_to(weights_of(block), (GROUP, LANES))
@@ -238,7 +253,9 @@
     buf_ref, chirp_ref, twist_ref, table_ref, acc_ref, sorted_ref, gains, marks, *scratches = refs
     me = me_ref[0]
     for turn in range(RUNS):
-        sorted_ref[(me - turn + RUNS) % RUNS] = letter_refs[turn][...]
+        slab = (me - turn + RUNS) % RUNS
+        sorted_ref[slab] = letter_refs[turn][...].astype(jnp.float32)
+        sorted_ref[slab, :GROUP, :PARTS_APART] = joined(sorted_ref[slab, :GROUP])
     marks[...] = sorted_ref[:, GROUP : GROUP + KEPT].astype(jnp.int32)
     acc_ref[...] = jnp.zeros_like(acc_ref)
 
@@ -256,7 +273,7 @@
             return own[:, block - RIM // 2 : block - RIM // 2 + 1]
 
         lay_gains(gains, weights_of)
-        bases = sorted_ref[frame, BASE_ROW : BASE_ROW + 1].astype(jnp.int32)
+        bases = 8 * sorted_ref[frame, BASE_ROW : BASE_ROW + 1].astype(jnp.int32)
         frame_profile(
             row_of,
             lambda block: gains[block],
@@ -277,8 +294,7 @@
     buf_ref, tail_ref, sorted_ref, chirp_ref, twist_ref, table_ref, given_ref, out_ref, acc, gains, marks, *scratches
 ):
     acc[...] = given_ref[...]
-    high, middle, low = (tail_ref[0, 0, part // 2, part % 2, :, :LANES].astype(jnp.float32) for part in range(3))
-    before = (high + middle) + low
+    before = joined(tail_ref[0, 0, 0, 0, :, :LANES].astype(jnp.float32))
     own = sorted_ref[0, :GROUP]
     marks[0] = sorted_ref[0, GROUP : GROUP + KEPT].astype(jnp.int32)
 
@@ -293,7 +309,7 @@
         return own_row(buf_ref, 0, row - RIM, pol, part)
 
     lay_gains(gains, weights_of)
-    bases = sorted_ref[0, BASE_ROW : BASE_ROW + 1].astype(jnp.int32)
+    bases = 8 * sorted_ref[0, BASE_ROW : BASE_ROW + 1].astype(jnp.int32)
     frame_profile(
         row_of,
         lambda block: gains[block],
@@ -316,13 +332,9 @@
     me = me_ref[0]
     for turn in range(RUNS):
         sorted_ref[(me - turn + RUNS) % RUNS] = letter_refs[turn][:GROUP]
-    rest = sorted_ref[RUNS - 1]
     for index, piece in enumerate(piece_refs):
         out_ref[index] = piece[0]
-    for part in range(3):
-        rounded = rest.astype(jnp.bfloat16)
-        out_ref[0, 0, part // 2, part % 2, :, :LANES] = rounded
-        rest = rest - rounded.astype(jnp.float32)
+    out_ref[0, 0, 0, 0, :, :LANES] = sorted_ref[RUNS - 1]
 
 
 def spread_kernel(samples_ref, out_ref, held, in_sems, out_sems):
@@ -370,7 +382,7 @@
         + [whole()] * RUNS
         + [pl.BlockSpec(block, lambda i, at=first + at: (at, RUNS - 1, 0, 0, 0, 0)) for at in range(3)],
         out_specs=whole(),
-        scratch_shapes=[pltpu.VMEM((RUNS, GROUP, LANES), jnp.float32)],
+        scratch_shapes=[pltpu.VMEM((RUNS, GROUP, LANES), jnp.bfloat16)],
         compiler_params=small_kernel(),
         name="tail_message",
     )(me, *letters, buf, buf, buf)
@@ -467,7 +479,7 @@
 
     me = lax.axis_index("zl")
     weight = scales * (1 - flags).astype(jnp.float32)
-    weight = jnp.pad(weight, ((0, 0), (0, LANES - BLOCKS)))
+    weight = in_parts(weight)
     bins = phase_bin.reshape(KEPT, LANES)
     base = bins[::2, 0] // 8 * 8
     marks = (bins - jnp.repeat(base, 2)[:, None]) % NBIN
@@ -475,8 +487,8 @@
     def weights_for(place):
         return lax.dynamic_slice_in_dim(weight, place * GROUP, GROUP, 0)
 
-    base_rows = jnp.pad(base[None, :], ((0, LETTER_ROWS - BASE_ROW - 1), (0, LANES - BLOCKS)))
-    below = jnp.concatenate([marks, base_rows]).astype(jnp.float32)
+    base_rows = jnp.pad(base[None, :] // 8, ((0, LETTER_ROWS - BASE_ROW - 1), (0, LANES - BLOCKS)))
+    below = jnp.concatenate([marks, base_rows]).astype(jnp.bfloat16)
     letters = [
         turned_to(lambda place: jnp.concatenate([weights_for(place), below]), "zl", turn) for turn in range(RUNS)
     ]

time: 130 us -> 130 us (level)
  no operation moved by 1% of the time
where the time goes in v8:
time: 130 us; the launch traced here: 129 us
  waiting for transfers between devices  64.6 us (50%)
  starting transfers between devices  30.6 us (24%)
  blocking collectives  19.6 us (15%)
  Pallas kernels  12.2 us (9%)
  other arithmetic  1.66 us (1%)
    ppermute x3, waiting for transfers between devices, turned_to(): lax.ppermute(block_for(there), axis, [(i, (i + turn) % size) for i in ran...  56.2 us
    all_to_all x1, blocking collectives, on_device(): lax.all_to_all(partial, ('zl', 'xy'), split_axis=0, concat_axis=0, tiled=...  19.6 us
    all_to_all x1, starting transfers between devices, on_device(): lax.all_to_all(parts, ('chan', 'zl'), split_axis=0, concat_axis=0, tiled=...  15.6 us
    ppermute x3, starting transfers between devices, turned_to(): lax.ppermute(block_for(there), axis, [(i, (i + turn) % size) for i in ran...  11.3 us
    all_to_all x1, waiting for transfers between devices, on_device(): lax.all_to_all(parts, ('chan', 'zl'), split_axis=0, concat_axis=0, tiled=...  8.4 us
    pallas_call x1, Pallas kernels, fold_frames(): pl.pallas_call(later_kernel, out_shape=[jax.ShapeDtypeStruct((ACC_ROWS, 4...  6.79 us
    ppermute x1, starting transfers between devices, from_before(): return lax.ppermute(block, 'xy', [(i, i + 1) for i in range(size - 1)])  3.62 us
  transfers between devices with their start and end apart: 5, of which 3 were waited for; matrix products, arithmetic and copies ran while one was open for 2% of the time, Pallas kernels for 5%

profile of v8, /device:TPU:8, one launch (start us, length us, event | category | flops | bytes accessed | tf_op | source)
XLA Modules:
  0.0 129.4 jit_solution(6658454843838395087)
XLA Ops:
  0.0 2.3 %spread.1 = bf16[32,2,2,16,384]{4,3,2,1,0:T(8,128)(2,1)} custom-call(bf16[2,2,32,16,384]{4,3,2,1,0:T(8,128)(2,1)} %bitcast.30), custom_call_target="tpu_custom_call" | custom-call | tf_op jit(solution)/shard_map/spread/pallas_call | solution.py:464
  2.3 0.0 copy-start.2
  2.3 0.0 copy-start.3
  2.3 0.0 copy-start.4
  2.3 0.0 copy-start.5
  2.3 15.6 %all-to-all-start = ((bf16[32,2,2,16,384]{4,3,2,1,0:T(8,128)(2,1)}), bf16[32,2,2,16,384]{4,3,2,1,0:T(8,128)(2,1)S(1)}, u32[]{:S(2)}, u32[]{:S(2)}) async-start(bf16[32,2,2,16,384]{4,3,2,1,0:T(8,128)(2,1)} %spread.1), calls=%async_computation | async-start | bytes 3145728 | tf_op jit(solution)/shard_map/all_to_all | solution.py:477
  18.0 0.0 copy-done.2
  18.0 0.1 reduce
  18.2 0.1 broadcast_in_dim.2
  18.2 0.1 sub.42
  18.3 0.0 copy-done.3
  18.3 0.1 copy.14
  18.4 0.0 copy-done.4
  18.4 0.1 copy.13
  18.5 0.1 fusion.9
  18.7 0.1 fusion.17
  18.8 3.7 %collective-permute-start = (bf16[48,128]{1,0:T(8,128)(2,1)S(1)}, bf16[48,128]{1,0:T(8,128)(2,1)S(1)}, u32[]{:S(2)}, u32[]{:S(2)}) collective-permute-start(bf16[48,128]{1,0:T(8,128)(2,1)S(1)} %get-tuple-element.19), channel_id=1, source_target_pairs={{0,8},{8,16},{16,24},{24,0},{1,9},{9,17},{17,25},{25,1},{2,10},{10... | collective-permute-start | bytes 36872 | tf_op jit(solution)/shard_map/ppermute | solution.py:447
  22.5 4.3 %collective-permute-start.1 = (bf16[48,128]{1,0:T(8,128)(2,1)S(1)}, bf16[48,128]{1,0:T(8,128)(2,1)S(1)}, u32[]{:S(2)}, u32[]{:S(2)}) collective-permute-start(bf16[48,128]{1,0:T(8,128)(2,1)S(1)} %get-tuple-element.20), channel_id=1, source_target_pairs={{0,16},{8,24},{16,0},{24,8},{1,17},{9,25},{17,1},{25,9},{2,18},{10... | collective-permute-start | bytes 36872 | tf_op jit(solution)/shard_map/ppermute | solution.py:447
  26.8 3.4 %collective-permute-start.2 = (bf16[48,128]{1,0:T(8,128)(2,1)S(1)}, bf16[48,128]{1,0:T(8,128)(2,1)S(1)}, u32[]{:S(2)}, u32[]{:S(2)}) collective-permute-start(bf16[48,128]{1,0:T(8,128)(2,1)S(1)} %get-tuple-element.18), channel_id=1, source_target_pairs={{0,24},{8,0},{16,8},{24,16},{1,25},{9,1},{17,9},{25,17},{2,26},{10... | collective-permute-start | bytes 36872 | tf_op jit(solution)/shard_map/ppermute | solution.py:447
  30.1 0.0 copy-done.5
  30.2 0.1 dynamic-slice_multiply_fusion
  30.2 0.1 mul.100
  30.4 1.2 fusion.1
  31.6 55.8 %collective-permute-done.refs_1_ = bf16[48,128]{1,0:T(8,128)(2,1)S(1)} collective-permute-done((bf16[48,128]{1,0:T(8,128)(2,1)S(1)}, bf16[48,128]{1,0:T(8,128)(2,1)S(1)}, u32[]{:S(2)}, u32[]{:S(2)}) %collective-permute-start) | collective-permute-done | bytes 12320 | tf_op jit(solution)/shard_map/ppermute | solution.py:447
  87.4 0.0 collective-permute-done.1.refs_2_
  87.4 0.4 collective-permute-done.2.refs_3_
  87.8 8.4 %all-to-all-done = bf16[32,2,2,16,384]{4,3,2,1,0:T(8,128)(2,1)S(1)} async-done(((bf16[32,2,2,16,384]{4,3,2,1,0:T(8,128)(2,1)}), bf16[32,2,2,16,384]{4,3,2,1,0:T(8,128)(2,1)S(1)}, u32[]{:S(2)}, u32[]{:S(2)}) %all-to-all-start) | async-done | bytes 1572896 | tf_op jit(solution)/shard_map/all_to_all | solution.py:477
  96.2 0.0 copy-start
  96.2 0.0 copy-start.1
  96.2 3.6 %collective-permute-start.3 = (bf16[3,1,2,2,16,384]{5,4,3,2,1,0:T(8,128)(2,1)S(1)}, bf16[3,1,2,2,16,384]{5,4,3,2,1,0:T(8,128)(2,1)S(1)}, u32[]{:S(2)}, u32[]{:S(2)}) collective-permute-start(bf16[3,1,2,2,16,384]{5,4,3,2,1,0:T(8,128)(2,1)S(1)} %tail_message.1), channel_id=1, source_target_pairs={{0,32},{32,64},{64,96},{96,128},{128,160},{160,192},{192,224},{224... | collective-permute-start | bytes 442376 | tf_op jit(solution)/shard_map/ppermute | solution.py:452
  99.8 0.0 copy-done
  99.8 0.0 copy-done.1
  99.8 6.8 %later_frames.1 = (f32[1168,64]{1,0:T(8,128)S(1)}, f32[4,48,128]{2,1,0:T(8,128)S(1)}) custom-call(s32[1]{0:T(128)} %bitcast.2.me_ref, bf16[48,128]{1,0:T(8,128)(2,1)S(1)} %get-tuple-element.21.refs_0_, bf16[48,128]{1,0:T(8,128)(2,1)S(1)} %collective-permute-done.refs_1_, bf16[48,128]{1,0:T(8,128)(2,1)S(1)} %collective-permute-done.1.refs_2_, ...), custom_call_target="tpu_custom_call" | custom-call | flops 2415919104 | bytes 30000000 | tf_op jit(solution)/shard_map/later_frames/pallas_call | solution.py:397
  106.6 0.0 collective-permute-done.3.tail_ref
  106.7 2.4 %first_frame.1 = f32[64,8,128]{2,1,0:T(8,128)S(1)} custom-call(bf16[8,4,2,2,16,384]{5,4,3,2,1,0:T(8,128)(2,1)S(1)} %bitcast.28, bf16[3,1,2,2,16,384]{5,4,3,2,1,0:T(8,128)(2,1)S(1)} %collective-permute-done.3.tail_ref, f32[4,48,128]{2,1,0:T(8,128)S(1)} %get-tuple-element.7.sorted_ref, f32[2,512,128]{2,1,0:T(8,128)S(1)} %maximum_multiply_fusion.refs_5_.chirp_ref, ...), custom_call_target="tpu_custom_call" | custom-call | flops 805306368 | bytes 10000000 | tf_op jit(solution)/shard_map/first_frame/pallas_call | solution.py:415
  109.1 19.6 %all_to_all.10 = f32[64,8,128]{2,1,0:T(8,128)S(1)} all-to-all(f32[64,8,128]{2,1,0:T(8,128)S(1)} %first_frame.1), channel_id=1, replica_groups=mesh['xy'=16,'zl'=4,'chan'=8] {'zl','xy'}, dimensions={0} | all-to-all | bytes 524288 | tf_op jit(solution)/shard_map/all_to_all | solution.py:498
  128.6 0.7 last_sum.1
  (12 shorter events, 0.2 us)
Async XLA Ops:
  2.3 15.7 %copy-start.2 = (s32[3072]{0:T(1024)S(1)}, s32[3072]{0:T(1024)}, u32[]{:S(2)}) copy-start(s32[3072]{0:T(1024)} %param.11) | copy-start | bytes 36868
  2.3 16.0 %copy-start.3 = (f32[64,12]{0,1:T(8,128)S(1)}, f32[64,12]{0,1:T(8,128)}, u32[]{:S(2)}) copy-start(f32[64,12]{0,1:T(8,128)} %param.8) | copy-start | bytes 9220
  2.3 16.1 %copy-start.4 = (s32[64,12]{0,1:T(8,128)S(1)}, s32[64,12]{0,1:T(8,128)}, u32[]{:S(2)}) copy-start(s32[64,12]{0,1:T(8,128)} %param.9) | copy-start | bytes 9220
  2.3 27.9 %copy-start.5 = (f32[64]{0:T(128)S(1)}, f32[64]{0:T(128)}, u32[]{:S(2)}) copy-start(f32[64]{0:T(128)} %param.10) | copy-start | bytes 772
  2.3 93.9 %all-to-all-start = ((bf16[32,2,2,16,384]{4,3,2,1,0:T(8,128)(2,1)}), bf16[32,2,2,16,384]{4,3,2,1,0:T(8,128)(2,1)S(1)}, u32[]{:S(2)}, u32[]{:S(2)}) async-start(bf16[32,2,2,16,384]{4,3,2,1,0:T(8,128)(2,1)} %spread.1), calls=%async_computation | async-start | bytes 3145728 | tf_op jit(solution)/shard_map/all_to_all | solution.py:477
  18.8 68.6 %collective-permute-start = (bf16[48,128]{1,0:T(8,128)(2,1)S(1)}, bf16[48,128]{1,0:T(8,128)(2,1)S(1)}, u32[]{:S(2)}, u32[]{:S(2)}) collective-permute-start(bf16[48,128]{1,0:T(8,128)(2,1)S(1)} %get-tuple-element.19), channel_id=1, source_target_pairs={{0,8},{8,16},{16,24},{24,0},{1,9},{9,17},{17,25},{25,1},{2,10},{10... | collective-permute-start | bytes 36872 | tf_op jit(solution)/shard_map/ppermute | solution.py:447
  22.5 64.9 %collective-permute-start.1 = (bf16[48,128]{1,0:T(8,128)(2,1)S(1)}, bf16[48,128]{1,0:T(8,128)(2,1)S(1)}, u32[]{:S(2)}, u32[]{:S(2)}) collective-permute-start(bf16[48,128]{1,0:T(8,128)(2,1)S(1)} %get-tuple-element.20), channel_id=1, source_target_pairs={{0,16},{8,24},{16,0},{24,8},{1,17},{9,25},{17,1},{25,9},{2,18},{10... | collective-permute-start | bytes 36872 | tf_op jit(solution)/shard_map/ppermute | solution.py:447
  26.8 61.0 %collective-permute-start.2 = (bf16[48,128]{1,0:T(8,128)(2,1)S(1)}, bf16[48,128]{1,0:T(8,128)(2,1)S(1)}, u32[]{:S(2)}, u32[]{:S(2)}) collective-permute-start(bf16[48,128]{1,0:T(8,128)(2,1)S(1)} %get-tuple-element.18), channel_id=1, source_target_pairs={{0,24},{8,0},{16,8},{24,16},{1,25},{9,1},{17,9},{25,17},{2,26},{10... | collective-permute-start | bytes 36872 | tf_op jit(solution)/shard_map/ppermute | solution.py:447
  96.2 3.7 %copy-start = (bf16[2,256,256]{2,1,0:T(8,128)(2,1)S(1)}, bf16[2,256,256]{2,1,0:T(8,128)(2,1)}, u32[]{:S(2)}) copy-start(bf16[2,256,256]{2,1,0:T(8,128)(2,1)} %constant.101.clone.refs_7_.table_ref) | copy-start | bytes 786436
  96.2 3.7 %copy-start.1 = (f32[2,32,128]{2,1,0:T(8,128)S(1)}, f32[2,32,128]{2,1,0:T(8,128)}, u32[]{:S(2)}) copy-start(f32[2,32,128]{2,1,0:T(8,128)} %constant.100.clone.refs_6_.twist_ref) | copy-start | bytes 98308
  96.2 10.4 %collective-permute-start.3 = (bf16[3,1,2,2,16,384]{5,4,3,2,1,0:T(8,128)(2,1)S(1)}, bf16[3,1,2,2,16,384]{5,4,3,2,1,0:T(8,128)(2,1)S(1)}, u32[]{:S(2)}, u32[]{:S(2)}) collective-permute-start(bf16[3,1,2,2,16,384]{5,4,3,2,1,0:T(8,128)(2,1)S(1)} %tail_message.1), channel_id=1, source_target_pairs={{0,32},{32,64},{64,96},{96,128},{128,160},{160,192},{192,224},{224... | collective-permute-start | bytes 442376 | tf_op jit(solution)/shard_map/ppermute | solution.py:452

commit v9 on v7

--- a/solution.py
+++ b/solution.py
@@ -23,6 +23,7 @@
 SLAB = MEMBERS * PIECE
 GROUP = 16
 BLOCKS = SLAB // BLK
+NARROW = 80
 WINDOW = 144
 ACC_ROWS = NBIN + WINDOW
 DOT_ROWS = 256
@@ -178,15 +179,15 @@
             for s, value in enumerate((power_x + power_y, power_x - power_y, cross_re, cross_im)):
                 stokes_ref[row // 2, pl.ds(GROUP * s, GROUP), lanes] = value.astype(jnp.bfloat16)
 
-    bins = lax.broadcasted_iota(jnp.int32, (WINDOW, BLK), 0).astype(jnp.bfloat16)
-
-    def fold(m):
-        onehot = jnp.where(bins == marks_of(m).astype(jnp.bfloat16), jnp.bfloat16(1), jnp.bfloat16(0))
-        part = lax.dot_general(
-            onehot, stokes_ref[m], (((1,), (1,)), ((), ())), preferred_element_type=jnp.float32
-        )
-        place = pl.ds(pl.multiple_of(base_of(m), 8), WINDOW)
-        acc[place] += part
+    def fold(window):
+        bins = lax.broadcasted_iota(jnp.int32, (window, BLK), 0).astype(jnp.bfloat16)
+        for m in range(BLOCKS):
+            onehot = jnp.where(bins == marks_of(m).astype(jnp.bfloat16), jnp.bfloat16(1), jnp.bfloat16(0))
+            part = lax.dot_general(
+                onehot, stokes_ref[m], (((1,), (1,)), ((), ())), preferred_element_type=jnp.float32
+            )
+            place = pl.ds(pl.multiple_of(base_of(m), 8), window)
+            acc[place] += part
 
     spans = ROWS * GROUP // DOT_ROWS
     for b in range(4):
@@ -215,9 +216,9 @@
         rows_back(1, b)
     for na in range(8):
         rows_out(na)
-        if na % 2:
-            for m in range(na // 2, BLOCKS, 4):
-                fold(m)
+    narrow = base_of(BLOCKS) < NARROW
+    pl.when(narrow)(functools.partial(fold, NARROW))
+    pl.when(jnp.logical_not(narrow))(functools.partial(fold, WINDOW))
 
 
 def own_row(buf_ref, slab, row, pol, part):
@@ -475,7 +476,8 @@
     def weights_for(place):
         return lax.dynamic_slice_in_dim(weight, place * GROUP, GROUP, 0)
 
-    base_rows = jnp.pad(base[None, :], ((0, LETTER_ROWS - BASE_ROW - 1), (0, LANES - BLOCKS)))
+    places = jnp.concatenate([base, jnp.max(marks)[None]])
+    base_rows = jnp.pad(places[None, :], ((0, LETTER_ROWS - BASE_ROW - 1), (0, LANES - BLOCKS - 1)))
     below = jnp.concatenate([marks, base_rows]).astype(jnp.float32)
     letters = [
         turned_to(lambda place: jnp.concatenate([weights_for(place), below]), "zl", turn) for turn in range(RUNS)

time: 130 us -> 130 us (level)
  the two profiles are of different devices: /device:TPU:8 before, /device:TPU:2 now
where the time goes in v9:
time: 130 us
  waiting for transfers between devices  63.9 us (49%)
  starting transfers between devices  30.6 us (24%)
  blocking collectives  19.2 us (15%)
  Pallas kernels  12.2 us (9%)
  other arithmetic  2.86 us (2%)
    ppermute x3, waiting for transfers between devices, turned_to(): lax.ppermute(block_for(there), axis, [(i, (i + turn) % size) for i in ran...  56 us
    all_to_all x1, blocking collectives, on_device(): lax.all_to_all(partial, ('zl', 'xy'), split_axis=0, concat_axis=0, tiled=...  19.2 us
    all_to_all x1, starting transfers between devices, on_device(): lax.all_to_all(parts, ('chan', 'zl'), split_axis=0, concat_axis=0, tiled=...  15.6 us
    ppermute x3, starting transfers between devices, turned_to(): lax.ppermute(block_for(there), axis, [(i, (i + turn) % size) for i in ran...  11.3 us
    all_to_all x1, waiting for transfers between devices, on_device(): lax.all_to_all(parts, ('chan', 'zl'), split_axis=0, concat_axis=0, tiled=...  7.93 us
    pallas_call x1, Pallas kernels, fold_frames(): pl.pallas_call(later_kernel, out_shape=[jax.ShapeDtypeStruct((ACC_ROWS, 4...  6.84 us
    ppermute x1, starting transfers between devices, from_before(): return lax.ppermute(block, 'xy', [(i, i + 1) for i in range(size - 1)])  3.62 us
  transfers between devices with their start and end apart: 5, of which 3 were waited for; matrix products, arithmetic and copies ran while one was open for 3% of the time, Pallas kernels for 5%

profile of v9, /device:TPU:2, one launch (start us, length us, event | category | flops | bytes accessed | tf_op | source)
XLA Modules:
  0.0 129.6 jit_solution(7997808555261343554)
XLA Ops:
  0.0 2.2 %spread.1 = bf16[32,2,2,16,384]{4,3,2,1,0:T(8,128)(2,1)} custom-call(bf16[2,2,32,16,384]{4,3,2,1,0:T(8,128)(2,1)} %bitcast.29), custom_call_target="tpu_custom_call" | custom-call | tf_op jit(solution)/shard_map/spread/pallas_call | solution.py:453
  2.2 0.0 copy-start.2
  2.2 0.0 copy-start.3
  2.2 0.0 copy-start.4
  2.3 0.0 copy-start.5
  2.3 15.6 %all-to-all-start = ((bf16[32,2,2,16,384]{4,3,2,1,0:T(8,128)(2,1)}), bf16[32,2,2,16,384]{4,3,2,1,0:T(8,128)(2,1)S(1)}, u32[]{:S(2)}, u32[]{:S(2)}) async-start(bf16[32,2,2,16,384]{4,3,2,1,0:T(8,128)(2,1)} %spread.1), calls=%async_computation | async-start | bytes 3145728 | tf_op jit(solution)/shard_map/all_to_all | solution.py:466
  18.0 0.0 copy-done.2
  18.0 0.1 reduce.1
  18.1 0.1 broadcast_in_dim.6
  18.2 0.1 sub.32
  18.3 0.0 copy-done.3
  18.3 0.1 copy.14
  18.4 0.0 copy-done.4
  18.4 0.1 copy.13
  18.5 0.7 fusion.7
  19.2 0.6 add_bitcast_fusion
  19.8 0.1 add_select_fusion.1
  19.9 3.7 %collective-permute-start = (f32[48,128]{1,0:T(8,128)S(1)}, f32[48,128]{1,0:T(8,128)S(1)}, u32[]{:S(2)}, u32[]{:S(2)}) collective-permute-start(f32[48,128]{1,0:T(8,128)S(1)} %get-tuple-element.16), channel_id=1, source_target_pairs={{0,8},{8,16},{16,24},{24,0},{1,9},{9,17},{17,25},{25,1},{2,10},{10... | collective-permute-start | bytes 73736 | tf_op jit(solution)/shard_map/ppermute | solution.py:436
  23.6 4.3 %collective-permute-start.1 = (f32[48,128]{1,0:T(8,128)S(1)}, f32[48,128]{1,0:T(8,128)S(1)}, u32[]{:S(2)}, u32[]{:S(2)}) collective-permute-start(f32[48,128]{1,0:T(8,128)S(1)} %get-tuple-element.17), channel_id=1, source_target_pairs={{0,16},{8,24},{16,0},{24,8},{1,17},{9,25},{17,1},{25,9},{2,18},{10... | collective-permute-start | bytes 73736 | tf_op jit(solution)/shard_map/ppermute | solution.py:436
  27.9 3.4 %collective-permute-start.2 = (f32[48,128]{1,0:T(8,128)S(1)}, f32[48,128]{1,0:T(8,128)S(1)}, u32[]{:S(2)}, u32[]{:S(2)}) collective-permute-start(f32[48,128]{1,0:T(8,128)S(1)} %get-tuple-element.15), channel_id=1, source_target_pairs={{0,24},{8,0},{16,8},{24,16},{1,25},{9,1},{17,9},{25,17},{2,26},{10... | collective-permute-start | bytes 73736 | tf_op jit(solution)/shard_map/ppermute | solution.py:436
  31.3 0.0 copy-done.5
  31.3 0.1 dynamic-slice_multiply_fusion
  31.4 0.1 mul.90
  31.5 1.2 fusion.1
  32.8 55.2 %collective-permute-done.refs_1_ = f32[48,128]{1,0:T(8,128)S(1)} collective-permute-done((f32[48,128]{1,0:T(8,128)S(1)}, f32[48,128]{1,0:T(8,128)S(1)}, u32[]{:S(2)}, u32[]{:S(2)}) %collective-permute-start) | collective-permute-done | bytes 24608 | tf_op jit(solution)/shard_map/ppermute | solution.py:436
  88.0 0.0 collective-permute-done.1.refs_2_
  88.0 0.7 collective-permute-done.2.refs_3_
  88.7 7.9 %all-to-all-done = bf16[32,2,2,16,384]{4,3,2,1,0:T(8,128)(2,1)S(1)} async-done(((bf16[32,2,2,16,384]{4,3,2,1,0:T(8,128)(2,1)}), bf16[32,2,2,16,384]{4,3,2,1,0:T(8,128)(2,1)S(1)}, u32[]{:S(2)}, u32[]{:S(2)}) %all-to-all-start) | async-done | bytes 1572896 | tf_op jit(solution)/shard_map/all_to_all | solution.py:466
  96.7 0.0 copy-start
  96.7 0.0 copy-start.1
  96.7 3.6 %collective-permute-start.3 = (bf16[3,1,2,2,16,384]{5,4,3,2,1,0:T(8,128)(2,1)S(1)}, bf16[3,1,2,2,16,384]{5,4,3,2,1,0:T(8,128)(2,1)S(1)}, u32[]{:S(2)}, u32[]{:S(2)}) collective-permute-start(bf16[3,1,2,2,16,384]{5,4,3,2,1,0:T(8,128)(2,1)S(1)} %tail_message.1), channel_id=1, source_target_pairs={{0,32},{32,64},{64,96},{96,128},{128,160},{160,192},{192,224},{224... | collective-permute-start | bytes 442376 | tf_op jit(solution)/shard_map/ppermute | solution.py:441
  100.3 0.0 copy-done
  100.3 0.0 copy-done.1
  100.3 6.8 %later_frames.1 = (f32[1168,64]{1,0:T(8,128)S(1)}, f32[4,48,128]{2,1,0:T(8,128)S(1)}) custom-call(s32[1]{0:T(128)} %bitcast.2.me_ref, f32[48,128]{1,0:T(8,128)S(1)} %get-tuple-element.18.refs_0_, f32[48,128]{1,0:T(8,128)S(1)} %collective-permute-done.refs_1_, f32[48,128]{1,0:T(8,128)S(1)} %collective-permute-done.1.refs_2_, ...), custom_call_target="tpu_custom_call" | custom-call | flops 2415919104 | bytes 30000000 | tf_op jit(solution)/shard_map/later_frames/pallas_call | solution.py:386
  107.2 0.0 collective-permute-done.3.tail_ref
  107.2 2.4 %first_frame.1 = f32[64,8,128]{2,1,0:T(8,128)S(1)} custom-call(bf16[8,4,2,2,16,384]{5,4,3,2,1,0:T(8,128)(2,1)S(1)} %bitcast.27, bf16[3,1,2,2,16,384]{5,4,3,2,1,0:T(8,128)(2,1)S(1)} %collective-permute-done.3.tail_ref, f32[4,48,128]{2,1,0:T(8,128)S(1)} %get-tuple-element.7.sorted_ref, f32[2,512,128]{2,1,0:T(8,128)S(1)} %maximum_multiply_fusion.refs_5_.chirp_ref, ...), custom_call_target="tpu_custom_call" | custom-call | flops 805306368 | bytes 10000000 | tf_op jit(solution)/shard_map/first_frame/pallas_call | solution.py:404
  109.6 19.2 %all_to_all.10 = f32[64,8,128]{2,1,0:T(8,128)S(1)} all-to-all(f32[64,8,128]{2,1,0:T(8,128)S(1)} %first_frame.1), channel_id=1, replica_groups=mesh['xy'=16,'zl'=4,'chan'=8] {'zl','xy'}, dimensions={0} | all-to-all | bytes 524288 | tf_op jit(solution)/shard_map/all_to_all | solution.py:488
  128.8 0.7 last_sum.1
  (12 shorter events, 0.2 us)
Async XLA Ops:
  2.2 15.7 %copy-start.2 = (s32[3072]{0:T(1024)S(1)}, s32[3072]{0:T(1024)}, u32[]{:S(2)}) copy-start(s32[3072]{0:T(1024)} %param.11) | copy-start | bytes 36868
  2.2 16.0 %copy-start.3 = (f32[64,12]{0,1:T(8,128)S(1)}, f32[64,12]{0,1:T(8,128)}, u32[]{:S(2)}) copy-start(f32[64,12]{0,1:T(8,128)} %param.8) | copy-start | bytes 9220
  2.2 16.1 %copy-start.4 = (s32[64,12]{0,1:T(8,128)S(1)}, s32[64,12]{0,1:T(8,128)}, u32[]{:S(2)}) copy-start(s32[64,12]{0,1:T(8,128)} %param.9) | copy-start | bytes 9220
  2.3 29.0 %copy-start.5 = (f32[64]{0:T(128)S(1)}, f32[64]{0:T(128)}, u32[]{:S(2)}) copy-start(f32[64]{0:T(128)} %param.10) | copy-start | bytes 772
  2.3 94.4 %all-to-all-start = ((bf16[32,2,2,16,384]{4,3,2,1,0:T(8,128)(2,1)}), bf16[32,2,2,16,384]{4,3,2,1,0:T(8,128)(2,1)S(1)}, u32[]{:S(2)}, u32[]{:S(2)}) async-start(bf16[32,2,2,16,384]{4,3,2,1,0:T(8,128)(2,1)} %spread.1), calls=%async_computation | async-start | bytes 3145728 | tf_op jit(solution)/shard_map/all_to_all | solution.py:466
  19.9 68.0 %collective-permute-start = (f32[48,128]{1,0:T(8,128)S(1)}, f32[48,128]{1,0:T(8,128)S(1)}, u32[]{:S(2)}, u32[]{:S(2)}) collective-permute-start(f32[48,128]{1,0:T(8,128)S(1)} %get-tuple-element.16), channel_id=1, source_target_pairs={{0,8},{8,16},{16,24},{24,0},{1,9},{9,17},{17,25},{25,1},{2,10},{10... | collective-permute-start | bytes 73736 | tf_op jit(solution)/shard_map/ppermute | solution.py:436
  23.6 64.3 %collective-permute-start.1 = (f32[48,128]{1,0:T(8,128)S(1)}, f32[48,128]{1,0:T(8,128)S(1)}, u32[]{:S(2)}, u32[]{:S(2)}) collective-permute-start(f32[48,128]{1,0:T(8,128)S(1)} %get-tuple-element.17), channel_id=1, source_target_pairs={{0,16},{8,24},{16,0},{24,8},{1,17},{9,25},{17,1},{25,9},{2,18},{10... | collective-permute-start | bytes 73736 | tf_op jit(solution)/shard_map/ppermute | solution.py:436
  27.9 60.8 %collective-permute-start.2 = (f32[48,128]{1,0:T(8,128)S(1)}, f32[48,128]{1,0:T(8,128)S(1)}, u32[]{:S(2)}, u32[]{:S(2)}) collective-permute-start(f32[48,128]{1,0:T(8,128)S(1)} %get-tuple-element.15), channel_id=1, source_target_pairs={{0,24},{8,0},{16,8},{24,16},{1,25},{9,1},{17,9},{25,17},{2,26},{10... | collective-permute-start | bytes 73736 | tf_op jit(solution)/shard_map/ppermute | solution.py:436
  96.7 3.7 %copy-start = (bf16[2,256,256]{2,1,0:T(8,128)(2,1)S(1)}, bf16[2,256,256]{2,1,0:T(8,128)(2,1)}, u32[]{:S(2)}) copy-start(bf16[2,256,256]{2,1,0:T(8,128)(2,1)} %constant.94.clone.refs_7_.table_ref) | copy-start | bytes 786436
  96.7 3.7 %copy-start.1 = (f32[2,32,128]{2,1,0:T(8,128)S(1)}, f32[2,32,128]{2,1,0:T(8,128)}, u32[]{:S(2)}) copy-start(f32[2,32,128]{2,1,0:T(8,128)} %constant.93.clone.refs_6_.twist_ref) | copy-start | bytes 98308
  96.7 10.5 %collective-permute-start.3 = (bf16[3,1,2,2,16,384]{5,4,3,2,1,0:T(8,128)(2,1)S(1)}, bf16[3,1,2,2,16,384]{5,4,3,2,1,0:T(8,128)(2,1)S(1)}, u32[]{:S(2)}, u32[]{:S(2)}) collective-permute-start(bf16[3,1,2,2,16,384]{5,4,3,2,1,0:T(8,128)(2,1)S(1)} %tail_message.1), channel_id=1, source_target_pairs={{0,32},{32,64},{64,96},{96,128},{128,160},{160,192},{192,224},{224... | collective-permute-start | bytes 442376 | tf_op jit(solution)/shard_map/ppermute | solution.py:441

commit v10 on v8

--- a/solution.py
+++ b/solution.py
@@ -23,6 +23,7 @@
 SLAB = MEMBERS * PIECE
 GROUP = 16
 BLOCKS = SLAB // BLK
+NARROW = 80
 WINDOW = 144
 ACC_ROWS = NBIN + WINDOW
 DOT_ROWS = 256
@@ -179,15 +180,15 @@
             for s, value in enumerate((power_x + power_y, power_x - power_y, cross_re, cross_im)):
                 stokes_ref[row // 2, pl.ds(GROUP * s, GROUP), lanes] = value.astype(jnp.bfloat16)
 
-    bins = lax.broadcasted_iota(jnp.int32, (WINDOW, BLK), 0).astype(jnp.bfloat16)
-
-    def fold(m):
-        onehot = jnp.where(bins == marks_of(m).astype(jnp.bfloat16), jnp.bfloat16(1), jnp.bfloat16(0))
-        part = lax.dot_general(
-            onehot, stokes_ref[m], (((1,), (1,)), ((), ())), preferred_element_type=jnp.float32
-        )
-        place = pl.ds(pl.multiple_of(base_of(m), 8), WINDOW)
-        acc[place] += part
+    def fold(window):
+        bins = lax.broadcasted_iota(jnp.int32, (window, BLK), 0).astype(jnp.bfloat16)
+        for m in range(BLOCKS):
+            onehot = jnp.where(bins == marks_of(m).astype(jnp.bfloat16), jnp.bfloat16(1), jnp.bfloat16(0))
+            part = lax.dot_general(
+                onehot, stokes_ref[m], (((1,), (1,)), ((), ())), preferred_element_type=jnp.float32
+            )
+            place = pl.ds(pl.multiple_of(base_of(m), 8), window)
+            acc[place] += part
 
     spans = ROWS * GROUP // DOT_ROWS
     for b in range(4):
@@ -216,9 +217,9 @@
         rows_back(1, b)
     for na in range(8):
         rows_out(na)
-        if na % 2:
-            for m in range(na // 2, BLOCKS, 4):
-                fold(m)
+    narrow = base_of(BLOCKS) < NARROW
+    pl.when(narrow)(functools.partial(fold, NARROW))
+    pl.when(jnp.logical_not(narrow))(functools.partial(fold, WINDOW))
 
 
 def own_row(buf_ref, slab, row, pol, part):
@@ -487,7 +488,8 @@
     def weights_for(place):
         return lax.dynamic_slice_in_dim(weight, place * GROUP, GROUP, 0)
 
-    base_rows = jnp.pad(base[None, :] // 8, ((0, LETTER_ROWS - BASE_ROW - 1), (0, LANES - BLOCKS)))
+    places = jnp.concatenate([base, jnp.max(marks)[None]])
+    base_rows = jnp.pad(places[None, :] // 8, ((0, LETTER_ROWS - BASE_ROW - 1), (0, LANES - BLOCKS - 1)))
     below = jnp.concatenate([marks, base_rows]).astype(jnp.bfloat16)
     letters = [
         turned_to(lambda place: jnp.concatenate([weights_for(place), below]), "zl", turn) for turn in range(RUNS)

time: 130 us -> 129 us (level)
  waiting for transfers between devices: 64.6 us -> 63.1 us
  other arithmetic: 1.66 us -> 3.1 us
    ppermute x3, waiting for transfers between devices: 56.2 us -> 54.7 us  [turned_to(): lax.ppermute(block_for(there), axis, [(i, (i + turn) % size) for i in ran...]
  transfers between devices with their start and end apart: 5 -> 5, of which waited for: 3 -> 3; matrix products, arithmetic and copies ran while one was open for 2% -> 3% of each run, Pallas kernels for 5% -> 5%
where the time goes in v10:
time: 129 us
  waiting for transfers between devices  63.1 us (49%)
  starting transfers between devices  30.6 us (24%)
  blocking collectives  19.6 us (15%)
  Pallas kernels  11.9 us (9%)
  other arithmetic  3.1 us (2%)
    ppermute x3, waiting for transfers between devices, turned_to(): lax.ppermute(block_for(there), axis, [(i, (i + turn) % size) for i in ran...  54.7 us
    all_to_all x1, blocking collectives, on_device(): lax.all_to_all(partial, ('zl', 'xy'), split_axis=0, concat_axis=0, tiled=...  19.6 us
    all_to_all x1, starting transfers between devices, on_device(): lax.all_to_all(parts, ('chan', 'zl'), split_axis=0, concat_axis=0, tiled=...  15.6 us
    ppermute x3, starting transfers between devices, turned_to(): lax.ppermute(block_for(there), axis, [(i, (i + turn) % size) for i in ran...  11.3 us
    all_to_all x1, waiting for transfers between devices, on_device(): lax.all_to_all(parts, ('chan', 'zl'), split_axis=0, concat_axis=0, tiled=...  8.4 us
    pallas_call x1, Pallas kernels, fold_frames(): pl.pallas_call(later_kernel, out_shape=[jax.ShapeDtypeStruct((ACC_ROWS, 4...  6.52 us
    ppermute x1, starting transfers between devices, from_before(): return lax.ppermute(block, 'xy', [(i, i + 1) for i in range(size - 1)])  3.62 us
  transfers between devices with their start and end apart: 5, of which 3 were waited for; matrix products, arithmetic and copies ran while one was open for 3% of the time, Pallas kernels for 5%

profile of v10, /device:TPU:8, one launch (start us, length us, event | category | flops | bytes accessed | tf_op | source)
XLA Modules:
  0.0 129.1 jit_solution(10853592052254056511)
XLA Ops:
  0.0 2.3 %spread.1 = bf16[32,2,2,16,384]{4,3,2,1,0:T(8,128)(2,1)} custom-call(bf16[2,2,32,16,384]{4,3,2,1,0:T(8,128)(2,1)} %bitcast.29), custom_call_target="tpu_custom_call" | custom-call | tf_op jit(solution)/shard_map/spread/pallas_call | solution.py:465
  2.3 0.0 copy-start.2
  2.3 0.0 copy-start.3
  2.3 0.0 copy-start.4
  2.3 0.0 copy-start.5
  2.3 15.6 %all-to-all-start = ((bf16[32,2,2,16,384]{4,3,2,1,0:T(8,128)(2,1)}), bf16[32,2,2,16,384]{4,3,2,1,0:T(8,128)(2,1)S(1)}, u32[]{:S(2)}, u32[]{:S(2)}) async-start(bf16[32,2,2,16,384]{4,3,2,1,0:T(8,128)(2,1)} %spread.1), calls=%async_computation | async-start | bytes 3145728 | tf_op jit(solution)/shard_map/all_to_all | solution.py:478
  18.0 0.0 copy-done.2
  18.0 0.1 reduce.1
  18.2 0.1 broadcast_in_dim.2
  18.2 0.1 sub.45
  18.3 0.0 copy-done.3
  18.3 0.1 copy.14
  18.4 0.0 copy-done.4
  18.4 0.1 copy.13
  18.5 0.7 fusion.19
  19.3 0.7 fusion.20
  20.0 0.1 fusion.9
  20.1 0.1 fusion.17
  20.2 3.7 %collective-permute-start = (bf16[48,128]{1,0:T(8,128)(2,1)S(1)}, bf16[48,128]{1,0:T(8,128)(2,1)S(1)}, u32[]{:S(2)}, u32[]{:S(2)}) collective-permute-start(bf16[48,128]{1,0:T(8,128)(2,1)S(1)} %get-tuple-element.19), channel_id=1, source_target_pairs={{0,8},{8,16},{16,24},{24,0},{1,9},{9,17},{17,25},{25,1},{2,10},{10... | collective-permute-start | bytes 36872 | tf_op jit(solution)/shard_map/ppermute | solution.py:448
  23.9 4.3 %collective-permute-start.1 = (bf16[48,128]{1,0:T(8,128)(2,1)S(1)}, bf16[48,128]{1,0:T(8,128)(2,1)S(1)}, u32[]{:S(2)}, u32[]{:S(2)}) collective-permute-start(bf16[48,128]{1,0:T(8,128)(2,1)S(1)} %get-tuple-element.20), channel_id=1, source_target_pairs={{0,16},{8,24},{16,0},{24,8},{1,17},{9,25},{17,1},{25,9},{2,18},{10... | collective-permute-start | bytes 36872 | tf_op jit(solution)/shard_map/ppermute | solution.py:448
  28.2 3.4 %collective-permute-start.2 = (bf16[48,128]{1,0:T(8,128)(2,1)S(1)}, bf16[48,128]{1,0:T(8,128)(2,1)S(1)}, u32[]{:S(2)}, u32[]{:S(2)}) collective-permute-start(bf16[48,128]{1,0:T(8,128)(2,1)S(1)} %get-tuple-element.18), channel_id=1, source_target_pairs={{0,24},{8,0},{16,8},{24,16},{1,25},{9,1},{17,9},{25,17},{2,26},{10... | collective-permute-start | bytes 36872 | tf_op jit(solution)/shard_map/ppermute | solution.py:448
  31.6 0.0 copy-done.5
  31.6 0.1 dynamic-slice_multiply_fusion
  31.7 0.1 mul.105
  31.8 1.2 fusion.1
  33.1 54.4 %collective-permute-done.refs_1_ = bf16[48,128]{1,0:T(8,128)(2,1)S(1)} collective-permute-done((bf16[48,128]{1,0:T(8,128)(2,1)S(1)}, bf16[48,128]{1,0:T(8,128)(2,1)S(1)}, u32[]{:S(2)}, u32[]{:S(2)}) %collective-permute-start) | collective-permute-done | bytes 12320 | tf_op jit(solution)/shard_map/ppermute | solution.py:448
  87.4 0.0 collective-permute-done.1.refs_2_
  87.4 0.4 collective-permute-done.2.refs_3_
  87.8 8.4 %all-to-all-done = bf16[32,2,2,16,384]{4,3,2,1,0:T(8,128)(2,1)S(1)} async-done(((bf16[32,2,2,16,384]{4,3,2,1,0:T(8,128)(2,1)}), bf16[32,2,2,16,384]{4,3,2,1,0:T(8,128)(2,1)S(1)}, u32[]{:S(2)}, u32[]{:S(2)}) %all-to-all-start) | async-done | bytes 1572896 | tf_op jit(solution)/shard_map/all_to_all | solution.py:478
  96.2 0.0 copy-start
  96.2 0.0 copy-start.1
  96.2 3.6 %collective-permute-start.3 = (bf16[3,1,2,2,16,384]{5,4,3,2,1,0:T(8,128)(2,1)S(1)}, bf16[3,1,2,2,16,384]{5,4,3,2,1,0:T(8,128)(2,1)S(1)}, u32[]{:S(2)}, u32[]{:S(2)}) collective-permute-start(bf16[3,1,2,2,16,384]{5,4,3,2,1,0:T(8,128)(2,1)S(1)} %tail_message.1), channel_id=1, source_target_pairs={{0,32},{32,64},{64,96},{96,128},{128,160},{160,192},{192,224},{224... | collective-permute-start | bytes 442376 | tf_op jit(solution)/shard_map/ppermute | solution.py:453
  99.8 0.0 copy-done
  99.9 0.0 copy-done.1
  99.9 6.5 %later_frames.1 = (f32[1168,64]{1,0:T(8,128)S(1)}, f32[4,48,128]{2,1,0:T(8,128)S(1)}) custom-call(s32[1]{0:T(128)} %bitcast.2.me_ref, bf16[48,128]{1,0:T(8,128)(2,1)S(1)} %get-tuple-element.21.refs_0_, bf16[48,128]{1,0:T(8,128)(2,1)S(1)} %collective-permute-done.refs_1_, bf16[48,128]{1,0:T(8,128)(2,1)S(1)} %collective-permute-done.1.refs_2_, ...), custom_call_target="tpu_custom_call" | custom-call | flops 2415919104 | bytes 30000000 | tf_op jit(solution)/shard_map/later_frames/pallas_call | solution.py:398
  106.4 0.0 collective-permute-done.3.tail_ref
  106.4 2.3 %first_frame.1 = f32[64,8,128]{2,1,0:T(8,128)S(1)} custom-call(bf16[8,4,2,2,16,384]{5,4,3,2,1,0:T(8,128)(2,1)S(1)} %bitcast.27, bf16[3,1,2,2,16,384]{5,4,3,2,1,0:T(8,128)(2,1)S(1)} %collective-permute-done.3.tail_ref, f32[4,48,128]{2,1,0:T(8,128)S(1)} %get-tuple-element.7.sorted_ref, f32[2,512,128]{2,1,0:T(8,128)S(1)} %maximum_multiply_fusion.refs_5_.chirp_ref, ...), custom_call_target="tpu_custom_call" | custom-call | flops 805306368 | bytes 10000000 | tf_op jit(solution)/shard_map/first_frame/pallas_call | solution.py:416
  108.7 19.6 %all_to_all.10 = f32[64,8,128]{2,1,0:T(8,128)S(1)} all-to-all(f32[64,8,128]{2,1,0:T(8,128)S(1)} %first_frame.1), channel_id=1, replica_groups=mesh['xy'=16,'zl'=4,'chan'=8] {'zl','xy'}, dimensions={0} | all-to-all | bytes 524288 | tf_op jit(solution)/shard_map/all_to_all | solution.py:500
  128.3 0.7 last_sum.1
  (12 shorter events, 0.2 us)
Async XLA Ops:
  2.3 15.7 %copy-start.2 = (s32[3072]{0:T(1024)S(1)}, s32[3072]{0:T(1024)}, u32[]{:S(2)}) copy-start(s32[3072]{0:T(1024)} %param.11) | copy-start | bytes 36868
  2.3 16.0 %copy-start.3 = (f32[64,12]{0,1:T(8,128)S(1)}, f32[64,12]{0,1:T(8,128)}, u32[]{:S(2)}) copy-start(f32[64,12]{0,1:T(8,128)} %param.8) | copy-start | bytes 9220
  2.3 16.1 %copy-start.4 = (s32[64,12]{0,1:T(8,128)S(1)}, s32[64,12]{0,1:T(8,128)}, u32[]{:S(2)}) copy-start(s32[64,12]{0,1:T(8,128)} %param.9) | copy-start | bytes 9220
  2.3 29.3 %copy-start.5 = (f32[64]{0:T(128)S(1)}, f32[64]{0:T(128)}, u32[]{:S(2)}) copy-start(f32[64]{0:T(128)} %param.10) | copy-start | bytes 772
  2.3 93.9 %all-to-all-start = ((bf16[32,2,2,16,384]{4,3,2,1,0:T(8,128)(2,1)}), bf16[32,2,2,16,384]{4,3,2,1,0:T(8,128)(2,1)S(1)}, u32[]{:S(2)}, u32[]{:S(2)}) async-start(bf16[32,2,2,16,384]{4,3,2,1,0:T(8,128)(2,1)} %spread.1), calls=%async_computation | async-start | bytes 3145728 | tf_op jit(solution)/shard_map/all_to_all | solution.py:478
  20.2 67.2 %collective-permute-start = (bf16[48,128]{1,0:T(8,128)(2,1)S(1)}, bf16[48,128]{1,0:T(8,128)(2,1)S(1)}, u32[]{:S(2)}, u32[]{:S(2)}) collective-permute-start(bf16[48,128]{1,0:T(8,128)(2,1)S(1)} %get-tuple-element.19), channel_id=1, source_target_pairs={{0,8},{8,16},{16,24},{24,0},{1,9},{9,17},{17,25},{25,1},{2,10},{10... | collective-permute-start | bytes 36872 | tf_op jit(solution)/shard_map/ppermute | solution.py:448
  23.9 63.5 %collective-permute-start.1 = (bf16[48,128]{1,0:T(8,128)(2,1)S(1)}, bf16[48,128]{1,0:T(8,128)(2,1)S(1)}, u32[]{:S(2)}, u32[]{:S(2)}) collective-permute-start(bf16[48,128]{1,0:T(8,128)(2,1)S(1)} %get-tuple-element.20), channel_id=1, source_target_pairs={{0,16},{8,24},{16,0},{24,8},{1,17},{9,25},{17,1},{25,9},{2,18},{10... | collective-permute-start | bytes 36872 | tf_op jit(solution)/shard_map/ppermute | solution.py:448
  28.2 59.6 %collective-permute-start.2 = (bf16[48,128]{1,0:T(8,128)(2,1)S(1)}, bf16[48,128]{1,0:T(8,128)(2,1)S(1)}, u32[]{:S(2)}, u32[]{:S(2)}) collective-permute-start(bf16[48,128]{1,0:T(8,128)(2,1)S(1)} %get-tuple-element.18), channel_id=1, source_target_pairs={{0,24},{8,0},{16,8},{24,16},{1,25},{9,1},{17,9},{25,17},{2,26},{10... | collective-permute-start | bytes 36872 | tf_op jit(solution)/shard_map/ppermute | solution.py:448
  96.2 3.7 %copy-start = (bf16[2,256,256]{2,1,0:T(8,128)(2,1)S(1)}, bf16[2,256,256]{2,1,0:T(8,128)(2,1)}, u32[]{:S(2)}) copy-start(bf16[2,256,256]{2,1,0:T(8,128)(2,1)} %constant.105.clone.refs_7_.table_ref) | copy-start | bytes 786436
  96.2 3.7 %copy-start.1 = (f32[2,32,128]{2,1,0:T(8,128)S(1)}, f32[2,32,128]{2,1,0:T(8,128)}, u32[]{:S(2)}) copy-start(f32[2,32,128]{2,1,0:T(8,128)} %constant.104.clone.refs_6_.twist_ref) | copy-start | bytes 98308
  96.2 10.2 %collective-permute-start.3 = (bf16[3,1,2,2,16,384]{5,4,3,2,1,0:T(8,128)(2,1)S(1)}, bf16[3,1,2,2,16,384]{5,4,3,2,1,0:T(8,128)(2,1)S(1)}, u32[]{:S(2)}, u32[]{:S(2)}) collective-permute-start(bf16[3,1,2,2,16,384]{5,4,3,2,1,0:T(8,128)(2,1)S(1)} %tail_message.1), channel_id=1, source_target_pairs={{0,32},{32,64},{64,96},{96,128},{128,160},{160,192},{192,224},{224... | collective-permute-start | bytes 442376 | tf_op jit(solution)/shard_map/ppermute | solution.py:453
